TPU v7x, 256 devices: a whole 4x4x8 slice. The times are simulated.
256 devices in a mesh: box: 128 (over x, y, z_lo, core), shift: 2 (over z_hi).
Axes of the slice: x: 4, y: 4, z: 8 (z_hi: 2, z_lo: 4; z = z_hi * 4 + z_lo), core: 2. Of those that a mesh axis runs over, the one named last changes fastest.
Arguments:
- vectors: bfloat16 [2, 8192, 128, 128], P('shift', 'box'), may hold values from -6 to 6
- sigma: float32 [2, 2], P('shift'), may hold values from 0.5 to 2
- near_blocks: bfloat16 [8192, 6, 128, 128], P('box', None, 'shift'), may hold values from -0.21875 to 0.21875
- near_index: int32 [8192, 6], P('box'), may hold values from -1 to 8191, as said below
- radiate: bfloat16 [128, 128], replicated, may hold values from -0.5 to 0.5
- interp_one: bfloat16 [8, 512, 128], replicated, may hold values from -0.1875 to 0.1875
- interp_two: bfloat16 [8, 2048, 512], replicated, may hold values from -0.09375 to 0.09375
- trans_one: float32 [316, 512], replicated, may hold values from -1.5 to 1.5
- level1_source: int32 [1024, 16], P('box'), may hold values from -1 to 1023, as said below
- level1_offset: int32 [1024, 16], P('box'), may hold values from 0 to 315
- trans_two: float32 [316, 2048], P(None, 'box'), may hold values from -1 to 1
- level2_source: int32 [128, 32], replicated, may hold values from -1 to 127, as said below
- level2_offset: int32 [128, 32], replicated, may hold values from 0 to 315
Outputs:
- applied: float32 [2, 8192, 128, 128], P('shift', 'box')
Inputs may be any that keep to these rules, and one draw needn't show every extreme that they name: `near_index`: leaf boxes are numbered along a space-filling curve. Entry 0 of each row is the box itself; every live entry names a box within 64 of the row's box; live entries come first, unused ones are -1; some rows use all 6 entries and some only one. `level1_source`: entry 0 of each row is live; every live entry names a box within 8 of the row's box; live entries come first, unused ones are -1; some rows use all 16 entries and some only one. `level2_source`: entry 0 of each row is live; live entries come first, unused ones are -1; some rows use all 32 entries and some only one.
All inputs are finite; a program needn't handle non-finite values.
Results may differ from a plain program's by a relative error of at most 0.0035.
Values may be sent and summed in bfloat16 or wider, within the bound.
A program may use at most 192 MiB of HBM per device.

v0:
```python
import jax
import jax.numpy as jnp
from jax import lax
from jax.sharding import PartitionSpec as P


def extended(block, sides, width):
    for axis, dim in sides:
        count = lax.axis_size(axis)
        forward = [(i, i + 1) for i in range(count - 1)]
        backward = [(target, source) for source, target in forward]
        low = lax.ppermute(
            lax.slice_in_dim(block, block.shape[dim] - width, None, axis=dim), axis, forward
        )
        high = lax.ppermute(lax.slice_in_dim(block, 0, width, axis=dim), axis, backward)
        block = jnp.concatenate([low, block, high], axis=dim)
    return block


def weighted_lists(pattern, table, offsets, sources, base):
    live = sources >= 0
    local = jnp.where(live, sources - base, 0)
    weights = table[offsets] * live[:, :, None].astype(jnp.float32)
    picked = pattern[local]
    return jnp.einsum("cjk,cjkr->ckr", weights, picked, preferred_element_type=jnp.float32)


def body(
    vectors,
    sigma,
    near_blocks,
    near_index,
    radiate,
    interp_one,
    interp_two,
    trans_one,
    level1_source,
    level1_offset,
    trans_two,
    level2_source,
    level2_offset,
):
    box_count = vectors.shape[1]
    unknowns = vectors.shape[2]
    columns = vectors.shape[3]
    samples0 = radiate.shape[0]
    samples1 = interp_one.shape[1]
    my_box = lax.axis_index("box")
    live = near_index >= 0
    local = jnp.where(live, near_index - (my_box * box_count - box_count), 0)
    live_mask = live[:, :, None, None].astype(jnp.bfloat16)
    haloed = extended(vectors, (("box", 1),), box_count)[0]
    near_source = haloed[local] * live_mask
    near = jnp.einsum(
        "bjvu,bjur->bvr",
        lax.all_gather(near_blocks, "shift", axis=2, tiled=True),
        near_source,
        preferred_element_type=jnp.float32,
    )
    field = vectors[0]
    leaf = jnp.einsum("ku,bur->bkr", radiate, field, preferred_element_type=jnp.float32).astype(
        jnp.bfloat16
    )
    upper = jnp.einsum(
        "oqk,cokr->cqr",
        interp_one,
        leaf.reshape(box_count // 8, 8, samples0, columns),
        preferred_element_type=jnp.float32,
    ).astype(jnp.bfloat16)
    coarse = jnp.einsum(
        "oqk,gokr->gqr",
        interp_two,
        upper.reshape(box_count // 64, 8, samples1, columns),
        preferred_element_type=jnp.float32,
    ).astype(jnp.bfloat16)
    turned = weighted_lists(
        lax.all_to_all(coarse, "box", split_axis=1, concat_axis=0, tiled=True),
        trans_two,
        level2_offset,
        level2_source,
        0,
    ).astype(jnp.bfloat16)
    incoming = lax.all_to_all(turned, "box", split_axis=0, concat_axis=1, tiled=True)
    parents = box_count // 8
    upper_rim = extended(upper, (("box", 0),), parents)
    across = weighted_lists(
        upper_rim, trans_one, level1_offset, level1_source, my_box * parents - parents
    )
    down = jnp.einsum(
        "oqk,gqr->gokr", interp_two, incoming, preferred_element_type=jnp.float32
    ).reshape(parents, samples1, columns)
    local_in = (across + down).astype(jnp.bfloat16)
    leaf_in = (
        jnp.einsum("oqk,cqr->cokr", interp_one, local_in, preferred_element_type=jnp.float32)
        .reshape(box_count, samples0, columns)
        .astype(jnp.bfloat16)
    )
    far = jnp.einsum("ku,bkr->bur", radiate, leaf_in, preferred_element_type=jnp.float32)
    real_part = field[:, : unknowns // 2].astype(jnp.float32)
    imag_part = field[:, unknowns // 2 :].astype(jnp.float32)
    sig_re = sigma[0, 0]
    sig_im = sigma[0, 1]
    scaled = jnp.concatenate(
        [sig_re * real_part - sig_im * imag_part, sig_re * imag_part + sig_im * real_part], axis=1
    )
    return (near + far - scaled)[None]


def solution(mesh):
    in_specs = (
        P("shift", "box", None, None),
        P("shift", None),
        P("box", None, "shift", None),
        P("box", None),
        P(),
        P(),
        P(),
        P(),
        P("box", None),
        P("box", None),
        P(None, "box"),
        P(),
        P(),
    )
    out_specs = P("shift", "box", None, None)
    return jax.shard_map(body, mesh=mesh, in_specs=in_specs, out_specs=out_specs, check_vma=False)
```

profile of v0, /device:TPU:2, one launch (start us, length us, event | category | flops | bytes accessed | tf_op | source)
XLA Modules:
  0.0 528.8 jit_solution(15764240590217312818)
XLA Ops:
  6.5 0.7 all-gather.2.cloned.1.call-update
  7.3 0.1 copy-done.4
  7.4 2.3 fusion.15
  9.7 2.3 fusion.18
  12.1 1.9 collective-permute-start.2
  14.0 8.4 %collective-permute-start.3 = (bf16[8,512,128]{1,2,0:T(8,128)(2,1)}, bf16[8,512,128]{1,2,0:T(8,128)(2,1)}, u32[]{:S(2)}, u32[]{:S(2)}) collective-permute-start(bf16[8,512,128]{1,2,0:T(8,128)(2,1)} %fusion.18), channel_id=1, source_target_pairs={{2,0},{4,2},{6,4},{8,6},{10,8},{12,10},{14,12},{16,14},{18,16},{20... | collective-permute-start | bytes 3145736 | tf_op jit(solution)/shard_map/ppermute | solution.py:15
  22.4 1.9 collective-permute-start
  24.4 8.5 %collective-permute-start.1 = (bf16[1,64,128,128]{3,2,1,0:T(8,128)(2,1)}, bf16[1,64,128,128]{3,2,1,0:T(8,128)(2,1)}, u32[]{:S(2)}, u32[]{:S(2)}) collective-permute-start(bf16[1,64,128,128]{3,2,1,0:T(8,128)(2,1)} %param.13), channel_id=1, source_target_pairs={{2,0},{4,2},{6,4},{8,6},{10,8},{12,10},{14,12},{16,14},{18,16},{20... | collective-permute-start | bytes 6291464 | tf_op jit(solution)/shard_map/ppermute | solution.py:15
  32.8 13.1 %fusion.9 = bf16[1,2048,128]{1,2,0:T(8,128)(2,1)S(1)} fusion(bf16[8,512,128]{1,2,0:T(8,128)(2,1)} %fusion.18, bf16[8,2048,512]{2,1,0:T(8,128)(2,1)} %param.19), kind=kOutput, calls=%fused_computation.24 | convolution fusion | flops 2147745792 | bytes 18350080 | tf_op jit(solution)/shard_map/oqk,gokr->gqr/dot_general | solution.py:70
  45.9 0.8 copy.38
  46.7 0.0 copy-start.9
  46.7 0.0 copy-start.10
  46.7 0.0 copy-start.5
  46.7 0.0 copy-start.6
  46.7 0.0 copy-start.7
  46.7 0.5 broadcast.52
  47.3 11.5 %reduce.2 = bf16[2048,128]{1,0:T(8,128)(2,1)S(1)} reduce(bf16[2048,1,128]{2,1,0:T(2,128)(2,1)S(1)} %bitcast.105, bf16[]{:T(256)} %broadcast.52), dimensions={1}, to_apply=%bitcast.88.reduce_sub_computation | reduce | bytes 1048578
  58.8 0.9 reshape.94
  59.7 7.1 %all-to-all-start = ((bf16[128,2,1024]{2,1,0:T(2,128)(2,1)}), bf16[128,2,1024]{2,1,0:T(2,128)(2,1)}, u32[]{:S(2)}, u32[]{:S(2)}) async-start(bf16[128,2,1024]{2,1,0:T(2,128)(2,1)} %reshape.94), calls=%async_computation | async-start | bytes 1048576 | tf_op jit(solution)/shard_map/all_to_all | solution.py:77
  66.8 3.2 copy.34
  70.1 0.0 copy-done.9
  70.1 0.1 reshape.51
  70.2 0.1 reshape.43
  70.3 0.1 copy.39
  70.4 0.1 reshape.67
  70.4 0.0 copy-done.6
  70.5 0.1 copy.36
  70.6 0.0 copy-done.7
  70.6 0.1 copy.35
  70.7 0.1 reshape.59
  70.8 0.1 copy.37
  70.9 14.2 %gather_fusion.3 = f32[4096,16]{1,0:T(8,128)} fusion(f32[316,16]{1,0:T(8,128)S(1)} %copy.36, s32[4096]{0:T(1024)S(1)} %broadcast_clamp_fusion.1), kind=kCustom, calls=%fused_computation.3 | custom fusion | bytes 540672 | tf_op jit(solution)/shard_map/gather | solution.py:23
  85.1 2.7 multiply_bitcast_fusion
  87.8 3.8 copy.51
  91.6 0.0 copy-done.8
  91.7 0.1 copy.31
  91.7 0.1 reshape.35
  91.9 0.1 copy.32
  92.0 2.7 gather_fusion.1
  94.7 0.7 fusion.27
  95.4 1.7 multiply_bitcast_fusion.1
  97.1 6.1 %fusion.5 = (f32[64,64,128]{1,2,0:T(8,128)}, f32[64,64,128]{1,2,0:T(8,128)}) fusion(f32[]{:T(128)} %bitcast.36, f32[]{:T(128)} %bitcast.35, bf16[64,128,128]{1,2,0:T(8,128)(2,1)S(1)} %bitcast.100), kind=kLoop, calls=%fused_computation.16 | loop fusion | flops 4194304 | bytes 6291464 | tf_op jit(solution)/shard_map/sub | solution.py:104
  103.3 267.5 %all-to-all-done = bf16[128,2,1024]{2,1,0:T(2,128)(2,1)} async-done(((bf16[128,2,1024]{2,1,0:T(2,128)(2,1)}), bf16[128,2,1024]{2,1,0:T(2,128)(2,1)}, u32[]{:S(2)}, u32[]{:S(2)}) %all-to-all-start) | async-done | bytes 524320 | tf_op jit(solution)/shard_map/all_to_all | solution.py:77
  370.7 3.6 reshape.95
  374.3 0.1 copy.57
  374.4 31.9 %gather_fusion.4 = bf16[4096,16,128]{2,1,0:T(8,128)(2,1)} fusion(bf16[128,16,128]{2,1,0:T(8,128)(2,1)S(1)} %bitcast.98, s32[4096]{0:T(1024)S(1)} %broadcast_clamp_fusion), kind=kCustom, calls=%fused_computation.4 | custom fusion | bytes 33570816 | tf_op jit(solution)/shard_map/gather | solution.py:24
  406.3 10.1 %fusion = f32[128,16,1,128]{3,2,1,0:T(1,128)S(1)} fusion(bf16[128,32,16,1]{1,3,2,0:T(2,128)(2,1)S(1)} %copy-done.3, bf16[128,32,16,128]{3,2,1,0:T(8,128)(2,1)} %bitcast.101), kind=kOutput, calls=%fused_computation.6 | convolution fusion | flops 16777216 | bytes 17956864 | tf_op jit(solution)/shard_map/cjk,cjkr->ckr/dot_general | solution.py:25
  416.5 0.9 convert_element_type.64
  417.3 8.7 %all-to-all-start.1 = ((bf16[128,16,128]{2,1,0:T(8,128)(2,1)}), bf16[128,16,128]{2,1,0:T(8,128)(2,1)}, u32[]{:S(2)}, u32[]{:S(2)}) async-start(bf16[128,16,128]{2,1,0:T(8,128)(2,1)} %convert_element_type.64), calls=%async_computation.1 | async-start | bytes 1048576 | tf_op jit(solution)/shard_map/all_to_all | solution.py:83
  426.1 0.0 collective-permute-done.2
  426.1 0.0 collective-permute-done.3
  426.1 3.2 pad_maximum_fusion
  429.3 10.1 %gather_fusion.2 = bf16[128,512,128]{1,2,0:T(8,128)(2,1)} fusion(bf16[24,512,128]{1,2,0:T(8,128)(2,1)} %pad_maximum_fusion, s32[1024]{0:T(1024)S(1)} %pad_clamp_fusion), kind=kCustom, calls=%fused_computation.2 | custom fusion | bytes 33554944 | tf_op jit(solution)/shard_map/gather | solution.py:24
  439.4 9.3 %multiply_reduce_fusion = f32[8,512,128]{1,2,0:T(8,128)S(1)} fusion(f32[8,512,16]{1,2,0:T(8,128)S(1)} %copy-done.2, bf16[128,512,128]{1,2,0:T(8,128)(2,1)} %gather_fusion.2), kind=kLoop, calls=%fused_computation.5 | loop fusion | flops 24641536 | bytes 19136512 | tf_op jit(solution)/shard_map/cjk,cjkr->ckr/dot_general | solution.py:25
  448.7 0.0 all-to-all-done.1
  448.7 10.8 %convolution_convert_fusion = bf16[8,128,8,128]{3,1,2,0:T(8,128)(2,1)} fusion(bf16[8,512,128]{2,1,0:T(8,128)(2,1)S(1)} %copy-done, f32[8,512,128]{1,2,0:T(8,128)S(1)} %multiply_reduce_fusion, bf16[2048,128,1]{1,0,2:T(8,128)(2,1)} %bitcast.26, bf16[8,2048,512]{2,1,0:T(8,128)(2,1)} %param.19), kind=kOutput, calls=%fused_computation.32 | convolution fusion | flops 3223322624 | bytes 22544384 | tf_op jit(solution)/shard_map/oqk,cqr->cokr/dot_general | solution.py:94
  459.5 4.2 fusion.22
  463.7 0.0 collective-permute-done
  463.7 0.0 collective-permute-done.1
  463.7 6.0 %maximum_bitcast_fusion = bf16[192,128,128]{2,1,0:T(8,128)(2,1)} fusion(bf16[1,64,128,128]{3,2,1,0:T(8,128)(2,1)} %collective-permute-done.1, bf16[1,64,128,128]{3,2,1,0:T(8,128)(2,1)} %param.13, bf16[1,64,128,128]{3,2,1,0:T(8,128)(2,1)} %collective-permute-done), kind=kLoop, calls=%fused_computation.10 | loop fusion | flops 6291456 | bytes 12582912 | tf_op jit(solution)/shard_map/squeeze | solution.py:52
  469.7 14.0 %gather_fusion = bf16[384,128,128]{2,1,0:T(8,128)(2,1)} fusion(bf16[192,128,128]{2,1,0:T(8,128)(2,1)} %maximum_bitcast_fusion, s32[1024]{0:T(1024)S(1)} %pad_clamp_fusion.2), kind=kCustom, calls=%fused_computation | custom fusion | bytes 25167360 | tf_op jit(solution)/shard_map/gather | solution.py:53
  483.7 16.6 %copy.33 = bf16[64,6,128,128]{2,3,1,0:T(8,128)(2,1)} copy(bf16[64,6,128,128]{3,2,1,0:T(8,128)(2,1)} %bitcast.99) | data formatting | bytes 25165824 | tf_op jit(solution)/shard_map/gather | solution.py:53
  500.3 16.0 %fusion.7 = f32[1,64,128,128]{2,3,1,0:T(8,128)} fusion(f32[64,64,128]{1,2,0:T(8,128)} %get-tuple-element.6, f32[64,64,128]{1,2,0:T(8,128)} %get-tuple-element.5, f32[64,128,128]{2,1,0:T(8,128)} %fusion.22, bf16[64,6,128,128]{3,2,1,0:T(8,128)(2,1)} %all-gather.2.cloned.1.call-done, bf16[64,6,128,128]{2,3,1,0:T(8,128)(2,1)} %copy.33, bf16[64,6]{1,0:T(8,128)(2,1)S(1)} %copy.32), kind=kOutput, calls=%fused_computation.19 | convolution fusion | flops 1620049920 | bytes 37749504 | tf_op jit(solution)/shard_map/bjvu,bjur->bvr/dot_general | solution.py:54
  516.4 5.6 %copy.41 = f32[1,64,128,128]{3,2,1,0:T(8,128)} copy(f32[1,64,128,128]{2,3,1,0:T(8,128)} %fusion.7) | data formatting | bytes 8388608 | tf_op jit(solution)/shard_map/broadcast_in_dim | solution.py:106
  (29 shorter events, 0.1 us)
Async XLA Ops:
  6.5 3.2 copy-start
  6.5 0.8 copy-start.4
  6.5 493.8 %all-gather.2.cloned.1.call-start = ((), (), s32[]{:S(2)}) async-start(), calls=%async_computation.2 | async-start | bytes 18874368 | tf_op jit(solution)/shard_map/all_gather | solution.py:56
  12.1 414.0 %collective-permute-start.2 = (bf16[8,512,128]{1,2,0:T(8,128)(2,1)}, bf16[8,512,128]{1,2,0:T(8,128)(2,1)}, u32[]{:S(2)}, u32[]{:S(2)}) collective-permute-start(bf16[8,512,128]{1,2,0:T(8,128)(2,1)} %fusion.18), channel_id=1, source_target_pairs={{0,2},{2,4},{4,6},{6,8},{8,10},{10,12},{12,14},{14,16},{16,18},{18... | collective-permute-start | bytes 3145736 | tf_op jit(solution)/shard_map/ppermute | solution.py:12
  14.0 412.1 %collective-permute-start.3 = (bf16[8,512,128]{1,2,0:T(8,128)(2,1)}, bf16[8,512,128]{1,2,0:T(8,128)(2,1)}, u32[]{:S(2)}, u32[]{:S(2)}) collective-permute-start(bf16[8,512,128]{1,2,0:T(8,128)(2,1)} %fusion.18), channel_id=1, source_target_pairs={{2,0},{4,2},{6,4},{8,6},{10,8},{12,10},{14,12},{16,14},{18,16},{20... | collective-permute-start | bytes 3145736 | tf_op jit(solution)/shard_map/ppermute | solution.py:15
  22.4 441.3 %collective-permute-start = (bf16[1,64,128,128]{3,2,1,0:T(8,128)(2,1)}, bf16[1,64,128,128]{3,2,1,0:T(8,128)(2,1)}, u32[]{:S(2)}, u32[]{:S(2)}) collective-permute-start(bf16[1,64,128,128]{3,2,1,0:T(8,128)(2,1)} %param.13), channel_id=1, source_target_pairs={{0,2},{2,4},{4,6},{6,8},{8,10},{10,12},{12,14},{14,16},{16,18},{18... | collective-permute-start | bytes 6291464 | tf_op jit(solution)/shard_map/ppermute | solution.py:12
  24.4 439.4 %collective-permute-start.1 = (bf16[1,64,128,128]{3,2,1,0:T(8,128)(2,1)}, bf16[1,64,128,128]{3,2,1,0:T(8,128)(2,1)}, u32[]{:S(2)}, u32[]{:S(2)}) collective-permute-start(bf16[1,64,128,128]{3,2,1,0:T(8,128)(2,1)} %param.13), channel_id=1, source_target_pairs={{2,0},{4,2},{6,4},{8,6},{10,8},{12,10},{14,12},{16,14},{18,16},{20... | collective-permute-start | bytes 6291464 | tf_op jit(solution)/shard_map/ppermute | solution.py:15
  46.7 23.4 %copy-start.9 = (s32[8,16]{1,0:T(8,128)S(1)}, s32[8,16]{1,0:T(8,128)}, u32[]{:S(2)}) copy-start(s32[8,16]{1,0:T(8,128)} %param.21) | copy-start | bytes 1540
  46.7 23.5 %copy-start.10 = (s32[8,16]{1,0:T(8,128)S(1)}, s32[8,16]{1,0:T(8,128)}, u32[]{:S(2)}) copy-start(s32[8,16]{1,0:T(8,128)} %param.22) | copy-start | bytes 1540
  46.7 23.5 %copy-start.5 = (s32[128,32]{0,1:T(8,128)S(1)}, s32[128,32]{0,1:T(8,128)}, u32[]{:S(2)}) copy-start(s32[128,32]{0,1:T(8,128)} %param.24) | copy-start | bytes 49156
  46.7 23.7 %copy-start.6 = (f32[316,16]{0,1:T(8,128)S(1)}, f32[316,16]{0,1:T(8,128)}, u32[]{:S(2)}) copy-start(f32[316,16]{0,1:T(8,128)} %param.23) | copy-start | bytes 60676
  46.7 23.8 %copy-start.7 = (s32[128,32]{0,1:T(8,128)S(1)}, s32[128,32]{0,1:T(8,128)}, u32[]{:S(2)}) copy-start(s32[128,32]{0,1:T(8,128)} %param.25) | copy-start | bytes 49156
  59.7 311.0 %all-to-all-start = ((bf16[128,2,1024]{2,1,0:T(2,128)(2,1)}), bf16[128,2,1024]{2,1,0:T(2,128)(2,1)}, u32[]{:S(2)}, u32[]{:S(2)}) async-start(bf16[128,2,1024]{2,1,0:T(2,128)(2,1)} %reshape.94), calls=%async_computation | async-start | bytes 1048576 | tf_op jit(solution)/shard_map/all_to_all | solution.py:77
  85.1 6.5 %copy-start.8 = (s32[64,6]{0,1:T(8,128)S(1)}, s32[64,6]{0,1:T(8,128)}, u32[]{:S(2)}) copy-start(s32[64,6]{0,1:T(8,128)} %param.16) | copy-start | bytes 4612
  85.1 9.6 %copy-start.11 = (f32[1,2]{1,0:T(1,128)S(1)}, f32[1,2]{1,0:T(1,128)}, u32[]{:S(2)}) copy-start(f32[1,2]{1,0:T(1,128)} %param.14) | copy-start | bytes 28
  374.4 32.0 %copy-start.3 = (bf16[128,32,16,1]{1,3,2,0:T(2,128)(2,1)S(1)}, bf16[128,32,16,1]{1,3,2,0:T(2,128)(2,1)}, u32[]{:S(2)}) copy-start(bf16[128,32,16,1]{1,3,2,0:T(2,128)(2,1)} %copy.51) | copy-start | bytes 393220
  417.3 31.4 %all-to-all-start.1 = ((bf16[128,16,128]{2,1,0:T(8,128)(2,1)}), bf16[128,16,128]{2,1,0:T(8,128)(2,1)}, u32[]{:S(2)}, u32[]{:S(2)}) async-start(bf16[128,16,128]{2,1,0:T(8,128)(2,1)} %convert_element_type.64), calls=%async_computation.1 | async-start | bytes 1048576 | tf_op jit(solution)/shard_map/all_to_all | solution.py:83
  429.3 10.1 %copy-start.2 = (f32[8,512,16]{1,2,0:T(8,128)S(1)}, f32[8,512,16]{1,2,0:T(8,128)}, u32[]{:S(2)}) copy-start(f32[8,512,16]{1,2,0:T(8,128)} %multiply_bitcast_fusion.1) | copy-start | bytes 786436
  500.3 21.6 %copy-start.1 = (bf16[8,512,128]{2,1,0:T(8,128)(2,1)S(1)}, bf16[8,512,128]{2,1,0:T(8,128)(2,1)}, u32[]{:S(2)}) copy-start(bf16[8,512,128]{2,1,0:T(8,128)(2,1)} %param.18) | copy-start | bytes 3145732
Sparse Core Ops, SparseCore 0:
  9.2 359.8 all-gather.1
where the time goes:
time: 532 us; the launch traced here: 529 us
  waiting for transfers between devices  268 us (50%)
  local copies, waits for them, and re-layouts  110 us (21%)
  matrix products  58.9 us (11%)
  other arithmetic  41.6 us (8%)
  starting transfers between devices  36.6 us (7%)
  between operations  13.7 us (3%)
    all_to_all x1, waiting for transfers between devices, body(): lax.all_to_all(coarse, 'box', split_axis=1, concat_axis=0, tiled=True)  267 us
    gather x2, local copies, waits for them, and re-layouts, weighted_lists(): picked = pattern[local]  42.1 us
    gather x2, local copies, waits for them, and re-layouts, body(): near_source = haloed[local] * live_mask  30.6 us
    ppermute x2, starting transfers between devices, extended(): lax.ppermute(lax.slice_in_dim(block, 0, width, axis=dim), axis, backward)  16.9 us
    gather x2, local copies, waits for them, and re-layouts, weighted_lists(): weights = table[offsets] * live[:, :, None].astype(jnp.float32)  16.9 us
    dot_general x1, matrix products, body(): jnp.einsum('bjvu,bjur->bvr', lax.all_gather(near_blocks, 'shift', axis=2,...  16 us
    unnamed x2, other arithmetic  13.3 us
    dot_general x1, matrix products, body(): jnp.einsum('oqk,gokr->gqr', interp_two, upper.reshape(box_count // 64, 8,...  13.1 us
  transfers between devices with their start and end apart: 7, of which 1 were waited for; matrix products, arithmetic and copies ran while one was open for 36% of the time, Pallas kernels for 0%

commit v1 on v0

v1 whole, which is shorter than its diff:
```python
import functools

import jax
import jax.numpy as jnp
from jax import lax
from jax.experimental import pallas as pl
from jax.experimental.pallas import tpu as pltpu
from jax.sharding import PartitionSpec as P

BF = jnp.bfloat16
F32 = jnp.float32
MIB = 1 << 20
ANY = pl.BlockSpec(memory_space=pl.ANY)
VMEM = pl.BlockSpec(memory_space=pltpu.VMEM)
BOTH = ("box", "shift")
DEPTH = 4


def dot(a, b):
    return jnp.dot(a, b, preferred_element_type=F32)


def dot_nt(a, b):
    return lax.dot_general(a, b, (((1,), (1,)), ((), ())), preferred_element_type=F32)


def routes(boxes):
    chips = boxes // 2

    def flat(chip, core, shift):
        return (chip % chips * 2 + core) * 2 + shift

    hops = ([], [], [])
    for chip in range(chips):
        for core in range(2):
            wraps = chip % DEPTH == (DEPTH - 1 if core else 0)
            beside = chip + (1 if core else -1)
            for shift in range(2):
                stops = [
                    flat(chip, core, shift),
                    flat(beside, 1 - core, 1 - shift if wraps else shift),
                    flat(chip, core, 1 - shift),
                    flat(beside, 1 - core, shift if wraps else 1 - shift),
                ]
                for hop in range(3):
                    hops[hop].append((stops[hop], stops[hop + 1]))
    return hops


def place():
    me = lax.axis_index("box")
    core = lax.rem(me, 2)
    depth = lax.rem(lax.div(me, 2), DEPTH)
    wraps = jnp.where(core == 0, depth == 0, depth == DEPTH - 1).astype(jnp.int32)
    return me, core, wraps


def exchange_kernel(count, x_ref, o_ref, send, recv, local):
    me = lax.axis_index("box")
    shift = lax.axis_index("shift")
    own = pltpu.make_async_copy(x_ref.at[me], o_ref.at[me], local)
    own.start()

    @pl.loop(1, count)
    def _(step):
        other = lax.rem(me + step, count)
        pltpu.make_async_remote_copy(
            x_ref.at[other],
            o_ref.at[me],
            send,
            recv,
            device_id=(other, shift),
            device_id_type=pl.DeviceIdType.MESH,
        ).start()

    own.wait()
    rest = pl.ds(0, count - 1)
    pltpu.make_async_copy(x_ref.at[rest], x_ref.at[rest], send).wait()
    pltpu.make_async_copy(o_ref.at[rest], o_ref.at[rest], recv).wait()


def exchange(blocks):
    count = blocks.shape[0]
    return pl.pallas_call(
        functools.partial(exchange_kernel, count),
        out_shape=jax.ShapeDtypeStruct(blocks.shape, BF),
        in_specs=[VMEM],
        out_specs=VMEM,
        scratch_shapes=[pltpu.SemaphoreType.DMA] * 3,
        compiler_params=pltpu.CompilerParams(has_side_effects=True),
        cost_estimate=pl.CostEstimate(flops=0, bytes_accessed=64 * MIB, transcendentals=0),
        name="exchange",
    )(blocks)


def parent_pattern(x_of, radiate, one_ref):
    total = None
    for pair in range(4):
        leaves = [dot(radiate, x_of(2 * pair + i)).astype(BF) for i in range(2)]
        lhs = jnp.concatenate([one_ref[2 * pair], one_ref[2 * pair + 1]], axis=1)
        term = dot(lhs, jnp.concatenate(leaves, axis=0))
        total = term if total is None else total + term
    return total


def upward_kernel(x_ref, radiate_ref, one_ref, two_ref, coarse_ref, total):
    step = pl.program_id(0)
    upper = parent_pattern(lambda i: x_ref[i], radiate_ref[...], one_ref).astype(BF)
    term = dot(two_ref[0], upper)

    @pl.when(step == 0)
    def _():
        total[...] = term

    @pl.when(step > 0)
    def _():
        total[...] += term

    @pl.when(step == pl.num_programs(0) - 1)
    def _():
        coarse_ref[...] = total[...].astype(BF)


def upward(x, radiate, one, two):
    octants, k2, k1 = two.shape
    _, u, r = x.shape
    return pl.pallas_call(
        upward_kernel,
        grid=(octants,),
        out_shape=jax.ShapeDtypeStruct((k2, r), BF),
        in_specs=[
            pl.BlockSpec((8, u, r), lambda i: (i, 0, 0)),
            VMEM,
            VMEM,
            pl.BlockSpec((1, k2, k1), lambda i: (i, 0, 0)),
        ],
        out_specs=pl.BlockSpec((k2, r), lambda i: (0, 0)),
        scratch_shapes=[pltpu.VMEM((k2, r), F32)],
        compiler_params=pltpu.CompilerParams(vmem_limit_bytes=24 * MIB),
        cost_estimate=pl.CostEstimate(flops=7_000_000_000, bytes_accessed=40 * MIB, transcendentals=0),
        name="upward",
    )(x, radiate, one, two)


def translate_kernel(width, source_ref, offset_ref, coarse_ref, weight_ref, out_ref):
    @pl.loop(0, out_ref.shape[0])
    def _(box):
        total = jnp.zeros(out_ref.shape[1:], F32)
        for j in range(width):
            at = box * width + j
            total += weight_ref[offset_ref[at]] * coarse_ref[source_ref[at]].astype(F32)
        out_ref[box] = total.astype(BF)


def translate(coarse, table, source, offset):
    boxes, width = source.shape
    classes, samples = table.shape
    live = source >= 0
    weights = jnp.broadcast_to(
        jnp.pad(table, ((0, 1), (0, 0)))[:, :, None], (classes + 1, samples, coarse.shape[2])
    )
    return pl.pallas_call(
        functools.partial(translate_kernel, width),
        out_shape=jax.ShapeDtypeStruct(coarse.shape, BF),
        grid_spec=pltpu.PrefetchScalarGridSpec(
            num_scalar_prefetch=2, grid=(), in_specs=[VMEM, VMEM], out_specs=VMEM
        ),
        compiler_params=pltpu.CompilerParams(vmem_limit_bytes=16 * MIB),
        cost_estimate=pl.CostEstimate(flops=2_000_000_000, bytes_accessed=40 * MIB, transcendentals=0),
        name="translate",
    )(
        jnp.where(live, source, 0).reshape(-1),
        jnp.where(live, offset, classes).reshape(-1),
        coarse,
        weights,
    )


def near_kernel(
    group, slots, index_ref, blocks_ref, x, mate, first, partner, partner_mate, last,
    own_ref, other_ref, held, sems,
):
    step = pl.program_id(0)
    me, core, wraps = place()
    count = x.shape[0]

    @pl.when(step == 0)
    def _():
        towards = 2 * core
        within = 2 - towards
        moves = (
            (x, 0, 1),
            (mate, 0, within),
            (first, wraps, towards),
            (partner, 1, 1),
            (partner_mate, 1, within),
            (last, 1 - wraps, towards),
        )
        copies = [
            pltpu.make_async_copy(src, held.at[kind, pl.ds(slot * count, count)], sems.at[i])
            for i, (src, kind, slot) in enumerate(moves)
        ]
        for copy in copies:
            copy.start()
        zero = jnp.zeros(held.shape[2:], BF)
        held[0, 3 * count] = zero
        held[1, 3 * count] = zero
        for copy in copies:
            copy.wait()

    base = me * count - count
    for b in range(group):
        total = None
        for pair in range(slots // 2):
            rows = []
            for i in range(2):
                at = index_ref[(step * group + b) * slots + 2 * pair + i]
                at = jnp.where(at >= 0, at - base, 3 * count)
                rows.append(jnp.concatenate([held[0, at], held[1, at]], axis=1))
            lhs = jnp.concatenate([blocks_ref[b, 2 * pair], blocks_ref[b, 2 * pair + 1]], axis=1)
            term = dot(lhs, jnp.concatenate(rows, axis=0))
            total = term if total is None else total + term
        r = own_ref.shape[2]
        own_ref[b] = total[:, :r]
        other_ref[b] = total[:, r:].astype(BF)


def near_field(index, blocks, *vectors):
    count, slots, half, u = blocks.shape
    r = vectors[0].shape[2]
    group = 8
    out = pl.BlockSpec((group, half, r), lambda i, _: (i, 0, 0))
    return pl.pallas_call(
        functools.partial(near_kernel, group, slots),
        out_shape=[
            jax.ShapeDtypeStruct((count, half, r), F32),
            jax.ShapeDtypeStruct((count, half, r), BF),
        ],
        grid_spec=pltpu.PrefetchScalarGridSpec(
            num_scalar_prefetch=1,
            grid=(count // group,),
            in_specs=[pl.BlockSpec((group, slots, half, u), lambda i, _: (i, 0, 0, 0))] + [ANY] * 6,
            out_specs=[out, out],
            scratch_shapes=[
                pltpu.VMEM((2, 3 * count + 1, u, r), BF),
                pltpu.SemaphoreType.DMA((6,)),
            ],
        ),
        compiler_params=pltpu.CompilerParams(vmem_limit_bytes=32 * MIB),
        cost_estimate=pl.CostEstimate(flops=6_000_000_000, bytes_accessed=30 * MIB, transcendentals=0),
        name="near_field",
    )(index.reshape(-1), blocks, *vectors)


def downward_kernel(
    width, source_ref, offset_ref, x, mate, first, last, own_ref, sigma_ref, radiate_ref, turned_ref,
    one_ref, two_ref, table_ref, incoming_ref, base_ref, held, patterns, flat, weights, across, sems,
):
    step = pl.program_id(0)
    me, core, wraps = place()
    count, u, r = x.shape
    parents = count // 8
    eye = (
        lax.broadcasted_iota(jnp.int32, (r, r), 0) == lax.broadcasted_iota(jnp.int32, (r, r), 1)
    ).astype(BF)

    @pl.when(step == 0)
    def _():
        towards = 2 * core
        within = 2 - towards
        beside = pl.ds(towards * count, count)
        pltpu.make_async_copy(x, held.at[pl.ds(count, count)], sems.at[0]).start()
        pltpu.make_async_copy(mate, held.at[pl.ds(within * count, count)], sems.at[1]).start()

        @pl.when(wraps == 0)
        def _():
            pltpu.make_async_copy(first, held.at[beside], sems.at[2]).start()

        @pl.when(wraps == 1)
        def _():
            pltpu.make_async_copy(last, held.at[beside], sems.at[2]).start()

        flat[...] = dot_nt(eye, incoming_ref[...]).astype(BF)
        for i in range(3):
            pltpu.make_async_copy(x, held.at[pl.ds(count, count)], sems.at[i]).wait()

        @pl.loop(0, 3 * parents)
        def _(c):
            upper = parent_pattern(lambda i: held[c * 8 + i], radiate_ref[...], one_ref).astype(BF)
            patterns[c] = dot_nt(eye, upper).astype(BF)

    origin = me * parents - parents
    at = []
    for j in range(width):
        source = source_ref[step * width + j]
        live = source >= 0
        at.append(jnp.where(live, source - origin, 0))
        row = table_ref[pl.ds(offset_ref[step * width + j], 1), :]
        weights[pl.ds(j, 1), :] = row * live.astype(F32)

    @pl.loop(0, r // 16)
    def _(part):
        rows = pl.ds(part * 16, 16)
        total = None
        for j in range(width):
            term = weights[pl.ds(j, 1), :] * patterns[at[j], rows, :].astype(F32)
            total = term if total is None else total + term
        across[rows, :] = total

    local = (across[...] + dot(flat[...], two_ref[0])).astype(BF)
    shift = lax.axis_index("shift")
    half = u // 2
    sig_re, sig_im = sigma_ref[0], sigma_ref[1]
    for child in range(8):
        leaf_in = dot(local, one_ref[child]).astype(BF)
        far = dot_nt(turned_ref[...], leaf_in)
        field = held[count + step * 8 + child].astype(F32)
        real, imag = field[:half], field[half:]
        base_ref[child, :half] = far[:half] - (sig_re * real - sig_im * imag)
        base_ref[child, half:] = far[half:] - (sig_re * imag + sig_im * real)
        mine = pl.ds(pl.multiple_of(shift * half, half), half)
        base_ref[child, mine] += own_ref[child]


def downward(source, offset, x, mate, first, last, own, sigma, radiate, one, two, table, incoming):
    octants, k2, k1 = two.shape
    count, u, r = x.shape
    parents, width = source.shape
    return pl.pallas_call(
        functools.partial(downward_kernel, width),
        out_shape=jax.ShapeDtypeStruct((count, u, r), F32),
        grid_spec=pltpu.PrefetchScalarGridSpec(
            num_scalar_prefetch=2,
            grid=(octants,),
            in_specs=[
                ANY,
                ANY,
                ANY,
                ANY,
                pl.BlockSpec((8, u // 2, r), lambda i, *_: (i, 0, 0)),
                pl.BlockSpec(memory_space=pltpu.SMEM),
                VMEM,
                VMEM,
                VMEM,
                pl.BlockSpec((1, k2, k1), lambda i, *_: (i, 0, 0)),
                VMEM,
                VMEM,
            ],
            out_specs=pl.BlockSpec((8, u, r), lambda i, *_: (i, 0, 0)),
            scratch_shapes=[
                pltpu.VMEM((3 * count, u, r), BF),
                pltpu.VMEM((3 * parents, r, k1), BF),
                pltpu.VMEM((r, k2), BF),
                pltpu.VMEM((width, k1), F32),
                pltpu.VMEM((r, k1), F32),
                pltpu.SemaphoreType.DMA((3,)),
            ],
        ),
        compiler_params=pltpu.CompilerParams(vmem_limit_bytes=40 * MIB),
        cost_estimate=pl.CostEstimate(flops=9_000_000_000, bytes_accessed=60 * MIB, transcendentals=0),
        name="downward",
    )(
        source.reshape(-1), offset.reshape(-1), x, mate, first, last, own, sigma.reshape(-1), radiate,
        radiate.T, one, two, table, incoming,
    )


def add_kernel(_, base_ref, back_ref, out_ref):
    out_ref[...] = base_ref[...] + back_ref[...].astype(F32)


def add_rows(base, back, half_at):
    count, u, r = base.shape
    group = 16
    rows = pl.BlockSpec((group, u // 2, r), lambda i, at: (i, at[0], 0))
    return pl.pallas_call(
        add_kernel,
        out_shape=jax.ShapeDtypeStruct((count, u, r), F32),
        grid_spec=pltpu.PrefetchScalarGridSpec(
            num_scalar_prefetch=1,
            grid=(count // group,),
            in_specs=[rows, pl.BlockSpec((group, u // 2, r), lambda i, at: (i, 0, 0))],
            out_specs=rows,
        ),
        input_output_aliases={1: 0},
        compiler_params=pltpu.CompilerParams(vmem_limit_bytes=16 * MIB),
        cost_estimate=pl.CostEstimate(flops=0, bytes_accessed=5 * MIB, transcendentals=0),
        name="add_rows",
    )(half_at, base, back)


def body(
    vectors,
    sigma,
    near_blocks,
    near_index,
    radiate,
    interp_one,
    interp_two,
    trans_one,
    level1_source,
    level1_offset,
    trans_two,
    level2_source,
    level2_offset,
):
    x = vectors[0]
    boxes = lax.axis_size("box")
    k2 = interp_two.shape[1]
    hops = routes(boxes)
    swap = [(i, i ^ 1) for i in range(boxes)]
    first = lax.ppermute(x, BOTH, hops[0])
    mate = lax.ppermute(x, "box", swap)
    partner = lax.ppermute(first, BOTH, hops[1])
    partner_mate = lax.ppermute(partner, "box", swap)
    last = lax.ppermute(partner, BOTH, hops[2])

    coarse = upward(x, radiate, interp_one, interp_two)
    gathered = exchange(coarse.reshape(boxes, k2 // boxes, -1))
    turned = translate(gathered, trans_two, level2_source, level2_offset)
    incoming = exchange(turned).reshape(k2, -1)

    own, other = near_field(near_index, near_blocks, x, mate, first, partner, partner_mate, last)
    back = lax.ppermute(other, "shift", [(0, 1), (1, 0)])
    base = downward(
        level1_source, level1_offset, x, mate, first, last, own, sigma, radiate, interp_one,
        interp_two, trans_one, incoming,
    )
    half_at = (1 - lax.axis_index("shift")).astype(jnp.int32).reshape(1)
    return add_rows(base, back, half_at)[None]


def solution(mesh):
    in_specs = (
        P("shift", "box", None, None),
        P("shift", None),
        P("box", None, "shift", None),
        P("box", None),
        P(),
        P(),
        P(),
        P(),
        P("box", None),
        P("box", None),
        P(None, "box"),
        P(),
        P(),
    )
    out_specs = P("shift", "box", None, None)
    return jax.shard_map(body, mesh=mesh, in_specs=in_specs, out_specs=out_specs, check_vma=False)
```

time: 532 us -> 353 us (0.66)
  Pallas kernels: 0 us -> 211 us
  waiting for transfers between devices: 268 us -> 91.2 us
  local copies, waits for them, and re-layouts: 110 us -> 23.8 us
  matrix products: 58.9 us -> 0 us
  other arithmetic: 41.6 us -> 0.01 us
  between operations: 13.7 us -> 0.27 us
  starting transfers between devices: 36.6 us -> 25.6 us
    all_to_all x2 -> x0, waiting for transfers between devices: 267 us -> none  [the longest x1 267 us: body(): lax.all_to_all(coarse, 'box', split_axis=1, concat_axis=0, tiled=True)]
    pallas_call x0 -> x7, Pallas kernels: none -> 211 us  [the longest x2 119 us: exchange(): pl.pallas_call(functools.partial(exchange_kernel, count), out_shape=jax.S...]
    ppermute x4 -> x6, waiting for transfers between devices: 0.01 us -> 91.2 us  [the longest x1 67.3 us: body(): partner = lax.ppermute(first, BOTH, hops[1])]
    gather x6 -> x0, local copies, waits for them, and re-layouts: 89.5 us -> none  [the longest x2 42.1 us: weighted_lists(): picked = pattern[local]]
    dot_general x7 -> x0, matrix products: 58.9 us -> none  [the longest x1 16 us: body(): jnp.einsum('bjvu,bjur->bvr', lax.all_gather(near_blocks, 'shift', axis=2,...]
    all_to_all x2 -> x0, starting transfers between devices: 15.8 us -> none  [the longest x1 8.74 us: body(): lax.all_to_all(turned, 'box', split_axis=0, concat_axis=1, tiled=True)]
    unnamed x30 -> x51, local copies, waits for them, and re-layouts: 8.61 us -> 22.4 us
    unnamed x2 -> x0, other arithmetic: 13.3 us -> none
  transfers between devices with their start and end apart: 7 -> 6, of which waited for: 1 -> 2; matrix products, arithmetic and copies ran while one was open for 36% -> 1% of each run, Pallas kernels for 0% -> 56%
where the time goes in v1:
time: 353 us; the launch traced here: 352 us
  Pallas kernels  211 us (60%)
  waiting for transfers between devices  91.2 us (26%)
  starting transfers between devices  25.6 us (7%)
  local copies, waits for them, and re-layouts  23.8 us (7%)
    pallas_call x2, Pallas kernels, exchange(): pl.pallas_call(functools.partial(exchange_kernel, count), out_shape=jax.S...  119 us
    ppermute x1, waiting for transfers between devices, body(): partner = lax.ppermute(first, BOTH, hops[1])  67.3 us
    pallas_call x1, Pallas kernels, downward(): pl.pallas_call(functools.partial(downward_kernel, width), out_shape=jax.S...  52.4 us
    ppermute x1, waiting for transfers between devices, body(): first = lax.ppermute(x, BOTH, hops[0])  23.9 us
    unnamed x51, local copies, waits for them, and re-layouts  22.4 us
    pallas_call x1, Pallas kernels, upward(): pl.pallas_call(upward_kernel, grid=(octants,), out_shape=jax.ShapeDtypeSt...  14.4 us
    pallas_call x1, Pallas kernels, near_field(): pl.pallas_call(functools.partial(near_kernel, group, slots), out_shape=[j...  10.6 us
    ppermute x1, starting transfers between devices, body(): last = lax.ppermute(partner, BOTH, hops[2])  10.2 us
  transfers between devices with their start and end apart: 6, of which 2 were waited for; matrix products, arithmetic and copies ran while one was open for 1% of the time, Pallas kernels for 56%

profile of v1, /device:TPU:2, one launch (start us, length us, event | category | flops | bytes accessed | tf_op | source)
XLA Modules:
  0.0 351.7 jit_solution(6188912442580095624)
XLA Ops:
  0.0 7.7 %collective-permute-start.1 = (bf16[64,128,128]{2,1,0:T(8,128)(2,1)}, bf16[64,128,128]{2,1,0:T(8,128)(2,1)S(1)}, u32[]{:S(2)}, u32[]{:S(2)}) collective-permute-start(bf16[64,128,128]{2,1,0:T(8,128)(2,1)} %bitcast.8), channel_id=1, source_target_pairs={{0,255},{1,254},{2,4},{3,5},{4,2},{5,3},{6,8},{7,9},{8,6},{9,7},{1... | collective-permute-start | bytes 6291464 | tf_op jit(solution)/shard_map/ppermute | solution.py:412
  7.7 23.9 %collective-permute-done.1.first = bf16[64,128,128]{2,1,0:T(8,128)(2,1)S(1)} collective-permute-done((bf16[64,128,128]{2,1,0:T(8,128)(2,1)}, bf16[64,128,128]{2,1,0:T(8,128)(2,1)S(1)}, u32[]{:S(2)}, u32[]{:S(2)}) %collective-permute-start.1) | collective-permute-done | bytes 2097184 | tf_op jit(solution)/shard_map/ppermute | solution.py:412
  31.6 4.7 %collective-permute-start.2 = (bf16[64,128,128]{2,1,0:T(8,128)(2,1)S(1)}, bf16[64,128,128]{2,1,0:T(8,128)(2,1)}, u32[]{:S(2)}, u32[]{:S(2)}) collective-permute-start(bf16[64,128,128]{2,1,0:T(8,128)(2,1)S(1)} %collective-permute-done.1.first), channel_id=1, source_target_pairs={{255,1},{254,0},{4,3},{5,2},{2,5},{3,4},{8,7},{9,6},{6,9},{7,8},{1... | collective-permute-start | bytes 6291464 | tf_op jit(solution)/shard_map/ppermute | solution.py:414
  36.4 0.0 copy-start.4
  36.4 1.3 copy-done.4
  37.7 0.0 collective-permute-start
  37.7 67.3 %collective-permute-done.2.partner = bf16[64,128,128]{2,1,0:T(8,128)(2,1)} collective-permute-done((bf16[64,128,128]{2,1,0:T(8,128)(2,1)S(1)}, bf16[64,128,128]{2,1,0:T(8,128)(2,1)}, u32[]{:S(2)}, u32[]{:S(2)}) %collective-permute-start.2) | collective-permute-done | bytes 2097184 | tf_op jit(solution)/shard_map/ppermute | solution.py:414
  105.0 10.2 %collective-permute-start.3 = (bf16[64,128,128]{2,1,0:T(8,128)(2,1)}, bf16[64,128,128]{2,1,0:T(8,128)(2,1)}, u32[]{:S(2)}, u32[]{:S(2)}) collective-permute-start(bf16[64,128,128]{2,1,0:T(8,128)(2,1)} %collective-permute-done.2.partner), channel_id=1, source_target_pairs={{1,254},{0,255},{3,5},{2,4},{5,3},{4,2},{7,9},{6,8},{9,7},{8,6},{1... | collective-permute-start | bytes 6291464 | tf_op jit(solution)/shard_map/ppermute | solution.py:416
  115.2 0.0 collective-permute-start.4
  115.2 0.8 copy.17
  116.0 0.1 reshape.31.index_ref
  116.1 0.0 copy-start
  116.1 5.8 %copy-done = bf16[8,2048,512]{2,1,0:T(8,128)(2,1)S(1)} copy-done((bf16[8,2048,512]{2,1,0:T(8,128)(2,1)S(1)}, bf16[8,2048,512]{2,1,0:T(8,128)(2,1)}, u32[]{:S(2)}) %copy-start) | copy-done | bytes 16777240
  121.9 1.6 copy-done.2
  123.5 1.2 copy-done.9
  124.7 0.8 copy-done.15
  125.5 0.0 copy-start.19
  125.5 14.4 %upward.1 = bf16[2048,128]{1,0:T(8,128)(2,1)S(1)} custom-call(bf16[64,128,128]{2,1,0:T(8,128)(2,1)S(1)} %bitcast.10, bf16[128,128]{1,0:T(8,128)(2,1)S(1)} %copy-done.15, bf16[8,512,128]{2,1,0:T(8,128)(2,1)S(1)} %copy-done.9, bf16[8,2048,512]{2,1,0:T(8,128)(2,1)S(1)} %copy-done), custom_call_target="tpu_custom_call" | custom-call | flops 7000000000 | bytes 41943040 | tf_op jit(solution)/shard_map/upward/pallas_call | solution.py:127
  140.0 0.0 copy-start.12
  140.0 0.0 copy-start.16
  140.0 0.0 collective-permute-done.mate
  140.0 0.0 collective-permute-done.3.last
  140.0 0.0 collective-permute-done.4.partner_mate
  140.0 0.0 copy-done.3
  140.0 0.0 copy-done.5
  140.0 0.0 copy-start.18
  140.0 2.9 copy-done.18
  143.0 10.6 %near_field.1 = (f32[64,64,128]{2,1,0:T(8,128)S(1)}, bf16[64,64,128]{2,1,0:T(8,128)(2,1)}) custom-call(s32[384]{0:T(512)S(1)} %reshape.31.index_ref, bf16[64,6,64,128]{3,2,1,0:T(8,128)(2,1)S(1)} %copy-done.18, bf16[64,128,128]{2,1,0:T(8,128)(2,1)S(1)} %bitcast.11, bf16[64,128,128]{2,1,0:T(8,128)(2,1)} %collective-permute-done.mate, ...), custom_call_target="tpu_custom_call" | custom-call | flops 6000000000 | bytes 31457280 | tf_op jit(solution)/shard_map/near_field/pallas_call | solution.py:233
  153.6 0.0 copy-done.12
  153.6 0.0 copy-start.7
  153.6 1.4 copy-done.7
  155.0 3.0 collective-permute-start.5
  158.0 0.0 copy-done.20
  158.0 0.0 copy-done.21
  158.0 0.0 copy-done.16
  158.0 0.1 copy.18
  158.1 86.7 %exchange.2.coarse_ref = bf16[128,16,128]{2,1,0:T(8,128)(2,1)} custom-call(bf16[128,16,128]{2,1,0:T(8,128)(2,1)} %bitcast.13), custom_call_target="tpu_custom_call" | custom-call | bytes 67108864 | tf_op jit(solution)/shard_map/exchange/pallas_call | solution.py:84
  244.8 0.1 copy.19
  244.9 0.1 reshape.33.source_ref
  245.0 0.1 copy.20
  245.1 0.1 reshape.34.offset_ref
  245.2 0.0 copy-done.19
  245.2 0.1 copy.22
  245.3 0.0 copy-start.13
  245.3 0.7 broadcast_in_dim.15.weight_ref
  246.1 0.3 copy-done.13
  246.4 9.9 %translate.1.x_ref = bf16[128,16,128]{2,1,0:T(8,128)(2,1)S(1)} custom-call(s32[4096]{0:T(1024)S(1)} %reshape.33.source_ref, s32[4096]{0:T(1024)S(1)} %reshape.34.offset_ref, bf16[128,16,128]{2,1,0:T(8,128)(2,1)S(1)} %copy-done.13, f32[317,16,128]{2,1,0:T(8,128)S(1)} %broadcast_in_dim.15.weight_ref), custom_call_target="tpu_custom_call" | custom-call | flops 2000000000 | bytes 41943040 | tf_op jit(solution)/shard_map/translate/pallas_call | solution.py:162
  256.3 0.0 copy-start.14
  256.3 0.8 copy-done.14
  257.1 32.7 %exchange.3 = bf16[128,16,128]{2,1,0:T(8,128)(2,1)} custom-call(bf16[128,16,128]{2,1,0:T(8,128)(2,1)} %copy-done.14), custom_call_target="tpu_custom_call" | custom-call | bytes 67108864 | tf_op jit(solution)/shard_map/exchange/pallas_call | solution.py:84
  289.8 0.0 copy-done.22
  289.8 0.1 reshape.29.source_ref
  289.9 0.0 copy-done.23
  289.9 0.1 reshape.30.offset_ref
  290.0 0.0 copy-done.10
  290.0 0.0 copy-done.17
  290.0 0.0 copy-start.1
  290.0 1.0 copy-done.1
  291.0 1.6 copy-done.6
  292.6 1.6 copy-done.8
  294.2 1.1 copy-done.11
  295.3 52.4 %downward.1.base_ref = f32[64,128,128]{2,1,0:T(8,128)} custom-call(s32[128]{0:T(128)S(1)} %reshape.29.source_ref, s32[128]{0:T(128)S(1)} %reshape.30.offset_ref, bf16[64,128,128]{2,1,0:T(8,128)(2,1)S(1)} %bitcast.12, bf16[64,128,128]{2,1,0:T(8,128)(2,1)} %collective-permute-done.mate, bf16[64,128,128]{2,1,0:T(8,128)(2,1)S(1)} %copy-done.6, ...), custom_call_target="tpu_custom_call" | custom-call | flops 8999999488 | bytes 62914560 | tf_op jit(solution)/shard_map/downward/pallas_call | solution.py:329
  347.7 0.0 collective-permute-done.5.back_ref
  347.7 4.0 %add_rows.1 = f32[64,128,128]{2,1,0:T(8,128)} custom-call(s32[1]{0:T(128)} %bitcast._, f32[64,128,128]{2,1,0:T(8,128)} %downward.1.base_ref, bf16[64,64,128]{2,1,0:T(8,128)(2,1)} %collective-permute-done.5.back_ref), custom_call_target="tpu_custom_call", output_to_operand_aliasing={{}: (1, {})} | custom-call | bytes 5242880 | tf_op jit(solution)/shard_map/add_rows/pallas_call | solution.py:376
  (16 shorter events, 0.0 us)
Async XLA Ops:
  0.0 31.6 %collective-permute-start.1 = (bf16[64,128,128]{2,1,0:T(8,128)(2,1)}, bf16[64,128,128]{2,1,0:T(8,128)(2,1)S(1)}, u32[]{:S(2)}, u32[]{:S(2)}) collective-permute-start(bf16[64,128,128]{2,1,0:T(8,128)(2,1)} %bitcast.8), channel_id=1, source_target_pairs={{0,255},{1,254},{2,4},{3,5},{4,2},{5,3},{6,8},{7,9},{8,6},{9,7},{1... | collective-permute-start | bytes 6291464 | tf_op jit(solution)/shard_map/ppermute | solution.py:412
  31.6 73.4 %collective-permute-start.2 = (bf16[64,128,128]{2,1,0:T(8,128)(2,1)S(1)}, bf16[64,128,128]{2,1,0:T(8,128)(2,1)}, u32[]{:S(2)}, u32[]{:S(2)}) collective-permute-start(bf16[64,128,128]{2,1,0:T(8,128)(2,1)S(1)} %collective-permute-done.1.first), channel_id=1, source_target_pairs={{255,1},{254,0},{4,3},{5,2},{2,5},{3,4},{8,7},{9,6},{6,9},{7,8},{1... | collective-permute-start | bytes 6291464 | tf_op jit(solution)/shard_map/ppermute | solution.py:414
  36.4 1.3 copy-start.4
  37.7 102.3 %collective-permute-start = (bf16[64,128,128]{2,1,0:T(8,128)(2,1)}, bf16[64,128,128]{2,1,0:T(8,128)(2,1)}, u32[]{:S(2)}, u32[]{:S(2)}) collective-permute-start(bf16[64,128,128]{2,1,0:T(8,128)(2,1)} %bitcast.9), channel_id=1, source_target_pairs={{0,2},{2,0},{4,6},{6,4},{8,10},{10,8},{12,14},{14,12},{16,18},{18,... | collective-permute-start | bytes 6291464 | tf_op jit(solution)/shard_map/ppermute | solution.py:413
  105.0 35.0 %collective-permute-start.3 = (bf16[64,128,128]{2,1,0:T(8,128)(2,1)}, bf16[64,128,128]{2,1,0:T(8,128)(2,1)}, u32[]{:S(2)}, u32[]{:S(2)}) collective-permute-start(bf16[64,128,128]{2,1,0:T(8,128)(2,1)} %collective-permute-done.2.partner), channel_id=1, source_target_pairs={{1,254},{0,255},{3,5},{2,4},{5,3},{4,2},{7,9},{6,8},{9,7},{8,6},{1... | collective-permute-start | bytes 6291464 | tf_op jit(solution)/shard_map/ppermute | solution.py:416
  115.2 24.8 %collective-permute-start.4 = (bf16[64,128,128]{2,1,0:T(8,128)(2,1)}, bf16[64,128,128]{2,1,0:T(8,128)(2,1)}, u32[]{:S(2)}, u32[]{:S(2)}) collective-permute-start(bf16[64,128,128]{2,1,0:T(8,128)(2,1)} %collective-permute-done.2.partner), channel_id=1, source_target_pairs={{0,2},{2,0},{4,6},{6,4},{8,10},{10,8},{12,14},{14,12},{16,18},{18,... | collective-permute-start | bytes 6291464 | tf_op jit(solution)/shard_map/ppermute | solution.py:415
  116.1 5.8 %copy-start = (bf16[8,2048,512]{2,1,0:T(8,128)(2,1)S(1)}, bf16[8,2048,512]{2,1,0:T(8,128)(2,1)}, u32[]{:S(2)}) copy-start(bf16[8,2048,512]{2,1,0:T(8,128)(2,1)} %two_ref.3) | copy-start | bytes 50331652
  121.9 1.6 copy-start.2
  123.5 1.2 copy-start.9
  124.7 0.8 copy-start.15
  125.5 14.5 %copy-start.3 = (bf16[1,64,128,128]{3,2,1,0:T(8,128)(2,1)S(1)}, bf16[1,64,128,128]{3,2,1,0:T(8,128)(2,1)}, u32[]{:S(2)}) copy-start(bf16[1,64,128,128]{3,2,1,0:T(8,128)(2,1)} %param.13) | copy-start | bytes 6291460
  125.5 14.5 %copy-start.5 = (bf16[64,128,128]{2,1,0:T(8,128)(2,1)S(1)}, bf16[64,128,128]{2,1,0:T(8,128)(2,1)}, u32[]{:S(2)}) copy-start(bf16[64,128,128]{2,1,0:T(8,128)(2,1)} %copy-done.4) | copy-start | bytes 6291460
  125.5 32.5 %copy-start.20 = (s32[128,32]{0,1:T(8,128)S(1)}, s32[128,32]{0,1:T(8,128)}, u32[]{:S(2)}) copy-start(s32[128,32]{0,1:T(8,128)} %param.25) | copy-start | bytes 49156
  125.5 32.5 %copy-start.21 = (s32[128,32]{0,1:T(8,128)S(1)}, s32[128,32]{0,1:T(8,128)}, u32[]{:S(2)}) copy-start(s32[128,32]{0,1:T(8,128)} %param.24) | copy-start | bytes 49156
  125.5 119.7 %copy-start.19 = (f32[316,16]{0,1:T(8,128)S(1)}, f32[316,16]{0,1:T(8,128)}, u32[]{:S(2)}) copy-start(f32[316,16]{0,1:T(8,128)} %param.23) | copy-start | bytes 60676
  140.0 13.7 %copy-start.12 = (bf16[2048,128]{1,0:T(8,128)(2,1)}, bf16[2048,128]{1,0:T(8,128)(2,1)S(1)}, u32[]{:S(2)}) copy-start(bf16[2048,128]{1,0:T(8,128)(2,1)S(1)} %upward.1) | copy-start | bytes 1572868
  140.0 18.0 %copy-start.16 = (bf16[128,128]{1,0:T(8,128)(2,1)S(1)}, bf16[128,128]{1,0:T(8,128)(2,1)}, u32[]{:S(2)}) copy-start(bf16[128,128]{1,0:T(8,128)(2,1)} %radiate_ref.3) | copy-start | bytes 98308
  140.0 2.9 copy-start.18
  153.6 1.4 copy-start.7
  155.0 192.7 %collective-permute-start.5 = (bf16[64,64,128]{2,1,0:T(8,128)(2,1)}, bf16[64,64,128]{2,1,0:T(8,128)(2,1)}, u32[]{:S(2)}, u32[]{:S(2)}) collective-permute-start(bf16[64,64,128]{2,1,0:T(8,128)(2,1)} %get-tuple-element.8), channel_id=1, source_target_pairs={{0,1},{1,0},{2,3},{3,2},{4,5},{5,4},{6,7},{7,6},{8,9},{9,8},{10,11... | collective-permute-start | bytes 3145736 | tf_op jit(solution)/shard_map/ppermute | solution.py:424
  245.3 1.0 copy-start.13
  246.3 43.5 %copy-start.22 = (s32[8,16]{1,0:T(8,128)S(1)}, s32[8,16]{1,0:T(8,128)}, u32[]{:S(2)}) copy-start(s32[8,16]{1,0:T(8,128)} %param.21) | copy-start | bytes 1540
  246.3 43.6 %copy-start.23 = (s32[8,16]{1,0:T(8,128)S(1)}, s32[8,16]{1,0:T(8,128)}, u32[]{:S(2)}) copy-start(s32[8,16]{1,0:T(8,128)} %param.22) | copy-start | bytes 1540
  246.3 43.6 %copy-start.10 = (bf16[8,512,128]{2,1,0:T(8,128)(2,1)S(1)}, bf16[8,512,128]{2,1,0:T(8,128)(2,1)}, u32[]{:S(2)}) copy-start(bf16[8,512,128]{2,1,0:T(8,128)(2,1)} %one_ref.3) | copy-start | bytes 3145732
  246.4 43.6 %copy-start.17 = (f32[1,2]{1,0:T(1,128)S(1)}, f32[1,2]{1,0:T(1,128)}, u32[]{:S(2)}) copy-start(f32[1,2]{1,0:T(1,128)} %param.14) | copy-start | bytes 28
  256.3 0.8 copy-start.14
  290.0 1.0 copy-start.1
  291.0 1.6 copy-start.6
  292.6 1.6 copy-start.8
  294.2 1.1 copy-start.11

commit v2 on v1

v2 whole, which is shorter than its diff:
```python
import functools

import jax
import jax.numpy as jnp
from jax import lax
from jax.experimental import pallas as pl
from jax.experimental.pallas import tpu as pltpu
from jax.sharding import PartitionSpec as P

BF = jnp.bfloat16
F32 = jnp.float32
MIB = 1 << 20
ANY = pl.BlockSpec(memory_space=pl.ANY)
VMEM = pl.BlockSpec(memory_space=pltpu.VMEM)
BOTH = ("box", "shift")
DEPTH = 4


def dot(a, b):
    return jnp.dot(a, b, preferred_element_type=F32)


def dot_nt(a, b):
    return lax.dot_general(a, b, (((1,), (1,)), ((), ())), preferred_element_type=F32)


def routes(boxes):
    chips = boxes // 2

    def flat(chip, core, shift):
        return (chip % chips * 2 + core) * 2 + shift

    hops = ([], [], [])
    for chip in range(chips):
        for core in range(2):
            wraps = chip % DEPTH == (DEPTH - 1 if core else 0)
            beside = chip + (1 if core else -1)
            for shift in range(2):
                stops = [
                    flat(chip, core, shift),
                    flat(beside, 1 - core, 1 - shift if wraps else shift),
                    flat(chip, core, 1 - shift),
                    flat(beside, 1 - core, shift if wraps else 1 - shift),
                ]
                for hop in range(3):
                    hops[hop].append((stops[hop], stops[hop + 1]))
    return hops


def place():
    me = lax.axis_index("box")
    core = lax.rem(me, 2)
    depth = lax.rem(lax.div(me, 2), DEPTH)
    wraps = jnp.where(core == 0, depth == 0, depth == DEPTH - 1).astype(jnp.int32)
    return me, core, wraps


def exchange_kernel(chips, parts, x_ref, *refs):
    sources, refs = refs[:parts], refs[parts:]
    o_ref, refs = refs[0], refs[1:]
    to_mate, refs = refs[:parts], refs[parts:]
    to_neighbour, refs = refs[:parts], refs[parts:]
    held, send, recv, mate_send, mate_recv, local, part_send, part_recv = refs
    me, core, wraps = place()
    shift = lax.axis_index("shift")
    chip = lax.div(me, 2)
    mate = me + 1 - 2 * core
    beside = lax.rem(chip + chips - 1 + 2 * core, chips) * 2 + 1 - core
    beside_shift = shift + wraps * (1 - 2 * shift)
    barrier = pltpu.get_barrier_semaphore()

    def greet(box, along):
        pl.semaphore_signal(
            barrier, inc=1, device_id=(box, along), device_id_type=pl.DeviceIdType.MESH
        )

    greet(mate, shift)
    if parts:
        greet(beside, beside_shift)

    @pl.loop(1, chips)
    def _(step):
        greet(lax.rem(chip + step, chips) * 2 + core, shift)

    own = pltpu.make_async_copy(x_ref.at[:, core], held.at[:, core], local)
    own.start()
    pl.semaphore_wait(barrier, chips + (1 if parts else 0))
    across = pltpu.make_async_remote_copy(
        x_ref.at[:, 1 - core],
        held.at[:, core],
        mate_send,
        mate_recv,
        device_id=(mate, shift),
        device_id_type=pl.DeviceIdType.MESH,
    )
    across.start()
    own.wait()
    across.wait()

    @pl.loop(1, chips)
    def _(step):
        other = lax.rem(chip + step, chips)
        pltpu.make_async_remote_copy(
            held.at[other],
            o_ref.at[chip],
            send,
            recv,
            device_id=(other * 2 + core, shift),
            device_id_type=pl.DeviceIdType.MESH,
        ).start()

    moves = []
    for i in range(parts):
        for j, (ref, device) in enumerate(
            ((to_neighbour[i], (beside, beside_shift)), (to_mate[i], (mate, shift)))
        ):
            move = pltpu.make_async_remote_copy(
                sources[i],
                ref,
                part_send.at[2 * i + j],
                part_recv.at[2 * i + j],
                device_id=device,
                device_id_type=pl.DeviceIdType.MESH,
            )
            move.start()
            moves.append(move)
    own = pltpu.make_async_copy(held.at[chip], o_ref.at[chip], local)
    own.start()
    own.wait()
    rest = pl.ds(0, chips - 1)
    pltpu.make_async_copy(held.at[rest], held.at[rest], send).wait()
    pltpu.make_async_copy(o_ref.at[rest], o_ref.at[rest], recv).wait()
    for move in moves:
        move.wait()


def exchange(blocks, *parts):
    count, samples, r = blocks.shape
    shape = (count // 2, 2, samples, r)
    n = len(parts)
    blocks, *moved = pl.pallas_call(
        functools.partial(exchange_kernel, count // 2, n),
        out_shape=[jax.ShapeDtypeStruct(shape, BF)]
        + [jax.ShapeDtypeStruct(part.shape, BF) for part in parts] * 2,
        in_specs=[VMEM] + [ANY] * n,
        out_specs=[VMEM] + [ANY] * (2 * n),
        scratch_shapes=[pltpu.VMEM(shape, BF)]
        + [pltpu.SemaphoreType.DMA] * 5
        + [pltpu.SemaphoreType.DMA((max(2 * n, 1),))] * 2,
        compiler_params=pltpu.CompilerParams(
            has_side_effects=True, collective_id=1 if n else 0, vmem_limit_bytes=56 * MIB
        ),
        cost_estimate=pl.CostEstimate(flops=0, bytes_accessed=80 * MIB, transcendentals=0),
        name="exchange",
    )(blocks.reshape(shape), *parts)
    return blocks.reshape(count, samples, r), *moved


def identity(n):
    shape = (n, n)
    same = lax.broadcasted_iota(jnp.int32, shape, 0) == lax.broadcasted_iota(jnp.int32, shape, 1)
    return same.astype(BF)


def two_parents(x_of, radiate, one_ref):
    total = None
    for pair in range(4):
        leaves = [
            dot(radiate, jnp.concatenate([x_of(o), x_of(8 + o)], axis=1)).astype(BF)
            for o in (2 * pair, 2 * pair + 1)
        ]
        lhs = jnp.concatenate([one_ref[2 * pair], one_ref[2 * pair + 1]], axis=1)
        term = dot(lhs, jnp.concatenate(leaves, axis=0))
        total = term if total is None else total + term
    return total


def upward_kernel(x_ref, radiate_ref, one_ref, two_ref, coarse_ref, patterns_ref, total):
    step = pl.program_id(0)
    upper = two_parents(lambda i: x_ref[i], radiate_ref[...], one_ref).astype(BF)
    r = x_ref.shape[2]
    left, right = upper[:, :r], upper[:, r:]
    term = dot(two_ref[0], left) + dot(two_ref[1], right)

    @pl.when(step == 0)
    def _():
        total[...] = term

    @pl.when(step > 0)
    def _():
        total[...] += term

    eye = identity(r)
    patterns_ref[0] = dot_nt(eye, left).astype(BF)
    patterns_ref[1] = dot_nt(eye, right).astype(BF)

    @pl.when(step == pl.num_programs(0) - 1)
    def _():
        coarse_ref[...] = total[...].astype(BF)


def upward(x, radiate, one, two):
    octants, k2, k1 = two.shape
    count, u, r = x.shape
    return pl.pallas_call(
        upward_kernel,
        grid=(octants // 2,),
        out_shape=[
            jax.ShapeDtypeStruct((k2, r), BF),
            jax.ShapeDtypeStruct((count // 8, r, k1), BF),
        ],
        in_specs=[
            pl.BlockSpec((16, u, r), lambda i: (i, 0, 0)),
            VMEM,
            VMEM,
            pl.BlockSpec((2, k2, k1), lambda i: (i, 0, 0)),
        ],
        out_specs=[
            pl.BlockSpec((k2, r), lambda i: (0, 0)),
            pl.BlockSpec((2, r, k1), lambda i: (i, 0, 0)),
        ],
        scratch_shapes=[pltpu.VMEM((k2, r), F32)],
        compiler_params=pltpu.CompilerParams(vmem_limit_bytes=56 * MIB),
        cost_estimate=pl.CostEstimate(flops=7_000_000_000, bytes_accessed=50 * MIB, transcendentals=0),
        name="upward",
    )(x, radiate, one, two)


def fill_patterns(x_of, patterns, at, radiate, one_ref):
    for pair in range(2):
        upper = two_parents(lambda i: x_of(16 * pair + i), radiate, one_ref).astype(BF)
        r = upper.shape[1] // 2
        eye = identity(r)
        patterns[at + 2 * pair] = dot_nt(eye, upper[:, :r]).astype(BF)
        patterns[at + 2 * pair + 1] = dot_nt(eye, upper[:, r:]).astype(BF)


def beside_kernel(_, mate_ref, a_ref, b_ref, radiate_ref, one_ref, patterns_ref):
    step = pl.program_id(0)
    for when, ref in ((step < 2, mate_ref), (step == 2, a_ref), (step == 3, b_ref)):

        @pl.when(when)
        def _(ref=ref):
            fill_patterns(lambda i: ref[i], patterns_ref, 0, radiate_ref[...], one_ref)


def patterns_beside(core, mate, first_a, first_b, radiate, one):
    count, u, r = mate.shape
    _, k1, k0 = one.shape

    def where(i, core):
        towards = 4 * core[0]
        return (jnp.where(i < 2, 4 - towards + i, towards + jnp.where(i == 2, 1 - core[0], core[0])), 0, 0)

    whole = pl.BlockSpec((count // 2, u, r), lambda i, _: (0, 0, 0))
    return pl.pallas_call(
        beside_kernel,
        out_shape=jax.ShapeDtypeStruct((3 * count // 8, r, k1), BF),
        grid_spec=pltpu.PrefetchScalarGridSpec(
            num_scalar_prefetch=1,
            grid=(4,),
            in_specs=[
                pl.BlockSpec((count // 2, u, r), lambda i, _: (jnp.minimum(i, 1), 0, 0)),
                whole,
                whole,
                VMEM,
                VMEM,
            ],
            out_specs=pl.BlockSpec((count // 16, r, k1), where),
        ),
        compiler_params=pltpu.CompilerParams(vmem_limit_bytes=56 * MIB),
        cost_estimate=pl.CostEstimate(flops=4_000_000_000, bytes_accessed=30 * MIB, transcendentals=0),
        name="patterns_beside",
    )(core, mate, first_a, first_b, radiate, one)


def translate_kernel(width, source_ref, offset_ref, rounds_ref, coarse_ref, weight_ref, out_ref):
    @pl.loop(0, out_ref.shape[0])
    def _(box):
        def four(step, total):
            for j in range(4):
                at = box * width + step * 4 + j
                total += weight_ref[offset_ref[at]] * coarse_ref[source_ref[at]].astype(F32)
            return total

        start = jnp.zeros(out_ref.shape[1:], F32)
        out_ref[box] = lax.fori_loop(0, rounds_ref[box], four, start).astype(BF)


def translation_lists(table, source, offset, columns):
    classes, samples = table.shape
    live = source >= 0
    rounds = (jnp.sum(live.astype(jnp.int32), axis=1) + 3) // 4
    weights = jnp.broadcast_to(
        jnp.pad(table, ((0, 1), (0, 0)))[:, :, None], (classes + 1, samples, columns)
    )
    return (
        jnp.where(live, source, 0).reshape(-1),
        jnp.where(live, offset, classes).reshape(-1),
        rounds,
        weights,
    )


def translate(coarse, source, offset, rounds, weights):
    return pl.pallas_call(
        functools.partial(translate_kernel, source.shape[0] // coarse.shape[0]),
        out_shape=jax.ShapeDtypeStruct(coarse.shape, BF),
        grid_spec=pltpu.PrefetchScalarGridSpec(
            num_scalar_prefetch=3, grid=(), in_specs=[VMEM, VMEM], out_specs=VMEM
        ),
        compiler_params=pltpu.CompilerParams(vmem_limit_bytes=16 * MIB),
        cost_estimate=pl.CostEstimate(flops=2_000_000_000, bytes_accessed=25 * MIB, transcendentals=0),
        name="translate",
    )(source, offset, rounds, coarse, weights)


def near_kernel(group, slots, part, index_ref, halves_ref, blocks_ref, *refs):
    sources, (own_ref, other_ref, held, sems) = refs[:-4], refs[-4:]
    step = pl.program_id(0)
    me, core, wraps = place()
    count = sources[0].shape[0]
    half = count // 2

    @pl.when(step == 0)
    def _():
        towards = 2 * core * count
        within = 2 * count - towards
        upper, lower = half * (1 - core), half * core
        places = (
            (0, count),
            (0, within),
            (1, count + lower),
            (1, count + upper),
            (1, within + upper),
            (1, within + lower),
            (wraps, towards + upper),
            (1 - wraps, towards + upper),
            (wraps, towards + lower),
            (1 - wraps, towards + lower),
        )
        copies = [
            pltpu.make_async_copy(src, held.at[kind, pl.ds(at, src.shape[0])], sems.at[i])
            for i, (src, (kind, at)) in enumerate(zip(sources, places))
        ]
        for copy in copies:
            copy.start()
        zero = jnp.zeros(held.shape[2:], BF)
        held[0, 3 * count] = zero
        held[1, 3 * count] = zero
        for copy in copies:
            copy.wait()

    base = me * count - count
    origin = halves_ref[part] * half + step * group
    for b in range(group):
        total = None
        for pair in range(slots // 2):
            rows = []
            for i in range(2):
                at = index_ref[(origin + b) * slots + 2 * pair + i]
                at = jnp.where(at >= 0, at - base, 3 * count)
                rows.append(jnp.concatenate([held[0, at], held[1, at]], axis=1))
            lhs = jnp.concatenate([blocks_ref[b, 2 * pair], blocks_ref[b, 2 * pair + 1]], axis=1)
            term = dot(lhs, jnp.concatenate(rows, axis=0))
            total = term if total is None else total + term
        r = own_ref.shape[2]
        own_ref[b] = total[:, :r]
        other_ref[b] = total[:, r:].astype(BF)


def near_field(part, halves, index, blocks, *sources):
    count, slots, rows, u = blocks.shape
    r = sources[0].shape[2]
    group = 8
    steps = count // 2 // group
    out = pl.BlockSpec((group, rows, r), lambda i, *_: (i, 0, 0))
    return pl.pallas_call(
        functools.partial(near_kernel, group, slots, part),
        out_shape=[
            jax.ShapeDtypeStruct((count // 2, rows, r), F32),
            jax.ShapeDtypeStruct((count // 2, rows, r), BF),
        ],
        grid_spec=pltpu.PrefetchScalarGridSpec(
            num_scalar_prefetch=2,
            grid=(steps,),
            in_specs=[
                pl.BlockSpec((group, slots, rows, u), lambda i, _, h: (h[part] * steps + i, 0, 0, 0))
            ]
            + [ANY] * len(sources),
            out_specs=[out, out],
            scratch_shapes=[
                pltpu.VMEM((2, 3 * count + 1, u, r), BF),
                pltpu.SemaphoreType.DMA((len(sources),)),
            ],
        ),
        compiler_params=pltpu.CompilerParams(vmem_limit_bytes=56 * MIB),
        cost_estimate=pl.CostEstimate(flops=3_000_000_000, bytes_accessed=20 * MIB, transcendentals=0),
        name="near_field",
    )(index, halves, blocks, *sources)


def local_step(
    width, step, source_ref, offset_ref, last_a, last_b, mine, beside, radiate_ref, one_ref, two_ref,
    table_ref, incoming_ref, held, patterns, flat, weights, across, local, sems,
):
    me, core, wraps = place()
    count, u, r = held.shape
    parents = count // 8
    half = count // 2

    @pl.when(step == 0)
    def _():
        towards = 2 * core * parents
        within = pl.ds(2 * parents - towards, parents)
        center = pl.ds(parents, parents)
        copies = [
            pltpu.make_async_copy(mine, patterns.at[center], sems.at[0]),
            pltpu.make_async_copy(beside.at[within], patterns.at[within], sems.at[1]),
        ]
        for copy in copies:
            copy.start()
        flat[...] = dot_nt(identity(r), incoming_ref[...]).astype(BF)

        @pl.when(wraps == 0)
        def _():
            there = pl.ds(towards, parents)
            copy = pltpu.make_async_copy(beside.at[there], patterns.at[there], sems.at[2])
            copy.start()
            copy.wait()

        @pl.when(wraps == 1)
        def _():
            halves = [
                pltpu.make_async_copy(last_a, held.at[pl.ds(half * (1 - core), half)], sems.at[2]),
                pltpu.make_async_copy(last_b, held.at[pl.ds(half * core, half)], sems.at[3]),
            ]
            for copy in halves:
                copy.start()
            for copy in halves:
                copy.wait()

            @pl.loop(0, 2)
            def _(i):
                fill_patterns(
                    lambda k: held[i * half + k], patterns, towards + i * 4, radiate_ref[...], one_ref
                )

        for copy in copies:
            copy.wait()

    origin = me * parents - parents
    at = []
    for j in range(width):
        source = source_ref[step * width + j]
        live = source >= 0
        at.append(jnp.where(live, source - origin, parents))
        row = table_ref[pl.ds(offset_ref[step * width + j], 1), :]
        weights[pl.ds(j, 1), :] = row * live.astype(F32)

    @pl.loop(0, r // 16)
    def _(part):
        rows = pl.ds(pl.multiple_of(part * 16, 16), 16)
        total = None
        for j in range(width):
            term = weights[pl.ds(j, 1), :] * patterns[at[j], rows, :].astype(F32)
            total = term if total is None else total + term
        across[rows, :] = total

    local[pl.ds(pl.multiple_of(step * r, r), r), :] = (
        across[...] + dot(flat[...], two_ref[0])
    ).astype(BF)


def downward_kernel(
    width, source_ref, offset_ref, x_ref, last_a, last_b, mine, beside, a_ref, b_ref, sigma_ref,
    radiate_ref, turned_ref, one_ref, two_ref, table_ref, incoming_ref, base_ref,
    held, patterns, flat, weights, across, local, sems,
):
    step = pl.program_id(0)
    parents, _, u, r = x_ref.shape
    rows = u // 2

    @pl.when(step < parents)
    def _():
        local_step(
            width, step, source_ref, offset_ref, last_a, last_b, mine, beside, radiate_ref, one_ref,
            two_ref, table_ref, incoming_ref, held, patterns, flat, weights, across, local, sems,
        )

    @pl.when(step >= parents)
    def _():
        core = lax.rem(lax.axis_index("box"), 2)
        own = pl.ds(pl.multiple_of(lax.axis_index("shift") * rows, rows), rows)
        sig_re, sig_im = sigma_ref[0], sigma_ref[1]
        leaf_in = dot(local[...], one_ref[step - parents]).astype(BF)
        far = dot_nt(turned_ref[...], leaf_in)
        for c in range(parents):
            part = far[:, c * r : (c + 1) * r]
            field = x_ref[c, 0].astype(F32)
            real, imag = field[:rows], field[rows:]
            base_ref[c, 0, :rows] = part[:rows] - (sig_re * real - sig_im * imag)
            base_ref[c, 0, rows:] = part[rows:] - (sig_re * imag + sig_im * real)
            at = c % (parents // 2)
            in_a = core == (1 if c < parents // 2 else 0)
            base_ref[c, 0, own] += jnp.where(in_a, a_ref[at, 0], b_ref[at, 0])


def downward(
    source, offset, x, last_a, last_b, mine, beside, own_a, own_b, sigma, radiate, turned, one, two,
    table, incoming,
):
    octants, k2, k1 = two.shape
    count, u, r = x.shape
    parents = count // 8
    width = source.shape[0] // parents

    def child(i, *_):
        return (0, jnp.maximum(i - parents, 0), 0, 0)

    near = pl.BlockSpec((parents // 2, 1, u // 2, r), child)
    box = pl.BlockSpec((parents, 1, u, r), child)
    return pl.pallas_call(
        functools.partial(downward_kernel, width),
        out_shape=jax.ShapeDtypeStruct((parents, 8, u, r), F32),
        grid_spec=pltpu.PrefetchScalarGridSpec(
            num_scalar_prefetch=2,
            grid=(parents + 8,),
            in_specs=[
                box,
                ANY,
                ANY,
                ANY,
                ANY,
                near,
                near,
                pl.BlockSpec(memory_space=pltpu.SMEM),
                VMEM,
                VMEM,
                VMEM,
                pl.BlockSpec((1, k2, k1), lambda i, *_: (jnp.minimum(i, parents - 1), 0, 0)),
                VMEM,
                VMEM,
            ],
            out_specs=box,
            scratch_shapes=[
                pltpu.VMEM((count, u, r), BF),
                pltpu.VMEM((3 * parents, r, k1), BF),
                pltpu.VMEM((r, k2), BF),
                pltpu.VMEM((width, k1), F32),
                pltpu.VMEM((r, k1), F32),
                pltpu.VMEM((parents * r, k1), BF),
                pltpu.SemaphoreType.DMA((4,)),
            ],
        ),
        compiler_params=pltpu.CompilerParams(vmem_limit_bytes=56 * MIB),
        cost_estimate=pl.CostEstimate(flops=9_000_000_000, bytes_accessed=80 * MIB, transcendentals=0),
        name="downward",
    )(
        source, offset, x.reshape(parents, 8, u, r), last_a, last_b, mine, beside,
        own_a.reshape(parents // 2, 8, u // 2, r), own_b.reshape(parents // 2, 8, u // 2, r),
        sigma.reshape(-1), radiate, turned, one, two, table, incoming,
    ).reshape(count, u, r)


def add_kernel(_, base_ref, back_ref, out_ref):
    out_ref[...] = base_ref[...] + back_ref[...].astype(F32)


def add_rows(where, base, back):
    count, u, r = base.shape
    group = count // 4
    rows = pl.BlockSpec((group, u // 2, r), lambda i, at: (at[0] * 2 + i, at[1], 0))
    return pl.pallas_call(
        add_kernel,
        out_shape=jax.ShapeDtypeStruct((count, u, r), F32),
        grid_spec=pltpu.PrefetchScalarGridSpec(
            num_scalar_prefetch=1,
            grid=(2,),
            in_specs=[rows, pl.BlockSpec((group, u // 2, r), lambda i, at: (i, 0, 0))],
            out_specs=rows,
        ),
        input_output_aliases={1: 0},
        compiler_params=pltpu.CompilerParams(vmem_limit_bytes=16 * MIB),
        cost_estimate=pl.CostEstimate(flops=0, bytes_accessed=3 * MIB, transcendentals=0),
        name="add_rows",
    )(where, base, back)


def after(arrays, *others):
    return lax.optimization_barrier((tuple(arrays), others))[0]


def body(
    vectors,
    sigma,
    near_blocks,
    near_index,
    radiate,
    interp_one,
    interp_two,
    trans_one,
    level1_source,
    level1_offset,
    trans_two,
    level2_source,
    level2_offset,
):
    x = vectors[0]
    count = x.shape[0]
    boxes = lax.axis_size("box")
    k2 = interp_two.shape[1]
    hops = routes(boxes)
    swap = [(i, i ^ 1) for i in range(boxes)]
    partners = [(0, 1), (1, 0)]
    core = lax.rem(lax.axis_index("box"), 2).astype(jnp.int32)
    shift = lax.axis_index("shift").astype(jnp.int32)
    halves = jnp.stack([1 - core, core])
    lists = (
        near_index.reshape(-1),
        level1_source.reshape(-1),
        level1_offset.reshape(-1),
        radiate.T,
        halves,
        jnp.stack([1 - core, 1 - shift]),
        jnp.stack([core, 1 - shift]),
        *translation_lists(trans_two, level2_source, level2_offset, x.shape[2]),
    )

    first_a, first_b = [
        lax.ppermute(lax.dynamic_slice_in_dim(x, at * (count // 2), count // 2), BOTH, hops[0])
        for at in (core, 1 - core)
    ]
    mate = lax.ppermute(x, "box", swap)
    coarse, mine = upward(x, radiate, interp_one, interp_two)

    (first_a,) = after([first_a], coarse)
    partner_a = lax.ppermute(first_a, BOTH, hops[1])
    coarse, *lists = after([coarse, *lists], first_a)
    index, source, offset, turned_radiate, halves, where_a, where_b, *translation = lists
    (gathered,) = exchange(coarse.reshape(boxes, k2 // boxes, -1))

    first_b, partner_a = after([first_b, partner_a], gathered)
    partner_b = lax.ppermute(first_b, BOTH, hops[1])
    turned = translate(gathered, *translation)
    beside = patterns_beside(core.reshape(1), mate, first_a, first_b, radiate, interp_one)
    (turned,) = after([turned], beside)
    incoming, partner_mate_a, partner_mate_b, last_a, last_b = exchange(turned, partner_a, partner_b)
    incoming = incoming.reshape(k2, -1)
    (index,) = after([index], incoming)
    here = (x, mate, partner_a, partner_b, partner_mate_a, partner_mate_b, first_a, last_a)
    own_a, other_a = near_field(0, halves, index, near_blocks, *here)
    back_a = lax.ppermute(other_a, "shift", partners)
    (index,) = after([index], other_a)
    own_b, other_b = near_field(1, halves, index, near_blocks, *here, first_b, last_b)
    back_b = lax.ppermute(other_b, "shift", partners)
    base = downward(
        source, offset, x, last_a, last_b, mine, beside, own_a, own_b, sigma, radiate, turned_radiate,
        interp_one, interp_two, trans_one, incoming,
    )
    base = add_rows(where_a, base, back_a)
    return add_rows(where_b, base, back_b)[None]


def solution(mesh):
    in_specs = (
        P("shift", "box", None, None),
        P("shift", None),
        P("box", None, "shift", None),
        P("box", None),
        P(),
        P(),
        P(),
        P(),
        P("box", None),
        P("box", None),
        P(None, "box"),
        P(),
        P(),
    )
    out_specs = P("shift", "box", None, None)
    return jax.shard_map(body, mesh=mesh, in_specs=in_specs, out_specs=out_specs, check_vma=False)
```

time: 353 us -> 225 us (0.64)
  waiting for transfers between devices: 91.2 us -> 3.95 us
  Pallas kernels: 211 us -> 185 us
  local copies, waits for them, and re-layouts: 23.8 us -> 9.75 us
    ppermute x5 -> x6, waiting for transfers between devices: 91.2 us -> 3.95 us  [the longest x1 2.39 us: body(): partner_b = lax.ppermute(first_b, BOTH, hops[1])]
    pallas_call x1, Pallas kernels: 52.4 us -> 29.2 us  [downward(): pl.pallas_call(functools.partial(downward_kernel, width), out_shape=jax.S...]
    unnamed x51 -> x27, local copies, waits for them, and re-layouts: 22.4 us -> 3.82 us
    pallas_call x5 -> x7, Pallas kernels: 154 us -> 150 us  [the longest x2 91.9 us: exchange(): pl.pallas_call(functools.partial(exchange_kernel, count // 2, n), out_sha...]
    ppermute x5 -> x6, starting transfers between devices: 25.6 us -> 23 us  [the longest x2 7.75 us: body(): lax.ppermute(lax.dynamic_slice_in_dim(x, at * (count // 2), count // 2),...]
  transfers between devices with their start and end apart: 6 -> 7, of which waited for: 2 -> 2; matrix products, arithmetic and copies ran while one was open for 1% -> 2% of each run, Pallas kernels for 56% -> 52%
where the time goes in v2:
time: 225 us; the launch traced here: 222 us
  Pallas kernels  185 us (82%)
  starting transfers between devices  23.1 us (10%)
  local copies, waits for them, and re-layouts  9.75 us (4%)
  waiting for transfers between devices  3.95 us (2%)
    pallas_call x2, Pallas kernels, exchange(): pl.pallas_call(functools.partial(exchange_kernel, count // 2, n), out_sha...  91.9 us
    pallas_call x1, Pallas kernels, downward(): pl.pallas_call(functools.partial(downward_kernel, width), out_shape=jax.S...  29.2 us
    pallas_call x2, Pallas kernels, near_field(): pl.pallas_call(functools.partial(near_kernel, group, slots, part), out_sh...  20.8 us
    pallas_call x1, Pallas kernels, upward(): pl.pallas_call(upward_kernel, grid=(octants // 2,), out_shape=[jax.ShapeD...  15.6 us
    pallas_call x1, Pallas kernels, patterns_beside(): pl.pallas_call(beside_kernel, out_shape=jax.ShapeDtypeStruct((3 * count /...  11.7 us
    pallas_call x1, Pallas kernels, translate(): pl.pallas_call(functools.partial(translate_kernel, source.shape[0] // coa...  10.2 us
    ppermute x2, starting transfers between devices, body(): lax.ppermute(lax.dynamic_slice_in_dim(x, at * (count // 2), count // 2),...  7.75 us
    pallas_call x2, Pallas kernels, add_rows(): pl.pallas_call(add_kernel, out_shape=jax.ShapeDtypeStruct((count, u, r),...  5.23 us
  transfers between devices with their start and end apart: 7, of which 2 were waited for; matrix products, arithmetic and copies ran while one was open for 2% of the time, Pallas kernels for 52%

profile of v2, /device:TPU:2, one launch (start us, length us, event | category | flops | bytes accessed | tf_op | source)
XLA Modules:
  0.0 222.3 jit_solution(14612236020245684044)
XLA Ops:
  0.0 0.0 copy-start.2
  0.0 2.9 %dynamic-slice_bitcast_fusion = (bf16[32,128,128]{2,1,0:T(8,128)(2,1)}, bf16[32,128,128]{2,1,0:T(8,128)(2,1)S(1)}) fusion(bf16[1,64,128,128]{3,2,1,0:T(8,128)(2,1)} %param.13, s32[]{:T(128)S(6)} %select_n.22, s32[]{:T(128)S(6)} %select_n.21), kind=kLoop, calls=%fused_computation | loop fusion | bytes 4194312 | tf_op jit(solution)/shard_map/dynamic_slice | solution.py:631
  2.9 7.7 %collective-permute-start = (bf16[32,128,128]{2,1,0:T(8,128)(2,1)S(1)}, bf16[32,128,128]{2,1,0:T(8,128)(2,1)}, u32[]{:S(2)}, u32[]{:S(2)}) collective-permute-start(bf16[32,128,128]{2,1,0:T(8,128)(2,1)S(1)} %get-tuple-element.64), channel_id=1, source_target_pairs={{0,255},{1,254},{2,4},{3,5},{4,2},{5,3},{6,8},{7,9},{8,6},{9,7},{1... | collective-permute-start | bytes 3145736 | tf_op jit(solution)/shard_map/ppermute | solution.py:631
  10.6 0.0 collective-permute-start.2
  10.7 0.0 copy-done.2
  10.7 0.0 copy-start.5
  10.7 0.0 copy-start.10
  10.7 0.0 copy-start.11
  10.7 0.0 copy-start.9
  10.7 0.0 copy-start.7
  10.7 0.0 copy-start.8
  10.7 0.0 copy-start.6
  10.7 0.1 collective-permute-start.1
  10.8 15.6 %upward.1 = (bf16[2048,128]{1,0:T(8,128)(2,1)}, bf16[8,128,512]{2,1,0:T(8,128)(2,1)}) custom-call(bf16[64,128,128]{2,1,0:T(8,128)(2,1)} %bitcast.22, bf16[128,128]{1,0:T(8,128)(2,1)} %radiate_ref.5, bf16[8,512,128]{2,1,0:T(8,128)(2,1)} %one_ref.5, bf16[8,2048,512]{2,1,0:T(8,128)(2,1)} %two_ref.3), custom_call_target="tpu_custom_call" | custom-call | flops 7000000000 | bytes 52428800 | tf_op jit(solution)/shard_map/upward/pallas_call | solution.py:205
  26.4 0.0 collective-permute-done.a_ref.refs_6_
  26.4 4.8 %collective-permute-start.3 = (bf16[32,128,128]{2,1,0:T(8,128)(2,1)}, bf16[32,128,128]{2,1,0:T(8,128)(2,1)S(1)}, u32[]{:S(2)}, u32[]{:S(2)}) collective-permute-start(bf16[32,128,128]{2,1,0:T(8,128)(2,1)} %collective-permute-done.a_ref.refs_6_), channel_id=1, source_target_pairs={{255,1},{254,0},{4,3},{5,2},{2,5},{3,4},{8,7},{9,6},{6,9},{7,8},{1... | collective-permute-start | bytes 3145736 | tf_op jit(solution)/shard_map/ppermute | solution.py:638
  31.1 0.0 copy-done.5
  31.1 0.7 copy.19
  31.8 0.0 copy-done.10
  31.9 0.7 reshape.38.source_ref
  32.5 0.0 copy-done.11
  32.5 0.6 reshape.39.offset_ref
  33.1 0.0 copy-done.9
  33.1 0.1 copy.18
  33.2 0.7 reshape.37.index_ref
  33.9 0.0 copy-done.7
  33.9 0.0 copy-done.8
  33.9 0.1 copy.20
  34.0 0.1 reshape.40.source_ref
  34.1 0.1 copy.21
  34.2 0.1 reshape.41.offset_ref
  34.3 0.0 copy-done.6
  34.3 0.1 copy.23
  34.4 0.1 pad_add_fusion.2._
  34.5 0.7 pad_add_fusion
  35.2 0.7 broadcast_in_dim.15.weight_ref
  35.9 36.3 %exchange.2 = bf16[64,2,16,128]{3,2,1,0:T(8,128)(2,1)} custom-call(bf16[64,2,16,128]{3,2,1,0:T(8,128)(2,1)} %bitcast.30), custom_call_target="tpu_custom_call" | custom-call | bytes 83886080 | tf_op jit(solution)/shard_map/exchange/pallas_call | solution.py:141
  72.2 0.0 collective-permute-done.2.b_ref.refs_8_
  72.2 0.0 collective-permute-done.3.refs_0_.refs_2_
  72.2 0.0 copy-start.3
  72.2 4.2 %collective-permute-start.4 = (bf16[32,128,128]{2,1,0:T(8,128)(2,1)}, bf16[32,128,128]{2,1,0:T(8,128)(2,1)S(1)}, u32[]{:S(2)}, u32[]{:S(2)}) collective-permute-start(bf16[32,128,128]{2,1,0:T(8,128)(2,1)} %collective-permute-done.2.b_ref.refs_8_), channel_id=1, source_target_pairs={{255,1},{254,0},{4,3},{5,2},{2,5},{3,4},{8,7},{9,6},{6,9},{7,8},{1... | collective-permute-start | bytes 3145736 | tf_op jit(solution)/shard_map/ppermute | solution.py:644
  76.4 0.0 copy-start.1
  76.4 1.0 copy-done.1
  77.4 10.2 %translate.1 = bf16[128,16,128]{2,1,0:T(8,128)(2,1)S(1)} custom-call(s32[4096]{0:T(1024)S(1)} %reshape.40.source_ref, s32[4096]{0:T(1024)S(1)} %reshape.41.offset_ref, s32[128]{0:T(128)S(1)} %and_select_fusion.rounds_ref, bf16[128,16,128]{2,1,0:T(8,128)(2,1)S(1)} %bitcast.20, f32[317,16,128]{2,1,0:T(8,128)S(1)} %broadcast_in_dim.15.weight_ref), custom_call_target="tpu_custom_call" | custom-call | flops 2000000000 | bytes 26214400 | tf_op jit(solution)/shard_map/translate/pallas_call | solution.py:306
  87.6 0.0 copy-start
  87.6 0.8 copy-done
  88.4 0.0 collective-permute-done.1.mate_ref.refs_1_
  88.4 11.7 %patterns_beside.1.beside = bf16[24,128,512]{2,1,0:T(8,128)(2,1)} custom-call(s32[1]{0:T(128)} %bitcast.3._, bf16[64,128,128]{2,1,0:T(8,128)(2,1)} %collective-permute-done.1.mate_ref.refs_1_, bf16[32,128,128]{2,1,0:T(8,128)(2,1)} %collective-permute-done.a_ref.refs_6_, bf16[32,128,128]{2,1,0:T(8,128)(2,1)} %collective-permute-done.2.b_ref.refs_8_, ...), custom_call_target="tpu_custom_call" | custom-call | flops 4000000000 | bytes 31457280 | tf_op jit(solution)/shard_map/patterns_beside/pallas_call | solution.py:256
  100.1 0.0 copy-done.3
  100.1 2.4 %collective-permute-done.4.refs_1_.refs_3_ = bf16[32,128,128]{2,1,0:T(8,128)(2,1)S(1)} collective-permute-done((bf16[32,128,128]{2,1,0:T(8,128)(2,1)}, bf16[32,128,128]{2,1,0:T(8,128)(2,1)S(1)}, u32[]{:S(2)}, u32[]{:S(2)}) %collective-permute-start.4) | collective-permute-done | bytes 1048608 | tf_op jit(solution)/shard_map/ppermute | solution.py:644
  102.5 0.0 copy-start.4
  102.5 1.0 copy-done.4
  103.5 55.6 %exchange.3 = (bf16[64,2,16,128]{3,2,1,0:T(8,128)(2,1)}, bf16[32,128,128]{2,1,0:T(8,128)(2,1)}, bf16[32,128,128]{2,1,0:T(8,128)(2,1)}, bf16[32,128,128]{2,1,0:T(8,128)(2,1)}, bf16[32,128,128]{2,1,0:T(8,128)(2,1)}) custom-call(bf16[64,2,16,128]{3,2,1,0:T(8,128)(2,1)} %bitcast.19, bf16[32,128,128]{2,1,0:T(8,128)(2,1)} %copy-done.3, bf16[32,128,128]{2,1,0:T(8,128)(2,1)} %copy-done.4), custom_call_target="tpu_custom_call" | custom-call | bytes 83886080 | tf_op jit(solution)/shard_map/exchange/pallas_call | solution.py:141
  159.2 10.1 %near_field.2 = (f32[32,64,128]{2,1,0:T(8,128)}, bf16[32,64,128]{2,1,0:T(8,128)(2,1)}) custom-call(s32[384]{0:T(512)} %reshape.37.index_ref, s32[2]{0:T(128)} %get-tuple-element.54.halves_ref, bf16[64,6,64,128]{3,2,1,0:T(8,128)(2,1)} %blocks_ref.3, bf16[64,128,128]{2,1,0:T(8,128)(2,1)} %bitcast.23, ...), custom_call_target="tpu_custom_call" | custom-call | flops 3000000000 | bytes 20971520 | tf_op jit(solution)/shard_map/near_field/pallas_call | solution.py:378
  169.3 2.7 %collective-permute-start.5 = (bf16[32,64,128]{2,1,0:T(8,128)(2,1)}, bf16[32,64,128]{2,1,0:T(8,128)(2,1)S(1)}, u32[]{:S(2)}, u32[]{:S(2)}) collective-permute-start(bf16[32,64,128]{2,1,0:T(8,128)(2,1)} %get-tuple-element.58), channel_id=1, source_target_pairs={{0,1},{1,0},{2,3},{3,2},{4,5},{5,4},{6,7},{7,6},{8,9},{9,8},{10,11... | collective-permute-start | bytes 1572872 | tf_op jit(solution)/shard_map/ppermute | solution.py:653
  171.9 10.7 %near_field.3 = (f32[32,64,128]{2,1,0:T(8,128)}, bf16[32,64,128]{2,1,0:T(8,128)(2,1)}) custom-call(s32[384]{0:T(512)} %reshape.37.index_ref, s32[2]{0:T(128)} %get-tuple-element.54.halves_ref, bf16[64,6,64,128]{3,2,1,0:T(8,128)(2,1)} %blocks_ref.3, bf16[64,128,128]{2,1,0:T(8,128)(2,1)} %bitcast.24, ...), custom_call_target="tpu_custom_call" | custom-call | flops 3000000000 | bytes 20971520 | tf_op jit(solution)/shard_map/near_field/pallas_call | solution.py:378
  182.7 3.6 %collective-permute-start.6 = (bf16[32,64,128]{2,1,0:T(8,128)(2,1)}, bf16[32,64,128]{2,1,0:T(8,128)(2,1)S(1)}, u32[]{:S(2)}, u32[]{:S(2)}) collective-permute-start(bf16[32,64,128]{2,1,0:T(8,128)(2,1)} %get-tuple-element.62), channel_id=1, source_target_pairs={{0,1},{1,0},{2,3},{3,2},{4,5},{5,4},{6,7},{7,6},{8,9},{9,8},{10,11... | collective-permute-start | bytes 1572872 | tf_op jit(solution)/shard_map/ppermute | solution.py:656
  186.3 29.2 %downward.1 = f32[8,8,128,128]{3,2,1,0:T(8,128)} custom-call(s32[128]{0:T(128)} %reshape.38.source_ref, s32[128]{0:T(128)} %reshape.39.offset_ref, bf16[8,8,128,128]{3,2,1,0:T(8,128)(2,1)} %bitcast.25, bf16[32,128,128]{2,1,0:T(8,128)(2,1)} %get-tuple-element.48.refs_7_.last_a, bf16[32,128,128]{2,1,0:T(8,128)(2,1)} %get-tuple-element.49.refs_9_.last_b, ...), custom_call_target="tpu_custom_call" | custom-call | flops 8999999488 | bytes 83886080 | tf_op jit(solution)/shard_map/downward/pallas_call | solution.py:523
  215.5 0.0 collective-permute-done.5.back_ref
  215.5 2.6 %add_rows.2.base_ref = f32[64,128,128]{2,1,0:T(8,128)} custom-call(s32[2]{0:T(128)S(1)} %pad_add_fusion.2._, f32[64,128,128]{2,1,0:T(8,128)} %bitcast.21, bf16[32,64,128]{2,1,0:T(8,128)(2,1)S(1)} %collective-permute-done.5.back_ref), custom_call_target="tpu_custom_call", output_to_operand_aliasing={{}: (1, {})} | custom-call | bytes 3145728 | tf_op jit(solution)/shard_map/add_rows/pallas_call | solution.py:574
  218.1 1.5 collective-permute-done.6.back_ref
  219.7 2.6 %add_rows.3 = f32[64,128,128]{2,1,0:T(8,128)} custom-call(s32[2]{0:T(128)S(1)} %get-tuple-element.36._, f32[64,128,128]{2,1,0:T(8,128)} %add_rows.2.base_ref, bf16[32,64,128]{2,1,0:T(8,128)(2,1)S(1)} %collective-permute-done.6.back_ref), custom_call_target="tpu_custom_call", output_to_operand_aliasing={{}: (1, {})} | custom-call | bytes 3145728 | tf_op jit(solution)/shard_map/add_rows/pallas_call | solution.py:574
  (3 shorter events, 0.0 us)
Async XLA Ops:
  0.0 10.7 %copy-start.2 = (bf16[1,64,128,128]{3,2,1,0:T(8,128)(2,1)S(1)}, bf16[1,64,128,128]{3,2,1,0:T(8,128)(2,1)}, u32[]{:S(2)}) copy-start(bf16[1,64,128,128]{3,2,1,0:T(8,128)(2,1)} %param.13) | copy-start | bytes 6291460
  2.9 23.5 %collective-permute-start = (bf16[32,128,128]{2,1,0:T(8,128)(2,1)S(1)}, bf16[32,128,128]{2,1,0:T(8,128)(2,1)}, u32[]{:S(2)}, u32[]{:S(2)}) collective-permute-start(bf16[32,128,128]{2,1,0:T(8,128)(2,1)S(1)} %get-tuple-element.64), channel_id=1, source_target_pairs={{0,255},{1,254},{2,4},{3,5},{4,2},{5,3},{6,8},{7,9},{8,6},{9,7},{1... | collective-permute-start | bytes 3145736 | tf_op jit(solution)/shard_map/ppermute | solution.py:631
  10.6 61.5 %collective-permute-start.2 = (bf16[32,128,128]{2,1,0:T(8,128)(2,1)}, bf16[32,128,128]{2,1,0:T(8,128)(2,1)}, u32[]{:S(2)}, u32[]{:S(2)}) collective-permute-start(bf16[32,128,128]{2,1,0:T(8,128)(2,1)} %get-tuple-element.63), channel_id=1, source_target_pairs={{0,255},{1,254},{2,4},{3,5},{4,2},{5,3},{6,8},{7,9},{8,6},{9,7},{1... | collective-permute-start | bytes 3145736 | tf_op jit(solution)/shard_map/ppermute | solution.py:631
  10.7 20.5 %copy-start.5 = (bf16[128,128]{1,0:T(8,128)(2,1)S(1)}, bf16[128,128]{1,0:T(8,128)(2,1)}, u32[]{:S(2)}) copy-start(bf16[128,128]{1,0:T(8,128)(2,1)} %radiate_ref.5) | copy-start | bytes 98308
  10.7 21.2 %copy-start.10 = (s32[8,16]{1,0:T(8,128)S(1)}, s32[8,16]{1,0:T(8,128)}, u32[]{:S(2)}) copy-start(s32[8,16]{1,0:T(8,128)} %param.21) | copy-start | bytes 1540
  10.7 21.8 %copy-start.11 = (s32[8,16]{1,0:T(8,128)S(1)}, s32[8,16]{1,0:T(8,128)}, u32[]{:S(2)}) copy-start(s32[8,16]{1,0:T(8,128)} %param.22) | copy-start | bytes 1540
  10.7 22.4 %copy-start.9 = (s32[64,6]{0,1:T(8,128)S(1)}, s32[64,6]{0,1:T(8,128)}, u32[]{:S(2)}) copy-start(s32[64,6]{0,1:T(8,128)} %param.16) | copy-start | bytes 4612
  10.7 23.2 %copy-start.7 = (s32[128,32]{0,1:T(8,128)S(1)}, s32[128,32]{0,1:T(8,128)}, u32[]{:S(2)}) copy-start(s32[128,32]{0,1:T(8,128)} %param.24) | copy-start | bytes 49156
  10.7 23.2 %copy-start.8 = (s32[128,32]{0,1:T(8,128)S(1)}, s32[128,32]{0,1:T(8,128)}, u32[]{:S(2)}) copy-start(s32[128,32]{0,1:T(8,128)} %param.25) | copy-start | bytes 49156
  10.7 23.6 %copy-start.6 = (f32[316,16]{0,1:T(8,128)S(1)}, f32[316,16]{0,1:T(8,128)}, u32[]{:S(2)}) copy-start(f32[316,16]{0,1:T(8,128)} %param.23) | copy-start | bytes 60676
  10.7 77.7 %collective-permute-start.1 = (bf16[64,128,128]{2,1,0:T(8,128)(2,1)S(1)}, bf16[64,128,128]{2,1,0:T(8,128)(2,1)}, u32[]{:S(2)}, u32[]{:S(2)}) collective-permute-start(bf16[64,128,128]{2,1,0:T(8,128)(2,1)S(1)} %bitcast.26), channel_id=1, source_target_pairs={{0,2},{2,0},{4,6},{6,4},{8,10},{10,8},{12,14},{14,12},{16,18},{18,... | collective-permute-start | bytes 6291464 | tf_op jit(solution)/shard_map/ppermute | solution.py:634
  26.4 45.8 %collective-permute-start.3 = (bf16[32,128,128]{2,1,0:T(8,128)(2,1)}, bf16[32,128,128]{2,1,0:T(8,128)(2,1)S(1)}, u32[]{:S(2)}, u32[]{:S(2)}) collective-permute-start(bf16[32,128,128]{2,1,0:T(8,128)(2,1)} %collective-permute-done.a_ref.refs_6_), channel_id=1, source_target_pairs={{255,1},{254,0},{4,3},{5,2},{2,5},{3,4},{8,7},{9,6},{6,9},{7,8},{1... | collective-permute-start | bytes 3145736 | tf_op jit(solution)/shard_map/ppermute | solution.py:638
  72.2 27.9 %copy-start.3 = (bf16[32,128,128]{2,1,0:T(8,128)(2,1)}, bf16[32,128,128]{2,1,0:T(8,128)(2,1)S(1)}, u32[]{:S(2)}) copy-start(bf16[32,128,128]{2,1,0:T(8,128)(2,1)S(1)} %collective-permute-done.3.refs_0_.refs_2_) | copy-start | bytes 3145732
  72.2 30.3 %collective-permute-start.4 = (bf16[32,128,128]{2,1,0:T(8,128)(2,1)}, bf16[32,128,128]{2,1,0:T(8,128)(2,1)S(1)}, u32[]{:S(2)}, u32[]{:S(2)}) collective-permute-start(bf16[32,128,128]{2,1,0:T(8,128)(2,1)} %collective-permute-done.2.b_ref.refs_8_), channel_id=1, source_target_pairs={{255,1},{254,0},{4,3},{5,2},{2,5},{3,4},{8,7},{9,6},{6,9},{7,8},{1... | collective-permute-start | bytes 3145736 | tf_op jit(solution)/shard_map/ppermute | solution.py:644
  76.4 1.0 copy-start.1
  87.6 0.8 copy-start
  102.5 1.0 copy-start.4
  169.3 46.2 %collective-permute-start.5 = (bf16[32,64,128]{2,1,0:T(8,128)(2,1)}, bf16[32,64,128]{2,1,0:T(8,128)(2,1)S(1)}, u32[]{:S(2)}, u32[]{:S(2)}) collective-permute-start(bf16[32,64,128]{2,1,0:T(8,128)(2,1)} %get-tuple-element.58), channel_id=1, source_target_pairs={{0,1},{1,0},{2,3},{3,2},{4,5},{5,4},{6,7},{7,6},{8,9},{9,8},{10,11... | collective-permute-start | bytes 1572872 | tf_op jit(solution)/shard_map/ppermute | solution.py:653
  182.7 37.0 %collective-permute-start.6 = (bf16[32,64,128]{2,1,0:T(8,128)(2,1)}, bf16[32,64,128]{2,1,0:T(8,128)(2,1)S(1)}, u32[]{:S(2)}, u32[]{:S(2)}) collective-permute-start(bf16[32,64,128]{2,1,0:T(8,128)(2,1)} %get-tuple-element.62), channel_id=1, source_target_pairs={{0,1},{1,0},{2,3},{3,2},{4,5},{5,4},{6,7},{7,6},{8,9},{9,8},{10,11... | collective-permute-start | bytes 1572872 | tf_op jit(solution)/shard_map/ppermute | solution.py:656

commit v3 on v2

--- a/solution.py
+++ b/solution.py
@@ -58,8 +58,7 @@
 def exchange_kernel(chips, parts, x_ref, *refs):
     sources, refs = refs[:parts], refs[parts:]
     o_ref, refs = refs[0], refs[1:]
-    to_mate, refs = refs[:parts], refs[parts:]
-    to_neighbour, refs = refs[:parts], refs[parts:]
+    targets, refs = refs[: parts + 1 if parts else 0], refs[parts + 1 if parts else 0 :]
     held, send, recv, mate_send, mate_recv, local, part_send, part_recv = refs
     me, core, wraps = place()
     shift = lax.axis_index("shift")
@@ -74,9 +73,9 @@
             barrier, inc=1, device_id=(box, along), device_id_type=pl.DeviceIdType.MESH
         )
 
-    greet(mate, shift)
     if parts:
         greet(beside, beside_shift)
+    greet(mate, shift)
 
     @pl.loop(1, chips)
     def _(step):
@@ -94,6 +93,21 @@
         device_id_type=pl.DeviceIdType.MESH,
     )
     across.start()
+    moves = []
+    if parts:
+        ends = [(source, (mate, shift)) for source in sources]
+        ends.append((sources[-1], (beside, beside_shift)))
+        for i in reversed(range(parts + 1)):
+            move = pltpu.make_async_remote_copy(
+                ends[i][0],
+                targets[i],
+                part_send.at[i],
+                part_recv.at[i],
+                device_id=ends[i][1],
+                device_id_type=pl.DeviceIdType.MESH,
+            )
+            move.start()
+            moves.append(move)
     own.wait()
     across.wait()
 
@@ -109,21 +123,6 @@
             device_id_type=pl.DeviceIdType.MESH,
         ).start()
 
-    moves = []
-    for i in range(parts):
-        for j, (ref, device) in enumerate(
-            ((to_neighbour[i], (beside, beside_shift)), (to_mate[i], (mate, shift)))
-        ):
-            move = pltpu.make_async_remote_copy(
-                sources[i],
-                ref,
-                part_send.at[2 * i + j],
-                part_recv.at[2 * i + j],
-                device_id=device,
-                device_id_type=pl.DeviceIdType.MESH,
-            )
-            move.start()
-            moves.append(move)
     own = pltpu.make_async_copy(held.at[chip], o_ref.at[chip], local)
     own.start()
     own.wait()
@@ -137,16 +136,17 @@
 def exchange(blocks, *parts):
     count, samples, r = blocks.shape
     shape = (count // 2, 2, samples, r)
+    moved = [*parts, *parts[-1:]]
     n = len(parts)
     blocks, *moved = pl.pallas_call(
         functools.partial(exchange_kernel, count // 2, n),
         out_shape=[jax.ShapeDtypeStruct(shape, BF)]
-        + [jax.ShapeDtypeStruct(part.shape, BF) for part in parts] * 2,
+        + [jax.ShapeDtypeStruct(part.shape, BF) for part in moved],
         in_specs=[VMEM] + [ANY] * n,
-        out_specs=[VMEM] + [ANY] * (2 * n),
+        out_specs=[VMEM] + [ANY] * len(moved),
         scratch_shapes=[pltpu.VMEM(shape, BF)]
         + [pltpu.SemaphoreType.DMA] * 5
-        + [pltpu.SemaphoreType.DMA((max(2 * n, 1),))] * 2,
+        + [pltpu.SemaphoreType.DMA((max(len(moved), 1),))] * 2,
         compiler_params=pltpu.CompilerParams(
             has_side_effects=True, collective_id=1 if n else 0, vmem_limit_bytes=56 * MIB
         ),
@@ -250,7 +250,7 @@
 
     def where(i, core):
         towards = 4 * core[0]
-        return (jnp.where(i < 2, 4 - towards + i, towards + jnp.where(i == 2, 1 - core[0], core[0])), 0, 0)
+        return (jnp.where(i < 2, 4 - towards + i, towards + i - 2), 0, 0)
 
     whole = pl.BlockSpec((count // 2, u, r), lambda i, _: (0, 0, 0))
     return pl.pallas_call(
@@ -315,7 +315,7 @@
     )(source, offset, rounds, coarse, weights)
 
 
-def near_kernel(group, slots, part, index_ref, halves_ref, blocks_ref, *refs):
+def near_kernel(group, slots, start, index_ref, blocks_ref, *refs):
     sources, (own_ref, other_ref, held, sems) = refs[:-4], refs[-4:]
     step = pl.program_id(0)
     me, core, wraps = place()
@@ -326,18 +326,17 @@
     def _():
         towards = 2 * core * count
         within = 2 * count - towards
-        upper, lower = half * (1 - core), half * core
         places = (
             (0, count),
             (0, within),
-            (1, count + lower),
-            (1, count + upper),
-            (1, within + upper),
-            (1, within + lower),
-            (wraps, towards + upper),
-            (1 - wraps, towards + upper),
-            (wraps, towards + lower),
-            (1 - wraps, towards + lower),
+            (1, count),
+            (1, count + half),
+            (1, within),
+            (1, within + half),
+            (wraps, towards),
+            (wraps, towards + half),
+            (1 - wraps, towards),
+            (1 - wraps, towards + half),
         )
         copies = [
             pltpu.make_async_copy(src, held.at[kind, pl.ds(at, src.shape[0])], sems.at[i])
@@ -352,7 +351,7 @@
             copy.wait()
 
     base = me * count - count
-    origin = halves_ref[part] * half + step * group
+    origin = start + step * group
     for b in range(group):
         total = None
         for pair in range(slots // 2):
@@ -369,23 +368,22 @@
         other_ref[b] = total[:, r:].astype(BF)
 
 
-def near_field(part, halves, index, blocks, *sources):
+def near_field(start, stop, index, blocks, *sources):
     count, slots, rows, u = blocks.shape
     r = sources[0].shape[2]
     group = 8
-    steps = count // 2 // group
     out = pl.BlockSpec((group, rows, r), lambda i, *_: (i, 0, 0))
     return pl.pallas_call(
-        functools.partial(near_kernel, group, slots, part),
+        functools.partial(near_kernel, group, slots, start),
         out_shape=[
-            jax.ShapeDtypeStruct((count // 2, rows, r), F32),
-            jax.ShapeDtypeStruct((count // 2, rows, r), BF),
+            jax.ShapeDtypeStruct((stop - start, rows, r), F32),
+            jax.ShapeDtypeStruct((stop - start, rows, r), BF),
         ],
         grid_spec=pltpu.PrefetchScalarGridSpec(
-            num_scalar_prefetch=2,
-            grid=(steps,),
+            num_scalar_prefetch=1,
+            grid=((stop - start) // group,),
             in_specs=[
-                pl.BlockSpec((group, slots, rows, u), lambda i, _, h: (h[part] * steps + i, 0, 0, 0))
+                pl.BlockSpec((group, slots, rows, u), lambda i, _: (start // group + i, 0, 0, 0))
             ]
             + [ANY] * len(sources),
             out_specs=[out, out],
@@ -397,13 +395,14 @@
         compiler_params=pltpu.CompilerParams(vmem_limit_bytes=56 * MIB),
         cost_estimate=pl.CostEstimate(flops=3_000_000_000, bytes_accessed=20 * MIB, transcendentals=0),
         name="near_field",
-    )(index, halves, blocks, *sources)
-
-
-def local_step(
-    width, step, source_ref, offset_ref, last_a, last_b, mine, beside, radiate_ref, one_ref, two_ref,
-    table_ref, incoming_ref, held, patterns, flat, weights, across, local, sems,
+    )(index, blocks, *sources)
+
+
+def local_kernel(
+    width, source_ref, offset_ref, last_a, last_b, mine, beside, radiate_ref, one_ref, two_ref,
+    table_ref, incoming_ref, local_ref, held, patterns, flat, weights, across, sems,
 ):
+    step = pl.program_id(0)
     me, core, wraps = place()
     count, u, r = held.shape
     parents = count // 8
@@ -432,8 +431,8 @@
         @pl.when(wraps == 1)
         def _():
             halves = [
-                pltpu.make_async_copy(last_a, held.at[pl.ds(half * (1 - core), half)], sems.at[2]),
-                pltpu.make_async_copy(last_b, held.at[pl.ds(half * core, half)], sems.at[3]),
+                pltpu.make_async_copy(last_a, held.at[pl.ds(0, half)], sems.at[2]),
+                pltpu.make_async_copy(last_b, held.at[pl.ds(half, half)], sems.at[3]),
             ]
             for copy in halves:
                 copy.start()
@@ -467,116 +466,101 @@
             total = term if total is None else total + term
         across[rows, :] = total
 
-    local[pl.ds(pl.multiple_of(step * r, r), r), :] = (
-        across[...] + dot(flat[...], two_ref[0])
-    ).astype(BF)
-
-
-def downward_kernel(
-    width, source_ref, offset_ref, x_ref, last_a, last_b, mine, beside, a_ref, b_ref, sigma_ref,
-    radiate_ref, turned_ref, one_ref, two_ref, table_ref, incoming_ref, base_ref,
-    held, patterns, flat, weights, across, local, sems,
-):
-    step = pl.program_id(0)
-    parents, _, u, r = x_ref.shape
-    rows = u // 2
-
-    @pl.when(step < parents)
-    def _():
-        local_step(
-            width, step, source_ref, offset_ref, last_a, last_b, mine, beside, radiate_ref, one_ref,
-            two_ref, table_ref, incoming_ref, held, patterns, flat, weights, across, local, sems,
-        )
-
-    @pl.when(step >= parents)
-    def _():
-        core = lax.rem(lax.axis_index("box"), 2)
-        own = pl.ds(pl.multiple_of(lax.axis_index("shift") * rows, rows), rows)
-        sig_re, sig_im = sigma_ref[0], sigma_ref[1]
-        leaf_in = dot(local[...], one_ref[step - parents]).astype(BF)
-        far = dot_nt(turned_ref[...], leaf_in)
-        for c in range(parents):
-            part = far[:, c * r : (c + 1) * r]
-            field = x_ref[c, 0].astype(F32)
-            real, imag = field[:rows], field[rows:]
-            base_ref[c, 0, :rows] = part[:rows] - (sig_re * real - sig_im * imag)
-            base_ref[c, 0, rows:] = part[rows:] - (sig_re * imag + sig_im * real)
-            at = c % (parents // 2)
-            in_a = core == (1 if c < parents // 2 else 0)
-            base_ref[c, 0, own] += jnp.where(in_a, a_ref[at, 0], b_ref[at, 0])
-
-
-def downward(
-    source, offset, x, last_a, last_b, mine, beside, own_a, own_b, sigma, radiate, turned, one, two,
-    table, incoming,
-):
+    local_ref[...] = (across[...] + dot(flat[...], two_ref[0])).astype(BF)
+
+
+def local_field(source, offset, last_a, last_b, mine, beside, radiate, one, two, table, incoming):
     octants, k2, k1 = two.shape
-    count, u, r = x.shape
-    parents = count // 8
-    width = source.shape[0] // parents
-
-    def child(i, *_):
-        return (0, jnp.maximum(i - parents, 0), 0, 0)
-
-    near = pl.BlockSpec((parents // 2, 1, u // 2, r), child)
-    box = pl.BlockSpec((parents, 1, u, r), child)
+    _, u, r = last_a.shape
+    width = source.shape[0] // octants
     return pl.pallas_call(
-        functools.partial(downward_kernel, width),
-        out_shape=jax.ShapeDtypeStruct((parents, 8, u, r), F32),
+        functools.partial(local_kernel, width),
+        out_shape=jax.ShapeDtypeStruct((octants * r, k1), BF),
         grid_spec=pltpu.PrefetchScalarGridSpec(
             num_scalar_prefetch=2,
-            grid=(parents + 8,),
-            in_specs=[
-                box,
-                ANY,
-                ANY,
-                ANY,
-                ANY,
-                near,
-                near,
-                pl.BlockSpec(memory_space=pltpu.SMEM),
-                VMEM,
-                VMEM,
-                VMEM,
-                pl.BlockSpec((1, k2, k1), lambda i, *_: (jnp.minimum(i, parents - 1), 0, 0)),
-                VMEM,
-                VMEM,
-            ],
-            out_specs=box,
+            grid=(octants,),
+            in_specs=[ANY] * 4
+            + [VMEM, VMEM, pl.BlockSpec((1, k2, k1), lambda i, *_: (i, 0, 0)), VMEM, VMEM],
+            out_specs=pl.BlockSpec((r, k1), lambda i, *_: (i, 0)),
             scratch_shapes=[
-                pltpu.VMEM((count, u, r), BF),
-                pltpu.VMEM((3 * parents, r, k1), BF),
+                pltpu.VMEM((octants * 8, u, r), BF),
+                pltpu.VMEM((3 * octants, r, k1), BF),
                 pltpu.VMEM((r, k2), BF),
                 pltpu.VMEM((width, k1), F32),
                 pltpu.VMEM((r, k1), F32),
-                pltpu.VMEM((parents * r, k1), BF),
                 pltpu.SemaphoreType.DMA((4,)),
             ],
         ),
         compiler_params=pltpu.CompilerParams(vmem_limit_bytes=56 * MIB),
-        cost_estimate=pl.CostEstimate(flops=9_000_000_000, bytes_accessed=80 * MIB, transcendentals=0),
-        name="downward",
-    )(
-        source, offset, x.reshape(parents, 8, u, r), last_a, last_b, mine, beside,
-        own_a.reshape(parents // 2, 8, u // 2, r), own_b.reshape(parents // 2, 8, u // 2, r),
-        sigma.reshape(-1), radiate, turned, one, two, table, incoming,
-    ).reshape(count, u, r)
+        cost_estimate=pl.CostEstimate(flops=5_000_000_000, bytes_accessed=50 * MIB, transcendentals=0),
+        name="local_field",
+    )(source, offset, last_a, last_b, mine, beside, radiate, one, two, table, incoming)
+
+
+def leaves_kernel(
+    early, x_ref, a_ref, b_ref, sigma_ref, turned_ref, one_ref, local_ref, base_ref
+):
+    parents, _, u, r = x_ref.shape
+    rows = u // 2
+    shift = lax.axis_index("shift")
+    own = pl.ds(pl.multiple_of(shift * rows, rows), rows)
+    sig_re, sig_im = sigma_ref[0], sigma_ref[1]
+    leaf_in = dot(local_ref[...], one_ref[0]).astype(BF)
+    far = dot_nt(turned_ref[...], leaf_in)
+    for c in range(parents):
+        part = far[:, c * r : (c + 1) * r]
+        field = x_ref[c, 0].astype(F32)
+        real, imag = field[:rows], field[rows:]
+        base_ref[c, 0, :rows] = part[:rows] - (sig_re * real - sig_im * imag)
+        base_ref[c, 0, rows:] = part[rows:] - (sig_re * imag + sig_im * real)
+        base_ref[c, 0, own] += a_ref[c, 0] if c < early else b_ref[c - early, 0]
+
+
+def leaf_fields(x, own_a, own_b, sigma, turned, one, local):
+    count, u, r = x.shape
+    octants, k1, k0 = one.shape
+    parents = count // octants
+    early = own_a.shape[0] // octants
+
+    def apart(array):
+        return array.reshape(array.shape[0] // octants, octants, *array.shape[1:])
+
+    def spec(array):
+        return pl.BlockSpec((array.shape[0], 1, *array.shape[2:]), lambda i: (0, i, 0, 0))
+
+    parts = [apart(array) for array in (x, own_a, own_b)]
+    return pl.pallas_call(
+        functools.partial(leaves_kernel, early),
+        grid=(octants,),
+        out_shape=jax.ShapeDtypeStruct((parents, octants, u, r), F32),
+        in_specs=[spec(part) for part in parts]
+        + [
+            pl.BlockSpec(memory_space=pltpu.SMEM),
+            VMEM,
+            pl.BlockSpec((1, k1, k0), lambda i: (i, 0, 0)),
+            VMEM,
+        ],
+        out_specs=spec(parts[0]),
+        compiler_params=pltpu.CompilerParams(vmem_limit_bytes=56 * MIB),
+        cost_estimate=pl.CostEstimate(flops=2_000_000_000, bytes_accessed=20 * MIB, transcendentals=0),
+        name="leaf_fields",
+    )(*parts, sigma.reshape(-1), turned, one, local).reshape(count, u, r)
 
 
 def add_kernel(_, base_ref, back_ref, out_ref):
     out_ref[...] = base_ref[...] + back_ref[...].astype(F32)
 
 
-def add_rows(where, base, back):
+def add_rows(half_at, start, base, back):
     count, u, r = base.shape
-    group = count // 4
-    rows = pl.BlockSpec((group, u // 2, r), lambda i, at: (at[0] * 2 + i, at[1], 0))
+    group = 16
+    rows = pl.BlockSpec((group, u // 2, r), lambda i, at: (start // group + i, at[0], 0))
     return pl.pallas_call(
         add_kernel,
         out_shape=jax.ShapeDtypeStruct((count, u, r), F32),
         grid_spec=pltpu.PrefetchScalarGridSpec(
             num_scalar_prefetch=1,
-            grid=(2,),
+            grid=(back.shape[0] // group,),
             in_specs=[rows, pl.BlockSpec((group, u // 2, r), lambda i, at: (i, 0, 0))],
             out_specs=rows,
         ),
@@ -584,7 +568,7 @@
         compiler_params=pltpu.CompilerParams(vmem_limit_bytes=16 * MIB),
         cost_estimate=pl.CostEstimate(flops=0, bytes_accessed=3 * MIB, transcendentals=0),
         name="add_rows",
-    )(where, base, back)
+    )(half_at, base, back)
 
 
 def after(arrays, *others):
@@ -615,21 +599,17 @@
     partners = [(0, 1), (1, 0)]
     core = lax.rem(lax.axis_index("box"), 2).astype(jnp.int32)
     shift = lax.axis_index("shift").astype(jnp.int32)
-    halves = jnp.stack([1 - core, core])
     lists = (
         near_index.reshape(-1),
         level1_source.reshape(-1),
         level1_offset.reshape(-1),
         radiate.T,
-        halves,
-        jnp.stack([1 - core, 1 - shift]),
-        jnp.stack([core, 1 - shift]),
+        (1 - shift).reshape(1),
         *translation_lists(trans_two, level2_source, level2_offset, x.shape[2]),
     )
 
     first_a, first_b = [
-        lax.ppermute(lax.dynamic_slice_in_dim(x, at * (count // 2), count // 2), BOTH, hops[0])
-        for at in (core, 1 - core)
+        lax.ppermute(half, BOTH, hops[0]) for half in (x[: count // 2], x[count // 2 :])
     ]
     mate = lax.ppermute(x, "box", swap)
     coarse, mine = upward(x, radiate, interp_one, interp_two)
@@ -637,29 +617,35 @@
     (first_a,) = after([first_a], coarse)
     partner_a = lax.ppermute(first_a, BOTH, hops[1])
     coarse, *lists = after([coarse, *lists], first_a)
-    index, source, offset, turned_radiate, halves, where_a, where_b, *translation = lists
+    index, source, offset, turned_radiate, half_at, *translation = lists
     (gathered,) = exchange(coarse.reshape(boxes, k2 // boxes, -1))
 
     first_b, partner_a = after([first_b, partner_a], gathered)
     partner_b = lax.ppermute(first_b, BOTH, hops[1])
+    last_a = lax.ppermute(partner_a, BOTH, hops[2])
     turned = translate(gathered, *translation)
     beside = patterns_beside(core.reshape(1), mate, first_a, first_b, radiate, interp_one)
-    (turned,) = after([turned], beside)
-    incoming, partner_mate_a, partner_mate_b, last_a, last_b = exchange(turned, partner_a, partner_b)
+    (turned,) = after([turned], beside, last_a)
+    incoming, partner_mate_a, partner_mate_b, last_b = exchange(turned, partner_a, partner_b)
     incoming = incoming.reshape(k2, -1)
+
     (index,) = after([index], incoming)
-    here = (x, mate, partner_a, partner_b, partner_mate_a, partner_mate_b, first_a, last_a)
-    own_a, other_a = near_field(0, halves, index, near_blocks, *here)
+    here = (
+        x, mate, partner_a, partner_b, partner_mate_a, partner_mate_b, first_a, first_b, last_a, last_b
+    )
+    early = count // 2
+    own_a, other_a = near_field(0, early, index, near_blocks, *here)
     back_a = lax.ppermute(other_a, "shift", partners)
     (index,) = after([index], other_a)
-    own_b, other_b = near_field(1, halves, index, near_blocks, *here, first_b, last_b)
+    own_b, other_b = near_field(early, count, index, near_blocks, *here)
     back_b = lax.ppermute(other_b, "shift", partners)
-    base = downward(
-        source, offset, x, last_a, last_b, mine, beside, own_a, own_b, sigma, radiate, turned_radiate,
-        interp_one, interp_two, trans_one, incoming,
+    source, offset = after([source, offset], other_b)
+    local = local_field(
+        source, offset, last_a, last_b, mine, beside, radiate, interp_one, interp_two, trans_one, incoming
     )
-    base = add_rows(where_a, base, back_a)
-    return add_rows(where_b, base, back_b)[None]
+    base = leaf_fields(x, own_a, own_b, sigma, turned_radiate, interp_one, local)
+    base = add_rows(half_at, 0, base, back_a)
+    return add_rows(half_at, early, base, back_b)[None]
 
 
 def solution(mesh):

time: 225 us -> 229 us (1.018)
  waiting for transfers between devices: 3.95 us -> 26.1 us
  Pallas kernels: 185 us -> 166 us
  starting transfers between devices: 23.1 us -> 27.2 us
    pallas_call x2, Pallas kernels: 91.9 us -> 71.7 us  [exchange(): pl.pallas_call(functools.partial(exchange_kernel, count // 2, n), out_sha...]
    ppermute x1, waiting for transfers between devices: 2.39 us -> 20.7 us  [body(): partner_b = lax.ppermute(first_b, BOTH, hops[1])]
    ppermute x2 -> x3, starting transfers between devices: 7.75 us -> 13.6 us  [the longest x2 7.75 us: body(): lax.ppermute(half, BOTH, hops[0])]
    ppermute x2 -> x3, waiting for transfers between devices: 0.01 us -> 5.38 us  [the longest x1 5.37 us: body(): last_a = lax.ppermute(partner_a, BOTH, hops[2])]
    dynamic_slice x1 -> x0, local copies, waits for them, and re-layouts: 2.91 us -> none  [body(): lax.dynamic_slice_in_dim(x, at * (count // 2), count // 2)]
    slice x0 -> x1, local copies, waits for them, and re-layouts: none -> 2.76 us  [body(): x[count // 2:]]
    pallas_call x3 -> x4, Pallas kernels: 50 us -> 52.1 us  [the longest x2 21.5 us: near_field(): pl.pallas_call(functools.partial(near_kernel, group, slots, start), out_s...]
  transfers between devices with their start and end apart: 7 -> 8, of which waited for: 2 -> 2; matrix products, arithmetic and copies ran while one was open for 2% -> 2% of each run, Pallas kernels for 52% -> 52%
where the time goes in v3:
time: 229 us; the launch traced here: 228 us
  Pallas kernels  166 us (72%)
  starting transfers between devices  27.2 us (12%)
  waiting for transfers between devices  26.1 us (11%)
  local copies, waits for them, and re-layouts  8.57 us (4%)
    pallas_call x2, Pallas kernels, exchange(): pl.pallas_call(functools.partial(exchange_kernel, count // 2, n), out_sha...  71.7 us
    pallas_call x2, Pallas kernels, near_field(): pl.pallas_call(functools.partial(near_kernel, group, slots, start), out_s...  21.5 us
    pallas_call x1, Pallas kernels, local_field(): pl.pallas_call(functools.partial(local_kernel, width), out_shape=jax.Shap...  20.8 us
    ppermute x1, waiting for transfers between devices, body(): partner_b = lax.ppermute(first_b, BOTH, hops[1])  20.7 us
    pallas_call x1, Pallas kernels, upward(): pl.pallas_call(upward_kernel, grid=(octants // 2,), out_shape=[jax.ShapeD...  15.6 us
    pallas_call x1, Pallas kernels, patterns_beside(): pl.pallas_call(beside_kernel, out_shape=jax.ShapeDtypeStruct((3 * count /...  11.7 us
    pallas_call x1, Pallas kernels, translate(): pl.pallas_call(functools.partial(translate_kernel, source.shape[0] // coa...  10.5 us
    pallas_call x1, Pallas kernels, leaf_fields(): pl.pallas_call(functools.partial(leaves_kernel, early), grid=(octants,),...  9.87 us
  transfers between devices with their start and end apart: 8, of which 2 were waited for; matrix products, arithmetic and copies ran while one was open for 2% of the time, Pallas kernels for 52%

profile of v3, /device:TPU:2, one launch (start us, length us, event | category | flops | bytes accessed | tf_op | source)
XLA Modules:
  0.0 227.8 jit_solution(7486511945579999334)
XLA Ops:
  0.0 2.8 %slice_bitcast_fusion = (bf16[32,128,128]{2,1,0:T(8,128)(2,1)}, bf16[32,128,128]{2,1,0:T(8,128)(2,1)S(1)}) fusion(bf16[1,64,128,128]{3,2,1,0:T(8,128)(2,1)} %param.13), kind=kLoop, calls=%fused_computation | loop fusion | bytes 4194304 | tf_op jit(solution)/shard_map/slice | solution.py:612
  2.8 7.7 %collective-permute-start = (bf16[32,128,128]{2,1,0:T(8,128)(2,1)S(1)}, bf16[32,128,128]{2,1,0:T(8,128)(2,1)}, u32[]{:S(2)}, u32[]{:S(2)}) collective-permute-start(bf16[32,128,128]{2,1,0:T(8,128)(2,1)S(1)} %get-tuple-element.62), channel_id=1, source_target_pairs={{0,255},{1,254},{2,4},{3,5},{4,2},{5,3},{6,8},{7,9},{8,6},{9,7},{1... | collective-permute-start | bytes 3145736 | tf_op jit(solution)/shard_map/ppermute | solution.py:612
  10.5 0.0 collective-permute-start.2
  10.5 0.0 copy-start.2
  10.5 0.0 copy-start.7
  10.5 0.0 copy-start.8
  10.5 0.0 copy-start.6
  10.5 0.0 copy-start.4
  10.5 0.0 copy-start.5
  10.5 0.0 copy-start.3
  10.6 0.1 collective-permute-start.1
  10.7 15.6 %upward.1 = (bf16[2048,128]{1,0:T(8,128)(2,1)}, bf16[8,128,512]{2,1,0:T(8,128)(2,1)}) custom-call(bf16[64,128,128]{2,1,0:T(8,128)(2,1)} %bitcast.x_ref.refs_0_, bf16[128,128]{1,0:T(8,128)(2,1)} %radiate_ref.5, bf16[8,512,128]{2,1,0:T(8,128)(2,1)} %one_ref.7, bf16[8,2048,512]{2,1,0:T(8,128)(2,1)} %two_ref.3), custom_call_target="tpu_custom_call" | custom-call | flops 7000000000 | bytes 52428800 | tf_op jit(solution)/shard_map/upward/pallas_call | solution.py:205
  26.2 0.0 collective-permute-done.a_ref.refs_6_
  26.2 4.8 %collective-permute-start.3 = (bf16[32,128,128]{2,1,0:T(8,128)(2,1)}, bf16[32,128,128]{2,1,0:T(8,128)(2,1)}, u32[]{:S(2)}, u32[]{:S(2)}) collective-permute-start(bf16[32,128,128]{2,1,0:T(8,128)(2,1)} %collective-permute-done.a_ref.refs_6_), channel_id=1, source_target_pairs={{255,1},{254,0},{4,3},{5,2},{2,5},{3,4},{8,7},{9,6},{6,9},{7,8},{1... | collective-permute-start | bytes 3145736 | tf_op jit(solution)/shard_map/ppermute | solution.py:618
  31.0 0.0 copy-done.2
  31.0 0.7 copy.19
  31.7 0.0 copy-done.7
  31.7 0.6 reshape.43.source_ref
  32.3 0.0 copy-done.8
  32.3 0.6 reshape.44.offset_ref
  32.9 0.0 copy-done.6
  32.9 0.1 copy.18
  33.0 0.7 reshape.42.index_ref
  33.7 0.0 copy-done.4
  33.7 0.0 copy-done.5
  33.7 0.1 copy.20
  33.8 0.1 reshape.46.source_ref
  33.9 0.1 copy.21
  34.0 0.1 reshape.47.offset_ref
  34.1 0.0 copy-done.3
  34.1 0.1 copy.23
  34.2 0.7 broadcast_in_dim.15.weight_ref
  35.0 37.0 %exchange.2 = bf16[64,2,16,128]{3,2,1,0:T(8,128)(2,1)} custom-call(bf16[64,2,16,128]{3,2,1,0:T(8,128)(2,1)} %bitcast.24), custom_call_target="tpu_custom_call" | custom-call | bytes 83886080 | tf_op jit(solution)/shard_map/exchange/pallas_call | solution.py:141
  72.0 0.0 collective-permute-done.2.b_ref.refs_7_
  72.0 0.0 collective-permute-done.3.refs_0_.refs_2_
  72.0 5.8 %collective-permute-start.4 = (bf16[32,128,128]{2,1,0:T(8,128)(2,1)}, bf16[32,128,128]{2,1,0:T(8,128)(2,1)}, u32[]{:S(2)}, u32[]{:S(2)}) collective-permute-start(bf16[32,128,128]{2,1,0:T(8,128)(2,1)} %collective-permute-done.3.refs_0_.refs_2_), channel_id=1, source_target_pairs={{1,254},{0,255},{3,5},{2,4},{5,3},{4,2},{7,9},{6,8},{9,7},{8,6},{1... | collective-permute-start | bytes 3145736 | tf_op jit(solution)/shard_map/ppermute | solution.py:625
  77.9 2.5 %collective-permute-start.5 = (bf16[32,128,128]{2,1,0:T(8,128)(2,1)}, bf16[32,128,128]{2,1,0:T(8,128)(2,1)}, u32[]{:S(2)}, u32[]{:S(2)}) collective-permute-start(bf16[32,128,128]{2,1,0:T(8,128)(2,1)} %collective-permute-done.2.b_ref.refs_7_), channel_id=1, source_target_pairs={{255,1},{254,0},{4,3},{5,2},{2,5},{3,4},{8,7},{9,6},{6,9},{7,8},{1... | collective-permute-start | bytes 3145736 | tf_op jit(solution)/shard_map/ppermute | solution.py:624
  80.4 0.0 copy-start.1
  80.4 1.0 copy-done.1
  81.4 10.5 %translate.1 = bf16[128,16,128]{2,1,0:T(8,128)(2,1)S(1)} custom-call(s32[4096]{0:T(1024)S(1)} %reshape.46.source_ref, s32[4096]{0:T(1024)S(1)} %reshape.47.offset_ref, s32[128]{0:T(128)S(1)} %and_select_fusion.rounds_ref, bf16[128,16,128]{2,1,0:T(8,128)(2,1)S(1)} %bitcast.19, f32[317,16,128]{2,1,0:T(8,128)S(1)} %broadcast_in_dim.15.weight_ref), custom_call_target="tpu_custom_call" | custom-call | flops 2000000000 | bytes 26214400 | tf_op jit(solution)/shard_map/translate/pallas_call | solution.py:306
  92.0 0.0 copy-start
  92.0 0.8 copy-done
  92.8 0.0 collective-permute-done.1.mate_ref.refs_1_
  92.8 11.7 %patterns_beside.1.beside = bf16[24,128,512]{2,1,0:T(8,128)(2,1)} custom-call(s32[1]{0:T(128)} %bitcast.7._, bf16[64,128,128]{2,1,0:T(8,128)(2,1)} %collective-permute-done.1.mate_ref.refs_1_, bf16[32,128,128]{2,1,0:T(8,128)(2,1)} %collective-permute-done.a_ref.refs_6_, bf16[32,128,128]{2,1,0:T(8,128)(2,1)} %collective-permute-done.2.b_ref.refs_7_, ...), custom_call_target="tpu_custom_call" | custom-call | flops 4000000000 | bytes 31457280 | tf_op jit(solution)/shard_map/patterns_beside/pallas_call | solution.py:256
  104.5 5.4 %collective-permute-done.4.refs_8_.last_a = bf16[32,128,128]{2,1,0:T(8,128)(2,1)} collective-permute-done((bf16[32,128,128]{2,1,0:T(8,128)(2,1)}, bf16[32,128,128]{2,1,0:T(8,128)(2,1)}, u32[]{:S(2)}, u32[]{:S(2)}) %collective-permute-start.4) | collective-permute-done | bytes 1048608 | tf_op jit(solution)/shard_map/ppermute | solution.py:625
  109.9 20.7 %collective-permute-done.5.refs_1_.refs_3_ = bf16[32,128,128]{2,1,0:T(8,128)(2,1)} collective-permute-done((bf16[32,128,128]{2,1,0:T(8,128)(2,1)}, bf16[32,128,128]{2,1,0:T(8,128)(2,1)}, u32[]{:S(2)}, u32[]{:S(2)}) %collective-permute-start.5) | collective-permute-done | bytes 1048608 | tf_op jit(solution)/shard_map/ppermute | solution.py:624
  130.6 34.6 %exchange.3 = (bf16[64,2,16,128]{3,2,1,0:T(8,128)(2,1)}, bf16[32,128,128]{2,1,0:T(8,128)(2,1)}, bf16[32,128,128]{2,1,0:T(8,128)(2,1)}, bf16[32,128,128]{2,1,0:T(8,128)(2,1)}) custom-call(bf16[64,2,16,128]{3,2,1,0:T(8,128)(2,1)} %bitcast.18, bf16[32,128,128]{2,1,0:T(8,128)(2,1)} %collective-permute-done.3.refs_0_.refs_2_, ...), custom_call_target="tpu_custom_call" | custom-call | bytes 83886080 | tf_op jit(solution)/shard_map/exchange/pallas_call | solution.py:141
  165.2 10.8 %near_field.2 = (f32[32,64,128]{2,1,0:T(8,128)}, bf16[32,64,128]{2,1,0:T(8,128)(2,1)}) custom-call(s32[384]{0:T(512)} %reshape.42.index_ref, bf16[64,6,64,128]{3,2,1,0:T(8,128)(2,1)} %blocks_ref.3, bf16[64,128,128]{2,1,0:T(8,128)(2,1)} %bitcast.x_ref.refs_0_, bf16[64,128,128]{2,1,0:T(8,128)(2,1)} %collective-permute-done.1.mate_ref.refs_1_, ...), custom_call_target="tpu_custom_call" | custom-call | flops 3000000000 | bytes 20971520 | tf_op jit(solution)/shard_map/near_field/pallas_call | solution.py:376
  176.0 2.0 collective-permute-start.6
  177.9 10.7 %near_field.3 = (f32[32,64,128]{2,1,0:T(8,128)}, bf16[32,64,128]{2,1,0:T(8,128)(2,1)}) custom-call(s32[384]{0:T(512)} %reshape.42.index_ref, bf16[64,6,64,128]{3,2,1,0:T(8,128)(2,1)} %blocks_ref.3, bf16[64,128,128]{2,1,0:T(8,128)(2,1)} %bitcast.x_ref.refs_0_, bf16[64,128,128]{2,1,0:T(8,128)(2,1)} %collective-permute-done.1.mate_ref.refs_1_, ...), custom_call_target="tpu_custom_call" | custom-call | flops 3000000000 | bytes 20971520 | tf_op jit(solution)/shard_map/near_field/pallas_call | solution.py:376
  188.7 4.3 %collective-permute-start.7 = (bf16[32,64,128]{2,1,0:T(8,128)(2,1)}, bf16[32,64,128]{2,1,0:T(8,128)(2,1)S(1)}, u32[]{:S(2)}, u32[]{:S(2)}) collective-permute-start(bf16[32,64,128]{2,1,0:T(8,128)(2,1)} %get-tuple-element.57), channel_id=1, source_target_pairs={{0,1},{1,0},{2,3},{3,2},{4,5},{5,4},{6,7},{7,6},{8,9},{9,8},{10,11... | collective-permute-start | bytes 1572872 | tf_op jit(solution)/shard_map/ppermute | solution.py:641
  193.0 20.8 %local_field.1.local_ref = bf16[1024,512]{1,0:T(8,128)(2,1)} custom-call(s32[128]{0:T(128)} %reshape.43.source_ref, s32[128]{0:T(128)} %reshape.44.offset_ref, bf16[32,128,128]{2,1,0:T(8,128)(2,1)} %collective-permute-done.4.refs_8_.last_a, bf16[32,128,128]{2,1,0:T(8,128)(2,1)} %get-tuple-element.49.refs_9_.last_b, ...), custom_call_target="tpu_custom_call" | custom-call | flops 5000000000 | bytes 52428800 | tf_op jit(solution)/shard_map/local_field/pallas_call | solution.py:476
  213.8 9.9 %leaf_fields.1 = f32[8,8,128,128]{3,2,1,0:T(8,128)} custom-call(bf16[8,8,128,128]{3,2,1,0:T(8,128)(2,1)} %bitcast.4.x_ref, f32[4,8,64,128]{3,2,1,0:T(8,128)} %bitcast.21, f32[4,8,64,128]{3,2,1,0:T(8,128)} %bitcast.22, f32[2]{0:T(128)} %bitcast.26, bf16[128,128]{1,0:T(8,128)(2,1)} %bitcast.25, bf16[8,512,128]{2,1,0:T(8,128)(2,1)} %one_ref.7, ...), custom_call_target="tpu_custom_call" | custom-call | flops 2000000000 | bytes 20971520 | tf_op jit(solution)/shard_map/leaf_fields/pallas_call | solution.py:532
  223.7 0.0 collective-permute-done.6.back_ref
  223.7 2.1 add_rows.2.base_ref
  225.7 0.0 collective-permute-done.7.back_ref
  225.7 2.1 add_rows.3
  (3 shorter events, 0.0 us)
Async XLA Ops:
  2.8 23.5 %collective-permute-start = (bf16[32,128,128]{2,1,0:T(8,128)(2,1)S(1)}, bf16[32,128,128]{2,1,0:T(8,128)(2,1)}, u32[]{:S(2)}, u32[]{:S(2)}) collective-permute-start(bf16[32,128,128]{2,1,0:T(8,128)(2,1)S(1)} %get-tuple-element.62), channel_id=1, source_target_pairs={{0,255},{1,254},{2,4},{3,5},{4,2},{5,3},{6,8},{7,9},{8,6},{9,7},{1... | collective-permute-start | bytes 3145736 | tf_op jit(solution)/shard_map/ppermute | solution.py:612
  10.5 61.5 %collective-permute-start.2 = (bf16[32,128,128]{2,1,0:T(8,128)(2,1)}, bf16[32,128,128]{2,1,0:T(8,128)(2,1)}, u32[]{:S(2)}, u32[]{:S(2)}) collective-permute-start(bf16[32,128,128]{2,1,0:T(8,128)(2,1)} %get-tuple-element.61), channel_id=1, source_target_pairs={{0,255},{1,254},{2,4},{3,5},{4,2},{5,3},{6,8},{7,9},{8,6},{9,7},{1... | collective-permute-start | bytes 3145736 | tf_op jit(solution)/shard_map/ppermute | solution.py:612
  10.5 20.5 %copy-start.2 = (bf16[128,128]{1,0:T(8,128)(2,1)S(1)}, bf16[128,128]{1,0:T(8,128)(2,1)}, u32[]{:S(2)}) copy-start(bf16[128,128]{1,0:T(8,128)(2,1)} %radiate_ref.5) | copy-start | bytes 98308
  10.5 21.2 %copy-start.7 = (s32[8,16]{1,0:T(8,128)S(1)}, s32[8,16]{1,0:T(8,128)}, u32[]{:S(2)}) copy-start(s32[8,16]{1,0:T(8,128)} %param.21) | copy-start | bytes 1540
  10.5 21.8 %copy-start.8 = (s32[8,16]{1,0:T(8,128)S(1)}, s32[8,16]{1,0:T(8,128)}, u32[]{:S(2)}) copy-start(s32[8,16]{1,0:T(8,128)} %param.22) | copy-start | bytes 1540
  10.5 22.4 %copy-start.6 = (s32[64,6]{0,1:T(8,128)S(1)}, s32[64,6]{0,1:T(8,128)}, u32[]{:S(2)}) copy-start(s32[64,6]{0,1:T(8,128)} %param.16) | copy-start | bytes 4612
  10.5 23.2 %copy-start.4 = (s32[128,32]{0,1:T(8,128)S(1)}, s32[128,32]{0,1:T(8,128)}, u32[]{:S(2)}) copy-start(s32[128,32]{0,1:T(8,128)} %param.24) | copy-start | bytes 49156
  10.5 23.2 %copy-start.5 = (s32[128,32]{0,1:T(8,128)S(1)}, s32[128,32]{0,1:T(8,128)}, u32[]{:S(2)}) copy-start(s32[128,32]{0,1:T(8,128)} %param.25) | copy-start | bytes 49156
  10.5 23.5 %copy-start.3 = (f32[316,16]{0,1:T(8,128)S(1)}, f32[316,16]{0,1:T(8,128)}, u32[]{:S(2)}) copy-start(f32[316,16]{0,1:T(8,128)} %param.23) | copy-start | bytes 60676
  10.6 82.3 %collective-permute-start.1 = (bf16[64,128,128]{2,1,0:T(8,128)(2,1)}, bf16[64,128,128]{2,1,0:T(8,128)(2,1)}, u32[]{:S(2)}, u32[]{:S(2)}) collective-permute-start(bf16[64,128,128]{2,1,0:T(8,128)(2,1)} %bitcast.x_ref.refs_0_), channel_id=1, source_target_pairs={{0,2},{2,0},{4,6},{6,4},{8,10},{10,8},{12,14},{14,12},{16,18},{18,... | collective-permute-start | bytes 6291464 | tf_op jit(solution)/shard_map/ppermute | solution.py:614
  26.2 45.8 %collective-permute-start.3 = (bf16[32,128,128]{2,1,0:T(8,128)(2,1)}, bf16[32,128,128]{2,1,0:T(8,128)(2,1)}, u32[]{:S(2)}, u32[]{:S(2)}) collective-permute-start(bf16[32,128,128]{2,1,0:T(8,128)(2,1)} %collective-permute-done.a_ref.refs_6_), channel_id=1, source_target_pairs={{255,1},{254,0},{4,3},{5,2},{2,5},{3,4},{8,7},{9,6},{6,9},{7,8},{1... | collective-permute-start | bytes 3145736 | tf_op jit(solution)/shard_map/ppermute | solution.py:618
  72.0 37.9 %collective-permute-start.4 = (bf16[32,128,128]{2,1,0:T(8,128)(2,1)}, bf16[32,128,128]{2,1,0:T(8,128)(2,1)}, u32[]{:S(2)}, u32[]{:S(2)}) collective-permute-start(bf16[32,128,128]{2,1,0:T(8,128)(2,1)} %collective-permute-done.3.refs_0_.refs_2_), channel_id=1, source_target_pairs={{1,254},{0,255},{3,5},{2,4},{5,3},{4,2},{7,9},{6,8},{9,7},{8,6},{1... | collective-permute-start | bytes 3145736 | tf_op jit(solution)/shard_map/ppermute | solution.py:625
  77.9 52.7 %collective-permute-start.5 = (bf16[32,128,128]{2,1,0:T(8,128)(2,1)}, bf16[32,128,128]{2,1,0:T(8,128)(2,1)}, u32[]{:S(2)}, u32[]{:S(2)}) collective-permute-start(bf16[32,128,128]{2,1,0:T(8,128)(2,1)} %collective-permute-done.2.b_ref.refs_7_), channel_id=1, source_target_pairs={{255,1},{254,0},{4,3},{5,2},{2,5},{3,4},{8,7},{9,6},{6,9},{7,8},{1... | collective-permute-start | bytes 3145736 | tf_op jit(solution)/shard_map/ppermute | solution.py:624
  80.4 1.0 copy-start.1
  92.0 0.9 copy-start
  176.0 47.7 %collective-permute-start.6 = (bf16[32,64,128]{2,1,0:T(8,128)(2,1)}, bf16[32,64,128]{2,1,0:T(8,128)(2,1)S(1)}, u32[]{:S(2)}, u32[]{:S(2)}) collective-permute-start(bf16[32,64,128]{2,1,0:T(8,128)(2,1)} %get-tuple-element.51), channel_id=1, source_target_pairs={{0,1},{1,0},{2,3},{3,2},{4,5},{5,4},{6,7},{7,6},{8,9},{9,8},{10,11... | collective-permute-start | bytes 1572872 | tf_op jit(solution)/shard_map/ppermute | solution.py:638
  188.7 37.1 %collective-permute-start.7 = (bf16[32,64,128]{2,1,0:T(8,128)(2,1)}, bf16[32,64,128]{2,1,0:T(8,128)(2,1)S(1)}, u32[]{:S(2)}, u32[]{:S(2)}) collective-permute-start(bf16[32,64,128]{2,1,0:T(8,128)(2,1)} %get-tuple-element.57), channel_id=1, source_target_pairs={{0,1},{1,0},{2,3},{3,2},{4,5},{5,4},{6,7},{7,6},{8,9},{9,8},{10,11... | collective-permute-start | bytes 1572872 | tf_op jit(solution)/shard_map/ppermute | solution.py:641

commit v4 on v3

--- a/solution.py
+++ b/solution.py
@@ -58,14 +58,12 @@
 def exchange_kernel(chips, parts, x_ref, *refs):
     sources, refs = refs[:parts], refs[parts:]
     o_ref, refs = refs[0], refs[1:]
-    targets, refs = refs[: parts + 1 if parts else 0], refs[parts + 1 if parts else 0 :]
+    targets, refs = refs[:parts], refs[parts:]
     held, send, recv, mate_send, mate_recv, local, part_send, part_recv = refs
-    me, core, wraps = place()
+    me, core, _ = place()
     shift = lax.axis_index("shift")
     chip = lax.div(me, 2)
     mate = me + 1 - 2 * core
-    beside = lax.rem(chip + chips - 1 + 2 * core, chips) * 2 + 1 - core
-    beside_shift = shift + wraps * (1 - 2 * shift)
     barrier = pltpu.get_barrier_semaphore()
 
     def greet(box, along):
@@ -73,8 +71,6 @@
             barrier, inc=1, device_id=(box, along), device_id_type=pl.DeviceIdType.MESH
         )
 
-    if parts:
-        greet(beside, beside_shift)
     greet(mate, shift)
 
     @pl.loop(1, chips)
@@ -83,7 +79,7 @@
 
     own = pltpu.make_async_copy(x_ref.at[:, core], held.at[:, core], local)
     own.start()
-    pl.semaphore_wait(barrier, chips + (1 if parts else 0))
+    pl.semaphore_wait(barrier, chips)
     across = pltpu.make_async_remote_copy(
         x_ref.at[:, 1 - core],
         held.at[:, core],
@@ -93,21 +89,19 @@
         device_id_type=pl.DeviceIdType.MESH,
     )
     across.start()
-    moves = []
-    if parts:
-        ends = [(source, (mate, shift)) for source in sources]
-        ends.append((sources[-1], (beside, beside_shift)))
-        for i in reversed(range(parts + 1)):
-            move = pltpu.make_async_remote_copy(
-                ends[i][0],
-                targets[i],
-                part_send.at[i],
-                part_recv.at[i],
-                device_id=ends[i][1],
-                device_id_type=pl.DeviceIdType.MESH,
-            )
-            move.start()
-            moves.append(move)
+    moves = [
+        pltpu.make_async_remote_copy(
+            sources[i],
+            targets[i],
+            part_send.at[i],
+            part_recv.at[i],
+            device_id=(mate, shift),
+            device_id_type=pl.DeviceIdType.MESH,
+        )
+        for i in range(parts)
+    ]
+    for move in moves:
+        move.start()
     own.wait()
     across.wait()
 
@@ -136,17 +130,16 @@
 def exchange(blocks, *parts):
     count, samples, r = blocks.shape
     shape = (count // 2, 2, samples, r)
-    moved = [*parts, *parts[-1:]]
     n = len(parts)
     blocks, *moved = pl.pallas_call(
         functools.partial(exchange_kernel, count // 2, n),
         out_shape=[jax.ShapeDtypeStruct(shape, BF)]
-        + [jax.ShapeDtypeStruct(part.shape, BF) for part in moved],
+        + [jax.ShapeDtypeStruct(part.shape, BF) for part in parts],
         in_specs=[VMEM] + [ANY] * n,
-        out_specs=[VMEM] + [ANY] * len(moved),
+        out_specs=[VMEM] + [ANY] * n,
         scratch_shapes=[pltpu.VMEM(shape, BF)]
         + [pltpu.SemaphoreType.DMA] * 5
-        + [pltpu.SemaphoreType.DMA((max(len(moved), 1),))] * 2,
+        + [pltpu.SemaphoreType.DMA((max(n, 1),))] * 2,
         compiler_params=pltpu.CompilerParams(
             has_side_effects=True, collective_id=1 if n else 0, vmem_limit_bytes=56 * MIB
         ),
@@ -235,16 +228,16 @@
         patterns[at + 2 * pair + 1] = dot_nt(eye, upper[:, r:]).astype(BF)
 
 
-def beside_kernel(_, mate_ref, a_ref, b_ref, radiate_ref, one_ref, patterns_ref):
+def beside_kernel(_, mate_ref, first_ref, radiate_ref, one_ref, patterns_ref):
     step = pl.program_id(0)
-    for when, ref in ((step < 2, mate_ref), (step == 2, a_ref), (step == 3, b_ref)):
+    for when, ref in ((step < 2, mate_ref), (step >= 2, first_ref)):
 
         @pl.when(when)
         def _(ref=ref):
             fill_patterns(lambda i: ref[i], patterns_ref, 0, radiate_ref[...], one_ref)
 
 
-def patterns_beside(core, mate, first_a, first_b, radiate, one):
+def patterns_beside(core, mate, first, radiate, one):
     count, u, r = mate.shape
     _, k1, k0 = one.shape
 
@@ -252,7 +245,6 @@
         towards = 4 * core[0]
         return (jnp.where(i < 2, 4 - towards + i, towards + i - 2), 0, 0)
 
-    whole = pl.BlockSpec((count // 2, u, r), lambda i, _: (0, 0, 0))
     return pl.pallas_call(
         beside_kernel,
         out_shape=jax.ShapeDtypeStruct((3 * count // 8, r, k1), BF),
@@ -261,8 +253,7 @@
             grid=(4,),
             in_specs=[
                 pl.BlockSpec((count // 2, u, r), lambda i, _: (jnp.minimum(i, 1), 0, 0)),
-                whole,
-                whole,
+                pl.BlockSpec((count // 2, u, r), lambda i, _: (jnp.maximum(i - 2, 0), 0, 0)),
                 VMEM,
                 VMEM,
             ],
@@ -271,7 +262,7 @@
         compiler_params=pltpu.CompilerParams(vmem_limit_bytes=56 * MIB),
         cost_estimate=pl.CostEstimate(flops=4_000_000_000, bytes_accessed=30 * MIB, transcendentals=0),
         name="patterns_beside",
-    )(core, mate, first_a, first_b, radiate, one)
+    )(core, mate, first, radiate, one)
 
 
 def translate_kernel(width, source_ref, offset_ref, rounds_ref, coarse_ref, weight_ref, out_ref):
@@ -320,7 +311,6 @@
     step = pl.program_id(0)
     me, core, wraps = place()
     count = sources[0].shape[0]
-    half = count // 2
 
     @pl.when(step == 0)
     def _():
@@ -330,13 +320,9 @@
             (0, count),
             (0, within),
             (1, count),
-            (1, count + half),
             (1, within),
-            (1, within + half),
             (wraps, towards),
-            (wraps, towards + half),
             (1 - wraps, towards),
-            (1 - wraps, towards + half),
         )
         copies = [
             pltpu.make_async_copy(src, held.at[kind, pl.ds(at, src.shape[0])], sems.at[i])
@@ -399,7 +385,7 @@
 
 
 def local_kernel(
-    width, source_ref, offset_ref, last_a, last_b, mine, beside, radiate_ref, one_ref, two_ref,
+    width, source_ref, offset_ref, last, mine, beside, radiate_ref, one_ref, two_ref,
     table_ref, incoming_ref, local_ref, held, patterns, flat, weights, across, sems,
 ):
     step = pl.program_id(0)
@@ -430,14 +416,9 @@
 
         @pl.when(wraps == 1)
         def _():
-            halves = [
-                pltpu.make_async_copy(last_a, held.at[pl.ds(0, half)], sems.at[2]),
-                pltpu.make_async_copy(last_b, held.at[pl.ds(half, half)], sems.at[3]),
-            ]
-            for copy in halves:
-                copy.start()
-            for copy in halves:
-                copy.wait()
+            copy = pltpu.make_async_copy(last, held, sems.at[2])
+            copy.start()
+            copy.wait()
 
             @pl.loop(0, 2)
             def _(i):
@@ -469,9 +450,9 @@
     local_ref[...] = (across[...] + dot(flat[...], two_ref[0])).astype(BF)
 
 
-def local_field(source, offset, last_a, last_b, mine, beside, radiate, one, two, table, incoming):
+def local_field(source, offset, last, mine, beside, radiate, one, two, table, incoming):
     octants, k2, k1 = two.shape
-    _, u, r = last_a.shape
+    _, u, r = last.shape
     width = source.shape[0] // octants
     return pl.pallas_call(
         functools.partial(local_kernel, width),
@@ -479,7 +460,7 @@
         grid_spec=pltpu.PrefetchScalarGridSpec(
             num_scalar_prefetch=2,
             grid=(octants,),
-            in_specs=[ANY] * 4
+            in_specs=[ANY] * 3
             + [VMEM, VMEM, pl.BlockSpec((1, k2, k1), lambda i, *_: (i, 0, 0)), VMEM, VMEM],
             out_specs=pl.BlockSpec((r, k1), lambda i, *_: (i, 0)),
             scratch_shapes=[
@@ -488,13 +469,13 @@
                 pltpu.VMEM((r, k2), BF),
                 pltpu.VMEM((width, k1), F32),
                 pltpu.VMEM((r, k1), F32),
-                pltpu.SemaphoreType.DMA((4,)),
+                pltpu.SemaphoreType.DMA((3,)),
             ],
         ),
         compiler_params=pltpu.CompilerParams(vmem_limit_bytes=56 * MIB),
         cost_estimate=pl.CostEstimate(flops=5_000_000_000, bytes_accessed=50 * MIB, transcendentals=0),
         name="local_field",
-    )(source, offset, last_a, last_b, mine, beside, radiate, one, two, table, incoming)
+    )(source, offset, last, mine, beside, radiate, one, two, table, incoming)
 
 
 def leaves_kernel(
@@ -608,31 +589,25 @@
         *translation_lists(trans_two, level2_source, level2_offset, x.shape[2]),
     )
 
-    first_a, first_b = [
-        lax.ppermute(half, BOTH, hops[0]) for half in (x[: count // 2], x[count // 2 :])
-    ]
+    first = lax.ppermute(x, BOTH, hops[0])
     mate = lax.ppermute(x, "box", swap)
     coarse, mine = upward(x, radiate, interp_one, interp_two)
 
-    (first_a,) = after([first_a], coarse)
-    partner_a = lax.ppermute(first_a, BOTH, hops[1])
-    coarse, *lists = after([coarse, *lists], first_a)
+    (first,) = after([first], coarse)
+    partner = lax.ppermute(first, BOTH, hops[1])
+    beside = patterns_beside(core.reshape(1), mate, first, radiate, interp_one)
+    coarse, *lists = after([coarse, *lists], beside)
     index, source, offset, turned_radiate, half_at, *translation = lists
     (gathered,) = exchange(coarse.reshape(boxes, k2 // boxes, -1))
 
-    first_b, partner_a = after([first_b, partner_a], gathered)
-    partner_b = lax.ppermute(first_b, BOTH, hops[1])
-    last_a = lax.ppermute(partner_a, BOTH, hops[2])
+    (partner,) = after([partner], gathered)
+    last = lax.ppermute(partner, BOTH, hops[2])
     turned = translate(gathered, *translation)
-    beside = patterns_beside(core.reshape(1), mate, first_a, first_b, radiate, interp_one)
-    (turned,) = after([turned], beside, last_a)
-    incoming, partner_mate_a, partner_mate_b, last_b = exchange(turned, partner_a, partner_b)
+    incoming, partner_mate = exchange(turned, partner)
     incoming = incoming.reshape(k2, -1)
 
     (index,) = after([index], incoming)
-    here = (
-        x, mate, partner_a, partner_b, partner_mate_a, partner_mate_b, first_a, first_b, last_a, last_b
-    )
+    here = (x, mate, partner, partner_mate, first, last)
     early = count // 2
     own_a, other_a = near_field(0, early, index, near_blocks, *here)
     back_a = lax.ppermute(other_a, "shift", partners)
@@ -641,7 +616,7 @@
     back_b = lax.ppermute(other_b, "shift", partners)
     source, offset = after([source, offset], other_b)
     local = local_field(
-        source, offset, last_a, last_b, mine, beside, radiate, interp_one, interp_two, trans_one, incoming
+        source, offset, last, mine, beside, radiate, interp_one, interp_two, trans_one, incoming
     )
     base = leaf_fields(x, own_a, own_b, sigma, turned_radiate, interp_one, local)
     base = add_rows(half_at, 0, base, back_a)

time: 229 us -> 231 us (level)
  Pallas kernels: 166 us -> 190 us
  waiting for transfers between devices: 26.1 us -> 9.31 us
  starting transfers between devices: 27.2 us -> 22.8 us
    pallas_call x2, Pallas kernels: 71.7 us -> 97.1 us  [exchange(): pl.pallas_call(functools.partial(exchange_kernel, count // 2, n), out_sha...]
    ppermute x5 -> x3, waiting for transfers between devices: 26 us -> 9.3 us  [the longest x1 9.3 us: body(): first = lax.ppermute(x, BOTH, hops[0])]
    ppermute x5 -> x3, starting transfers between devices: 20.8 us -> 16.5 us  [the longest x1 7.8 us: body(): first = lax.ppermute(x, BOTH, hops[0])]
    slice x1 -> x0, local copies, waits for them, and re-layouts: 2.76 us -> none  [body(): x[count // 2:]]
  transfers between devices with their start and end apart: 8 -> 6, of which waited for: 2 -> 1; matrix products, arithmetic and copies ran while one was open for 2% -> 2% of each run, Pallas kernels for 52% -> 77%
where the time goes in v4:
time: 231 us; the launch traced here: 229 us
  Pallas kernels  190 us (82%)
  starting transfers between devices  22.8 us (10%)
  waiting for transfers between devices  9.31 us (4%)
  local copies, waits for them, and re-layouts  7.08 us (3%)
    pallas_call x2, Pallas kernels, exchange(): pl.pallas_call(functools.partial(exchange_kernel, count // 2, n), out_sha...  97.1 us
    pallas_call x2, Pallas kernels, near_field(): pl.pallas_call(functools.partial(near_kernel, group, slots, start), out_s...  21.5 us
    pallas_call x1, Pallas kernels, local_field(): pl.pallas_call(functools.partial(local_kernel, width), out_shape=jax.Shap...  20.8 us
    pallas_call x1, Pallas kernels, upward(): pl.pallas_call(upward_kernel, grid=(octants // 2,), out_shape=[jax.ShapeD...  14.7 us
    pallas_call x1, Pallas kernels, patterns_beside(): pl.pallas_call(beside_kernel, out_shape=jax.ShapeDtypeStruct((3 * count /...  11.4 us
    pallas_call x1, Pallas kernels, translate(): pl.pallas_call(functools.partial(translate_kernel, source.shape[0] // coa...  10.3 us
    pallas_call x1, Pallas kernels, leaf_fields(): pl.pallas_call(functools.partial(leaves_kernel, early), grid=(octants,),...  9.87 us
    ppermute x1, waiting for transfers between devices, body(): first = lax.ppermute(x, BOTH, hops[0])  9.3 us
  transfers between devices with their start and end apart: 6, of which 1 were waited for; matrix products, arithmetic and copies ran while one was open for 2% of the time, Pallas kernels for 77%

profile of v4, /device:TPU:2, one launch (start us, length us, event | category | flops | bytes accessed | tf_op | source)
XLA Modules:
  0.0 229.3 jit_solution(14040365815827276711)
XLA Ops:
  0.0 0.0 copy-start.4
  0.0 0.0 copy-start.9
  0.0 0.0 copy-start.10
  0.0 0.0 copy-start.8
  0.0 0.0 copy-start.6
  0.0 0.0 copy-start.7
  0.0 0.0 copy-start.5
  0.0 7.8 %collective-permute-start.1 = (bf16[64,128,128]{2,1,0:T(8,128)(2,1)}, bf16[64,128,128]{2,1,0:T(8,128)(2,1)}, u32[]{:S(2)}, u32[]{:S(2)}) collective-permute-start(bf16[64,128,128]{2,1,0:T(8,128)(2,1)} %bitcast.17), channel_id=1, source_target_pairs={{0,255},{1,254},{2,4},{3,5},{4,2},{5,3},{6,8},{7,9},{8,6},{9,7},{1... | collective-permute-start | bytes 6291464 | tf_op jit(solution)/shard_map/ppermute | solution.py:592
  7.9 0.0 collective-permute-start
  7.9 14.7 %upward.1 = (bf16[2048,128]{1,0:T(8,128)(2,1)}, bf16[8,128,512]{2,1,0:T(8,128)(2,1)}) custom-call(bf16[64,128,128]{2,1,0:T(8,128)(2,1)} %bitcast.19, bf16[128,128]{1,0:T(8,128)(2,1)} %radiate_ref.5, bf16[8,512,128]{2,1,0:T(8,128)(2,1)} %one_ref.7, bf16[8,2048,512]{2,1,0:T(8,128)(2,1)} %two_ref.3), custom_call_target="tpu_custom_call" | custom-call | flops 7000000000 | bytes 52428800 | tf_op jit(solution)/shard_map/upward/pallas_call | solution.py:198
  22.6 9.3 %collective-permute-done.1.first_ref.refs_4_ = bf16[64,128,128]{2,1,0:T(8,128)(2,1)} collective-permute-done((bf16[64,128,128]{2,1,0:T(8,128)(2,1)}, bf16[64,128,128]{2,1,0:T(8,128)(2,1)}, u32[]{:S(2)}, u32[]{:S(2)}) %collective-permute-start.1) | collective-permute-done | bytes 2097184 | tf_op jit(solution)/shard_map/ppermute | solution.py:592
  31.9 4.7 %collective-permute-start.2 = (bf16[64,128,128]{2,1,0:T(8,128)(2,1)}, bf16[64,128,128]{2,1,0:T(8,128)(2,1)S(1)}, u32[]{:S(2)}, u32[]{:S(2)}) collective-permute-start(bf16[64,128,128]{2,1,0:T(8,128)(2,1)} %collective-permute-done.1.first_ref.refs_4_), channel_id=1, source_target_pairs={{255,1},{254,0},{4,3},{5,2},{2,5},{3,4},{8,7},{9,6},{6,9},{7,8},{1... | collective-permute-start | bytes 6291464 | tf_op jit(solution)/shard_map/ppermute | solution.py:597
  36.6 0.0 copy-done.4
  36.6 0.7 copy.19
  37.3 0.0 copy-done.9
  37.3 0.6 reshape.41.source_ref
  37.9 0.0 copy-done.10
  37.9 0.6 reshape.42.offset_ref
  38.5 0.0 copy-done.8
  38.5 0.1 copy.18
  38.6 0.7 reshape.40.index_ref
  39.3 0.0 copy-done.6
  39.3 0.0 copy-done.7
  39.3 0.1 copy.20
  39.4 0.1 reshape.44.source_ref
  39.5 0.1 copy.21
  39.6 0.1 reshape.45.offset_ref
  39.7 0.0 copy-done.5
  39.7 0.1 copy.23
  39.8 0.0 collective-permute-done.mate_ref.refs_1_
  39.9 11.4 %patterns_beside.1.beside = bf16[24,128,512]{2,1,0:T(8,128)(2,1)} custom-call(s32[1]{0:T(128)} %bitcast.3._, bf16[64,128,128]{2,1,0:T(8,128)(2,1)} %collective-permute-done.mate_ref.refs_1_, bf16[64,128,128]{2,1,0:T(8,128)(2,1)} %collective-permute-done.1.first_ref.refs_4_, bf16[128,128]{1,0:T(8,128)(2,1)} %radiate_ref.5, bf16[8,512,128]{2,1,0:T(8,128)(2,1)} %one_ref.7), custom_call_target="tpu_custom_call" | custom-call | flops 4000000000 | bytes 31457280 | tf_op jit(solution)/shard_map/patterns_beside/pallas_call | solution.py:248
  51.3 0.7 broadcast_in_dim.15.weight_ref
  52.0 61.2 %exchange.2 = bf16[64,2,16,128]{3,2,1,0:T(8,128)(2,1)} custom-call(bf16[64,2,16,128]{3,2,1,0:T(8,128)(2,1)} %bitcast.26), custom_call_target="tpu_custom_call" | custom-call | bytes 83886080 | tf_op jit(solution)/shard_map/exchange/pallas_call | solution.py:134
  113.2 0.0 collective-permute-done.2.refs_0_.refs_2_
  113.2 0.0 copy-start.2
  113.2 4.0 %collective-permute-start.3 = (bf16[64,128,128]{2,1,0:T(8,128)(2,1)S(1)}, bf16[64,128,128]{2,1,0:T(8,128)(2,1)S(1)}, u32[]{:S(2)}, u32[]{:S(2)}) collective-permute-start(bf16[64,128,128]{2,1,0:T(8,128)(2,1)S(1)} %collective-permute-done.2.refs_0_.refs_2_), channel_id=1, source_target_pairs={{1,254},{0,255},{3,5},{2,4},{5,3},{4,2},{7,9},{6,8},{9,7},{8,6},{1... | collective-permute-start | bytes 6291464 | tf_op jit(solution)/shard_map/ppermute | solution.py:604
  117.2 0.0 copy-start.1
  117.2 1.0 copy-done.1
  118.2 10.3 %translate.1 = bf16[128,16,128]{2,1,0:T(8,128)(2,1)S(1)} custom-call(s32[4096]{0:T(1024)S(1)} %reshape.44.source_ref, s32[4096]{0:T(1024)S(1)} %reshape.45.offset_ref, s32[128]{0:T(128)S(1)} %and_select_fusion.rounds_ref, bf16[128,16,128]{2,1,0:T(8,128)(2,1)S(1)} %bitcast.15, f32[317,16,128]{2,1,0:T(8,128)S(1)} %broadcast_in_dim.15.weight_ref), custom_call_target="tpu_custom_call" | custom-call | flops 2000000000 | bytes 26214400 | tf_op jit(solution)/shard_map/translate/pallas_call | solution.py:297
  128.5 0.0 copy-done.2
  128.5 0.0 copy-start
  128.5 0.8 copy-done
  129.3 35.9 %exchange.3 = (bf16[64,2,16,128]{3,2,1,0:T(8,128)(2,1)}, bf16[64,128,128]{2,1,0:T(8,128)(2,1)}) custom-call(bf16[64,2,16,128]{3,2,1,0:T(8,128)(2,1)} %bitcast.14, bf16[64,128,128]{2,1,0:T(8,128)(2,1)} %copy-done.2), custom_call_target="tpu_custom_call" | custom-call | bytes 83886080 | tf_op jit(solution)/shard_map/exchange/pallas_call | solution.py:134
  165.2 0.0 collective-permute-done.3.refs_5_.last
  165.2 0.0 copy-start.3
  165.2 1.3 copy-done.3
  166.6 10.8 %near_field.2 = (f32[32,64,128]{2,1,0:T(8,128)}, bf16[32,64,128]{2,1,0:T(8,128)(2,1)}) custom-call(s32[384]{0:T(512)} %reshape.40.index_ref, bf16[64,6,64,128]{3,2,1,0:T(8,128)(2,1)} %blocks_ref.3, bf16[64,128,128]{2,1,0:T(8,128)(2,1)} %bitcast.20, bf16[64,128,128]{2,1,0:T(8,128)(2,1)} %collective-permute-done.mate_ref.refs_1_, ...), custom_call_target="tpu_custom_call" | custom-call | flops 3000000000 | bytes 20971520 | tf_op jit(solution)/shard_map/near_field/pallas_call | solution.py:362
  177.4 3.2 %collective-permute-start.4 = (bf16[32,64,128]{2,1,0:T(8,128)(2,1)}, bf16[32,64,128]{2,1,0:T(8,128)(2,1)S(1)}, u32[]{:S(2)}, u32[]{:S(2)}) collective-permute-start(bf16[32,64,128]{2,1,0:T(8,128)(2,1)} %get-tuple-element.43), channel_id=1, source_target_pairs={{0,1},{1,0},{2,3},{3,2},{4,5},{5,4},{6,7},{7,6},{8,9},{9,8},{10,11... | collective-permute-start | bytes 1572872 | tf_op jit(solution)/shard_map/ppermute | solution.py:613
  180.5 10.8 %near_field.3 = (f32[32,64,128]{2,1,0:T(8,128)}, bf16[32,64,128]{2,1,0:T(8,128)(2,1)}) custom-call(s32[384]{0:T(512)} %reshape.40.index_ref, bf16[64,6,64,128]{3,2,1,0:T(8,128)(2,1)} %blocks_ref.3, bf16[64,128,128]{2,1,0:T(8,128)(2,1)} %bitcast.21, bf16[64,128,128]{2,1,0:T(8,128)(2,1)} %collective-permute-done.mate_ref.refs_1_, ...), custom_call_target="tpu_custom_call" | custom-call | flops 3000000000 | bytes 20971520 | tf_op jit(solution)/shard_map/near_field/pallas_call | solution.py:362
  191.3 3.1 %collective-permute-start.5 = (bf16[32,64,128]{2,1,0:T(8,128)(2,1)}, bf16[32,64,128]{2,1,0:T(8,128)(2,1)S(1)}, u32[]{:S(2)}, u32[]{:S(2)}) collective-permute-start(bf16[32,64,128]{2,1,0:T(8,128)(2,1)} %get-tuple-element.49), channel_id=1, source_target_pairs={{0,1},{1,0},{2,3},{3,2},{4,5},{5,4},{6,7},{7,6},{8,9},{9,8},{10,11... | collective-permute-start | bytes 1572872 | tf_op jit(solution)/shard_map/ppermute | solution.py:616
  194.4 20.8 %local_field.1.local_ref = bf16[1024,512]{1,0:T(8,128)(2,1)} custom-call(s32[128]{0:T(128)} %reshape.41.source_ref, s32[128]{0:T(128)} %reshape.42.offset_ref, bf16[64,128,128]{2,1,0:T(8,128)(2,1)} %copy-done.3, bf16[8,128,512]{2,1,0:T(8,128)(2,1)} %get-tuple-element.52.mine, bf16[24,128,512]{2,1,0:T(8,128)(2,1)} %patterns_beside.1.beside, ...), custom_call_target="tpu_custom_call" | custom-call | flops 5000000000 | bytes 52428800 | tf_op jit(solution)/shard_map/local_field/pallas_call | solution.py:457
  215.3 9.9 %leaf_fields.1 = f32[8,8,128,128]{3,2,1,0:T(8,128)} custom-call(bf16[8,8,128,128]{3,2,1,0:T(8,128)(2,1)} %bitcast.22, f32[4,8,64,128]{3,2,1,0:T(8,128)} %bitcast.23, f32[4,8,64,128]{3,2,1,0:T(8,128)} %bitcast.24, f32[2]{0:T(128)} %bitcast.28, bf16[128,128]{1,0:T(8,128)(2,1)} %bitcast.27, bf16[8,512,128]{2,1,0:T(8,128)(2,1)} %one_ref.7, ...), custom_call_target="tpu_custom_call" | custom-call | flops 2000000000 | bytes 20971520 | tf_op jit(solution)/shard_map/leaf_fields/pallas_call | solution.py:513
  225.1 0.0 collective-permute-done.4.back_ref
  225.1 2.1 add_rows.2.base_ref
  227.2 0.0 collective-permute-done.5.back_ref
  227.2 2.1 add_rows.3
  (3 shorter events, 0.0 us)
Async XLA Ops:
  0.0 36.6 %copy-start.4 = (bf16[128,128]{1,0:T(8,128)(2,1)S(1)}, bf16[128,128]{1,0:T(8,128)(2,1)}, u32[]{:S(2)}) copy-start(bf16[128,128]{1,0:T(8,128)(2,1)} %radiate_ref.5) | copy-start | bytes 98308
  0.0 37.3 %copy-start.9 = (s32[8,16]{1,0:T(8,128)S(1)}, s32[8,16]{1,0:T(8,128)}, u32[]{:S(2)}) copy-start(s32[8,16]{1,0:T(8,128)} %param.21) | copy-start | bytes 1540
  0.0 37.9 %copy-start.10 = (s32[8,16]{1,0:T(8,128)S(1)}, s32[8,16]{1,0:T(8,128)}, u32[]{:S(2)}) copy-start(s32[8,16]{1,0:T(8,128)} %param.22) | copy-start | bytes 1540
  0.0 38.5 %copy-start.8 = (s32[64,6]{0,1:T(8,128)S(1)}, s32[64,6]{0,1:T(8,128)}, u32[]{:S(2)}) copy-start(s32[64,6]{0,1:T(8,128)} %param.16) | copy-start | bytes 4612
  0.0 39.3 %copy-start.6 = (s32[128,32]{0,1:T(8,128)S(1)}, s32[128,32]{0,1:T(8,128)}, u32[]{:S(2)}) copy-start(s32[128,32]{0,1:T(8,128)} %param.24) | copy-start | bytes 49156
  0.0 39.3 %copy-start.7 = (s32[128,32]{0,1:T(8,128)S(1)}, s32[128,32]{0,1:T(8,128)}, u32[]{:S(2)}) copy-start(s32[128,32]{0,1:T(8,128)} %param.25) | copy-start | bytes 49156
  0.0 39.6 %copy-start.5 = (f32[316,16]{0,1:T(8,128)S(1)}, f32[316,16]{0,1:T(8,128)}, u32[]{:S(2)}) copy-start(f32[316,16]{0,1:T(8,128)} %param.23) | copy-start | bytes 60676
  0.0 31.8 %collective-permute-start.1 = (bf16[64,128,128]{2,1,0:T(8,128)(2,1)}, bf16[64,128,128]{2,1,0:T(8,128)(2,1)}, u32[]{:S(2)}, u32[]{:S(2)}) collective-permute-start(bf16[64,128,128]{2,1,0:T(8,128)(2,1)} %bitcast.17), channel_id=1, source_target_pairs={{0,255},{1,254},{2,4},{3,5},{4,2},{5,3},{6,8},{7,9},{8,6},{9,7},{1... | collective-permute-start | bytes 6291464 | tf_op jit(solution)/shard_map/ppermute | solution.py:592
  7.9 32.0 %collective-permute-start = (bf16[64,128,128]{2,1,0:T(8,128)(2,1)}, bf16[64,128,128]{2,1,0:T(8,128)(2,1)}, u32[]{:S(2)}, u32[]{:S(2)}) collective-permute-start(bf16[64,128,128]{2,1,0:T(8,128)(2,1)} %bitcast.18), channel_id=1, source_target_pairs={{0,2},{2,0},{4,6},{6,4},{8,10},{10,8},{12,14},{14,12},{16,18},{18,... | collective-permute-start | bytes 6291464 | tf_op jit(solution)/shard_map/ppermute | solution.py:593
  31.9 81.3 %collective-permute-start.2 = (bf16[64,128,128]{2,1,0:T(8,128)(2,1)}, bf16[64,128,128]{2,1,0:T(8,128)(2,1)S(1)}, u32[]{:S(2)}, u32[]{:S(2)}) collective-permute-start(bf16[64,128,128]{2,1,0:T(8,128)(2,1)} %collective-permute-done.1.first_ref.refs_4_), channel_id=1, source_target_pairs={{255,1},{254,0},{4,3},{5,2},{2,5},{3,4},{8,7},{9,6},{6,9},{7,8},{1... | collective-permute-start | bytes 6291464 | tf_op jit(solution)/shard_map/ppermute | solution.py:597
  113.2 15.3 %copy-start.2 = (bf16[64,128,128]{2,1,0:T(8,128)(2,1)}, bf16[64,128,128]{2,1,0:T(8,128)(2,1)S(1)}, u32[]{:S(2)}) copy-start(bf16[64,128,128]{2,1,0:T(8,128)(2,1)S(1)} %collective-permute-done.2.refs_0_.refs_2_) | copy-start | bytes 6291460
  113.2 52.0 %collective-permute-start.3 = (bf16[64,128,128]{2,1,0:T(8,128)(2,1)S(1)}, bf16[64,128,128]{2,1,0:T(8,128)(2,1)S(1)}, u32[]{:S(2)}, u32[]{:S(2)}) collective-permute-start(bf16[64,128,128]{2,1,0:T(8,128)(2,1)S(1)} %collective-permute-done.2.refs_0_.refs_2_), channel_id=1, source_target_pairs={{1,254},{0,255},{3,5},{2,4},{5,3},{4,2},{7,9},{6,8},{9,7},{8,6},{1... | collective-permute-start | bytes 6291464 | tf_op jit(solution)/shard_map/ppermute | solution.py:604
  117.2 1.0 copy-start.1
  128.5 0.8 copy-start
  165.2 1.4 copy-start.3
  177.4 47.8 %collective-permute-start.4 = (bf16[32,64,128]{2,1,0:T(8,128)(2,1)}, bf16[32,64,128]{2,1,0:T(8,128)(2,1)S(1)}, u32[]{:S(2)}, u32[]{:S(2)}) collective-permute-start(bf16[32,64,128]{2,1,0:T(8,128)(2,1)} %get-tuple-element.43), channel_id=1, source_target_pairs={{0,1},{1,0},{2,3},{3,2},{4,5},{5,4},{6,7},{7,6},{8,9},{9,8},{10,11... | collective-permute-start | bytes 1572872 | tf_op jit(solution)/shard_map/ppermute | solution.py:613
  191.3 35.9 %collective-permute-start.5 = (bf16[32,64,128]{2,1,0:T(8,128)(2,1)}, bf16[32,64,128]{2,1,0:T(8,128)(2,1)S(1)}, u32[]{:S(2)}, u32[]{:S(2)}) collective-permute-start(bf16[32,64,128]{2,1,0:T(8,128)(2,1)} %get-tuple-element.49), channel_id=1, source_target_pairs={{0,1},{1,0},{2,3},{3,2},{4,5},{5,4},{6,7},{7,6},{8,9},{9,8},{10,11... | collective-permute-start | bytes 1572872 | tf_op jit(solution)/shard_map/ppermute | solution.py:616

commit v5 on v2

--- a/solution.py
+++ b/solution.py
@@ -94,21 +94,6 @@
         device_id_type=pl.DeviceIdType.MESH,
     )
     across.start()
-    own.wait()
-    across.wait()
-
-    @pl.loop(1, chips)
-    def _(step):
-        other = lax.rem(chip + step, chips)
-        pltpu.make_async_remote_copy(
-            held.at[other],
-            o_ref.at[chip],
-            send,
-            recv,
-            device_id=(other * 2 + core, shift),
-            device_id_type=pl.DeviceIdType.MESH,
-        ).start()
-
     moves = []
     for i in range(parts):
         for j, (ref, device) in enumerate(
@@ -124,6 +109,21 @@
             )
             move.start()
             moves.append(move)
+    own.wait()
+    across.wait()
+
+    @pl.loop(1, chips)
+    def _(step):
+        other = lax.rem(chip + step, chips)
+        pltpu.make_async_remote_copy(
+            held.at[other],
+            o_ref.at[chip],
+            send,
+            recv,
+            device_id=(other * 2 + core, shift),
+            device_id_type=pl.DeviceIdType.MESH,
+        ).start()
+
     own = pltpu.make_async_copy(held.at[chip], o_ref.at[chip], local)
     own.start()
     own.wait()

time: 225 us -> 226 us (level)
  Pallas kernels: 185 us -> 189 us
    pallas_call x2, Pallas kernels: 91.9 us -> 96 us  [exchange(): pl.pallas_call(functools.partial(exchange_kernel, count // 2, n), out_sha...]
  transfers between devices with their start and end apart: 7 -> 7, of which waited for: 2 -> 1; matrix products, arithmetic and copies ran while one was open for 2% -> 2% of each run, Pallas kernels for 52% -> 52%
where the time goes in v5:
time: 226 us; the launch traced here: 225 us
  Pallas kernels  189 us (84%)
  starting transfers between devices  23 us (10%)
  local copies, waits for them, and re-layouts  9.75 us (4%)
    pallas_call x2, Pallas kernels, exchange(): pl.pallas_call(functools.partial(exchange_kernel, count // 2, n), out_sha...  96 us
    pallas_call x1, Pallas kernels, downward(): pl.pallas_call(functools.partial(downward_kernel, width), out_shape=jax.S...  29.2 us
    pallas_call x2, Pallas kernels, near_field(): pl.pallas_call(functools.partial(near_kernel, group, slots, part), out_sh...  20.8 us
    pallas_call x1, Pallas kernels, upward(): pl.pallas_call(upward_kernel, grid=(octants // 2,), out_shape=[jax.ShapeD...  15.6 us
    pallas_call x1, Pallas kernels, patterns_beside(): pl.pallas_call(beside_kernel, out_shape=jax.ShapeDtypeStruct((3 * count /...  11.7 us
    pallas_call x1, Pallas kernels, translate(): pl.pallas_call(functools.partial(translate_kernel, source.shape[0] // coa...  10.6 us
    ppermute x2, starting transfers between devices, body(): lax.ppermute(lax.dynamic_slice_in_dim(x, at * (count // 2), count // 2),...  7.75 us
    pallas_call x2, Pallas kernels, add_rows(): pl.pallas_call(add_kernel, out_shape=jax.ShapeDtypeStruct((count, u, r),...  5.23 us
  transfers between devices with their start and end apart: 7, of which 1 were waited for; matrix products, arithmetic and copies ran while one was open for 2% of the time, Pallas kernels for 52%

profile of v5, /device:TPU:2, one launch (start us, length us, event | category | flops | bytes accessed | tf_op | source)
XLA Modules:
  0.0 224.8 jit_solution(16154555453435880629)
XLA Ops:
  0.0 0.0 copy-start.2
  0.0 2.9 %dynamic-slice_bitcast_fusion = (bf16[32,128,128]{2,1,0:T(8,128)(2,1)}, bf16[32,128,128]{2,1,0:T(8,128)(2,1)S(1)}) fusion(bf16[1,64,128,128]{3,2,1,0:T(8,128)(2,1)} %param.13, s32[]{:T(128)S(6)} %select_n.22, s32[]{:T(128)S(6)} %select_n.21), kind=kLoop, calls=%fused_computation | loop fusion | bytes 4194312 | tf_op jit(solution)/shard_map/dynamic_slice | solution.py:631
  2.9 7.7 %collective-permute-start = (bf16[32,128,128]{2,1,0:T(8,128)(2,1)S(1)}, bf16[32,128,128]{2,1,0:T(8,128)(2,1)}, u32[]{:S(2)}, u32[]{:S(2)}) collective-permute-start(bf16[32,128,128]{2,1,0:T(8,128)(2,1)S(1)} %get-tuple-element.64), channel_id=1, source_target_pairs={{0,255},{1,254},{2,4},{3,5},{4,2},{5,3},{6,8},{7,9},{8,6},{9,7},{1... | collective-permute-start | bytes 3145736 | tf_op jit(solution)/shard_map/ppermute | solution.py:631
  10.6 0.0 collective-permute-start.2
  10.7 0.0 copy-done.2
  10.7 0.0 copy-start.5
  10.7 0.0 copy-start.10
  10.7 0.0 copy-start.11
  10.7 0.0 copy-start.9
  10.7 0.0 copy-start.7
  10.7 0.0 copy-start.8
  10.7 0.0 copy-start.6
  10.7 0.1 collective-permute-start.1
  10.8 15.6 %upward.1 = (bf16[2048,128]{1,0:T(8,128)(2,1)}, bf16[8,128,512]{2,1,0:T(8,128)(2,1)}) custom-call(bf16[64,128,128]{2,1,0:T(8,128)(2,1)} %bitcast.22, bf16[128,128]{1,0:T(8,128)(2,1)} %radiate_ref.5, bf16[8,512,128]{2,1,0:T(8,128)(2,1)} %one_ref.5, bf16[8,2048,512]{2,1,0:T(8,128)(2,1)} %two_ref.3), custom_call_target="tpu_custom_call" | custom-call | flops 7000000000 | bytes 52428800 | tf_op jit(solution)/shard_map/upward/pallas_call | solution.py:205
  26.4 0.0 collective-permute-done.a_ref.refs_6_
  26.4 4.8 %collective-permute-start.3 = (bf16[32,128,128]{2,1,0:T(8,128)(2,1)}, bf16[32,128,128]{2,1,0:T(8,128)(2,1)S(1)}, u32[]{:S(2)}, u32[]{:S(2)}) collective-permute-start(bf16[32,128,128]{2,1,0:T(8,128)(2,1)} %collective-permute-done.a_ref.refs_6_), channel_id=1, source_target_pairs={{255,1},{254,0},{4,3},{5,2},{2,5},{3,4},{8,7},{9,6},{6,9},{7,8},{1... | collective-permute-start | bytes 3145736 | tf_op jit(solution)/shard_map/ppermute | solution.py:638
  31.1 0.0 copy-done.5
  31.1 0.7 copy.19
  31.8 0.0 copy-done.10
  31.9 0.7 reshape.38.source_ref
  32.5 0.0 copy-done.11
  32.5 0.6 reshape.39.offset_ref
  33.1 0.0 copy-done.9
  33.1 0.1 copy.18
  33.2 0.7 reshape.37.index_ref
  33.9 0.0 copy-done.7
  33.9 0.0 copy-done.8
  33.9 0.1 copy.20
  34.0 0.1 reshape.40.source_ref
  34.1 0.1 copy.21
  34.2 0.1 reshape.41.offset_ref
  34.3 0.0 copy-done.6
  34.3 0.1 copy.23
  34.4 0.1 pad_add_fusion.2._
  34.5 0.7 pad_add_fusion
  35.2 0.7 broadcast_in_dim.15.weight_ref
  35.9 36.3 %exchange.2 = bf16[64,2,16,128]{3,2,1,0:T(8,128)(2,1)} custom-call(bf16[64,2,16,128]{3,2,1,0:T(8,128)(2,1)} %bitcast.30), custom_call_target="tpu_custom_call" | custom-call | bytes 83886080 | tf_op jit(solution)/shard_map/exchange/pallas_call | solution.py:141
  72.2 0.0 collective-permute-done.2.b_ref.refs_8_
  72.2 0.0 collective-permute-done.3.refs_0_.refs_2_
  72.2 0.0 copy-start.3
  72.2 4.2 %collective-permute-start.4 = (bf16[32,128,128]{2,1,0:T(8,128)(2,1)}, bf16[32,128,128]{2,1,0:T(8,128)(2,1)S(1)}, u32[]{:S(2)}, u32[]{:S(2)}) collective-permute-start(bf16[32,128,128]{2,1,0:T(8,128)(2,1)} %collective-permute-done.2.b_ref.refs_8_), channel_id=1, source_target_pairs={{255,1},{254,0},{4,3},{5,2},{2,5},{3,4},{8,7},{9,6},{6,9},{7,8},{1... | collective-permute-start | bytes 3145736 | tf_op jit(solution)/shard_map/ppermute | solution.py:644
  76.4 0.0 copy-start.1
  76.4 1.0 copy-done.1
  77.4 10.6 %translate.1 = bf16[128,16,128]{2,1,0:T(8,128)(2,1)S(1)} custom-call(s32[4096]{0:T(1024)S(1)} %reshape.40.source_ref, s32[4096]{0:T(1024)S(1)} %reshape.41.offset_ref, s32[128]{0:T(128)S(1)} %and_select_fusion.rounds_ref, bf16[128,16,128]{2,1,0:T(8,128)(2,1)S(1)} %bitcast.20, f32[317,16,128]{2,1,0:T(8,128)S(1)} %broadcast_in_dim.15.weight_ref), custom_call_target="tpu_custom_call" | custom-call | flops 2000000000 | bytes 26214400 | tf_op jit(solution)/shard_map/translate/pallas_call | solution.py:306
  88.0 0.0 copy-start
  88.0 0.8 copy-done
  88.8 0.0 collective-permute-done.1.mate_ref.refs_1_
  88.8 11.7 %patterns_beside.1.beside = bf16[24,128,512]{2,1,0:T(8,128)(2,1)} custom-call(s32[1]{0:T(128)} %bitcast.3._, bf16[64,128,128]{2,1,0:T(8,128)(2,1)} %collective-permute-done.1.mate_ref.refs_1_, bf16[32,128,128]{2,1,0:T(8,128)(2,1)} %collective-permute-done.a_ref.refs_6_, bf16[32,128,128]{2,1,0:T(8,128)(2,1)} %collective-permute-done.2.b_ref.refs_8_, ...), custom_call_target="tpu_custom_call" | custom-call | flops 4000000000 | bytes 31457280 | tf_op jit(solution)/shard_map/patterns_beside/pallas_call | solution.py:256
  100.6 0.0 copy-done.3
  100.6 1.9 collective-permute-done.4.refs_1_.refs_3_
  102.5 0.0 copy-start.4
  102.5 1.0 copy-done.4
  103.5 59.7 %exchange.3 = (bf16[64,2,16,128]{3,2,1,0:T(8,128)(2,1)}, bf16[32,128,128]{2,1,0:T(8,128)(2,1)}, bf16[32,128,128]{2,1,0:T(8,128)(2,1)}, bf16[32,128,128]{2,1,0:T(8,128)(2,1)}, bf16[32,128,128]{2,1,0:T(8,128)(2,1)}) custom-call(bf16[64,2,16,128]{3,2,1,0:T(8,128)(2,1)} %bitcast.19, bf16[32,128,128]{2,1,0:T(8,128)(2,1)} %copy-done.3, bf16[32,128,128]{2,1,0:T(8,128)(2,1)} %copy-done.4), custom_call_target="tpu_custom_call" | custom-call | bytes 83886080 | tf_op jit(solution)/shard_map/exchange/pallas_call | solution.py:141
  163.2 10.1 %near_field.2 = (f32[32,64,128]{2,1,0:T(8,128)}, bf16[32,64,128]{2,1,0:T(8,128)(2,1)}) custom-call(s32[384]{0:T(512)} %reshape.37.index_ref, s32[2]{0:T(128)} %get-tuple-element.54.halves_ref, bf16[64,6,64,128]{3,2,1,0:T(8,128)(2,1)} %blocks_ref.3, bf16[64,128,128]{2,1,0:T(8,128)(2,1)} %bitcast.23, ...), custom_call_target="tpu_custom_call" | custom-call | flops 3000000000 | bytes 20971520 | tf_op jit(solution)/shard_map/near_field/pallas_call | solution.py:378
  173.4 3.6 %collective-permute-start.5 = (bf16[32,64,128]{2,1,0:T(8,128)(2,1)}, bf16[32,64,128]{2,1,0:T(8,128)(2,1)S(1)}, u32[]{:S(2)}, u32[]{:S(2)}) collective-permute-start(bf16[32,64,128]{2,1,0:T(8,128)(2,1)} %get-tuple-element.58), channel_id=1, source_target_pairs={{0,1},{1,0},{2,3},{3,2},{4,5},{5,4},{6,7},{7,6},{8,9},{9,8},{10,11... | collective-permute-start | bytes 1572872 | tf_op jit(solution)/shard_map/ppermute | solution.py:653
  176.9 10.7 %near_field.3 = (f32[32,64,128]{2,1,0:T(8,128)}, bf16[32,64,128]{2,1,0:T(8,128)(2,1)}) custom-call(s32[384]{0:T(512)} %reshape.37.index_ref, s32[2]{0:T(128)} %get-tuple-element.54.halves_ref, bf16[64,6,64,128]{3,2,1,0:T(8,128)(2,1)} %blocks_ref.3, bf16[64,128,128]{2,1,0:T(8,128)(2,1)} %bitcast.24, ...), custom_call_target="tpu_custom_call" | custom-call | flops 3000000000 | bytes 20971520 | tf_op jit(solution)/shard_map/near_field/pallas_call | solution.py:378
  187.7 2.7 %collective-permute-start.6 = (bf16[32,64,128]{2,1,0:T(8,128)(2,1)}, bf16[32,64,128]{2,1,0:T(8,128)(2,1)S(1)}, u32[]{:S(2)}, u32[]{:S(2)}) collective-permute-start(bf16[32,64,128]{2,1,0:T(8,128)(2,1)} %get-tuple-element.62), channel_id=1, source_target_pairs={{0,1},{1,0},{2,3},{3,2},{4,5},{5,4},{6,7},{7,6},{8,9},{9,8},{10,11... | collective-permute-start | bytes 1572872 | tf_op jit(solution)/shard_map/ppermute | solution.py:656
  190.4 29.2 %downward.1 = f32[8,8,128,128]{3,2,1,0:T(8,128)} custom-call(s32[128]{0:T(128)} %reshape.38.source_ref, s32[128]{0:T(128)} %reshape.39.offset_ref, bf16[8,8,128,128]{3,2,1,0:T(8,128)(2,1)} %bitcast.25, bf16[32,128,128]{2,1,0:T(8,128)(2,1)} %get-tuple-element.48.refs_7_.last_a, bf16[32,128,128]{2,1,0:T(8,128)(2,1)} %get-tuple-element.49.refs_9_.last_b, ...), custom_call_target="tpu_custom_call" | custom-call | flops 8999999488 | bytes 83886080 | tf_op jit(solution)/shard_map/downward/pallas_call | solution.py:523
  219.6 0.0 collective-permute-done.5.back_ref
  219.6 2.6 %add_rows.2.base_ref = f32[64,128,128]{2,1,0:T(8,128)} custom-call(s32[2]{0:T(128)S(1)} %pad_add_fusion.2._, f32[64,128,128]{2,1,0:T(8,128)} %bitcast.21, bf16[32,64,128]{2,1,0:T(8,128)(2,1)S(1)} %collective-permute-done.5.back_ref), custom_call_target="tpu_custom_call", output_to_operand_aliasing={{}: (1, {})} | custom-call | bytes 3145728 | tf_op jit(solution)/shard_map/add_rows/pallas_call | solution.py:574
  222.2 0.0 collective-permute-done.6.back_ref
  222.2 2.6 %add_rows.3 = f32[64,128,128]{2,1,0:T(8,128)} custom-call(s32[2]{0:T(128)S(1)} %get-tuple-element.36._, f32[64,128,128]{2,1,0:T(8,128)} %add_rows.2.base_ref, bf16[32,64,128]{2,1,0:T(8,128)(2,1)S(1)} %collective-permute-done.6.back_ref), custom_call_target="tpu_custom_call", output_to_operand_aliasing={{}: (1, {})} | custom-call | bytes 3145728 | tf_op jit(solution)/shard_map/add_rows/pallas_call | solution.py:574
  (3 shorter events, 0.0 us)
Async XLA Ops:
  0.0 10.7 %copy-start.2 = (bf16[1,64,128,128]{3,2,1,0:T(8,128)(2,1)S(1)}, bf16[1,64,128,128]{3,2,1,0:T(8,128)(2,1)}, u32[]{:S(2)}) copy-start(bf16[1,64,128,128]{3,2,1,0:T(8,128)(2,1)} %param.13) | copy-start | bytes 6291460
  2.9 23.5 %collective-permute-start = (bf16[32,128,128]{2,1,0:T(8,128)(2,1)S(1)}, bf16[32,128,128]{2,1,0:T(8,128)(2,1)}, u32[]{:S(2)}, u32[]{:S(2)}) collective-permute-start(bf16[32,128,128]{2,1,0:T(8,128)(2,1)S(1)} %get-tuple-element.64), channel_id=1, source_target_pairs={{0,255},{1,254},{2,4},{3,5},{4,2},{5,3},{6,8},{7,9},{8,6},{9,7},{1... | collective-permute-start | bytes 3145736 | tf_op jit(solution)/shard_map/ppermute | solution.py:631
  10.6 61.5 %collective-permute-start.2 = (bf16[32,128,128]{2,1,0:T(8,128)(2,1)}, bf16[32,128,128]{2,1,0:T(8,128)(2,1)}, u32[]{:S(2)}, u32[]{:S(2)}) collective-permute-start(bf16[32,128,128]{2,1,0:T(8,128)(2,1)} %get-tuple-element.63), channel_id=1, source_target_pairs={{0,255},{1,254},{2,4},{3,5},{4,2},{5,3},{6,8},{7,9},{8,6},{9,7},{1... | collective-permute-start | bytes 3145736 | tf_op jit(solution)/shard_map/ppermute | solution.py:631
  10.7 20.5 %copy-start.5 = (bf16[128,128]{1,0:T(8,128)(2,1)S(1)}, bf16[128,128]{1,0:T(8,128)(2,1)}, u32[]{:S(2)}) copy-start(bf16[128,128]{1,0:T(8,128)(2,1)} %radiate_ref.5) | copy-start | bytes 98308
  10.7 21.2 %copy-start.10 = (s32[8,16]{1,0:T(8,128)S(1)}, s32[8,16]{1,0:T(8,128)}, u32[]{:S(2)}) copy-start(s32[8,16]{1,0:T(8,128)} %param.21) | copy-start | bytes 1540
  10.7 21.8 %copy-start.11 = (s32[8,16]{1,0:T(8,128)S(1)}, s32[8,16]{1,0:T(8,128)}, u32[]{:S(2)}) copy-start(s32[8,16]{1,0:T(8,128)} %param.22) | copy-start | bytes 1540
  10.7 22.4 %copy-start.9 = (s32[64,6]{0,1:T(8,128)S(1)}, s32[64,6]{0,1:T(8,128)}, u32[]{:S(2)}) copy-start(s32[64,6]{0,1:T(8,128)} %param.16) | copy-start | bytes 4612
  10.7 23.2 %copy-start.7 = (s32[128,32]{0,1:T(8,128)S(1)}, s32[128,32]{0,1:T(8,128)}, u32[]{:S(2)}) copy-start(s32[128,32]{0,1:T(8,128)} %param.24) | copy-start | bytes 49156
  10.7 23.2 %copy-start.8 = (s32[128,32]{0,1:T(8,128)S(1)}, s32[128,32]{0,1:T(8,128)}, u32[]{:S(2)}) copy-start(s32[128,32]{0,1:T(8,128)} %param.25) | copy-start | bytes 49156
  10.7 23.6 %copy-start.6 = (f32[316,16]{0,1:T(8,128)S(1)}, f32[316,16]{0,1:T(8,128)}, u32[]{:S(2)}) copy-start(f32[316,16]{0,1:T(8,128)} %param.23) | copy-start | bytes 60676
  10.7 78.1 %collective-permute-start.1 = (bf16[64,128,128]{2,1,0:T(8,128)(2,1)S(1)}, bf16[64,128,128]{2,1,0:T(8,128)(2,1)}, u32[]{:S(2)}, u32[]{:S(2)}) collective-permute-start(bf16[64,128,128]{2,1,0:T(8,128)(2,1)S(1)} %bitcast.26), channel_id=1, source_target_pairs={{0,2},{2,0},{4,6},{6,4},{8,10},{10,8},{12,14},{14,12},{16,18},{18,... | collective-permute-start | bytes 6291464 | tf_op jit(solution)/shard_map/ppermute | solution.py:634
  26.4 45.8 %collective-permute-start.3 = (bf16[32,128,128]{2,1,0:T(8,128)(2,1)}, bf16[32,128,128]{2,1,0:T(8,128)(2,1)S(1)}, u32[]{:S(2)}, u32[]{:S(2)}) collective-permute-start(bf16[32,128,128]{2,1,0:T(8,128)(2,1)} %collective-permute-done.a_ref.refs_6_), channel_id=1, source_target_pairs={{255,1},{254,0},{4,3},{5,2},{2,5},{3,4},{8,7},{9,6},{6,9},{7,8},{1... | collective-permute-start | bytes 3145736 | tf_op jit(solution)/shard_map/ppermute | solution.py:638
  72.2 28.4 %copy-start.3 = (bf16[32,128,128]{2,1,0:T(8,128)(2,1)}, bf16[32,128,128]{2,1,0:T(8,128)(2,1)S(1)}, u32[]{:S(2)}) copy-start(bf16[32,128,128]{2,1,0:T(8,128)(2,1)S(1)} %collective-permute-done.3.refs_0_.refs_2_) | copy-start | bytes 3145732
  72.2 30.3 %collective-permute-start.4 = (bf16[32,128,128]{2,1,0:T(8,128)(2,1)}, bf16[32,128,128]{2,1,0:T(8,128)(2,1)S(1)}, u32[]{:S(2)}, u32[]{:S(2)}) collective-permute-start(bf16[32,128,128]{2,1,0:T(8,128)(2,1)} %collective-permute-done.2.b_ref.refs_8_), channel_id=1, source_target_pairs={{255,1},{254,0},{4,3},{5,2},{2,5},{3,4},{8,7},{9,6},{6,9},{7,8},{1... | collective-permute-start | bytes 3145736 | tf_op jit(solution)/shard_map/ppermute | solution.py:644
  76.4 1.0 copy-start.1
  88.0 0.8 copy-start
  102.5 1.0 copy-start.4
  173.4 46.2 %collective-permute-start.5 = (bf16[32,64,128]{2,1,0:T(8,128)(2,1)}, bf16[32,64,128]{2,1,0:T(8,128)(2,1)S(1)}, u32[]{:S(2)}, u32[]{:S(2)}) collective-permute-start(bf16[32,64,128]{2,1,0:T(8,128)(2,1)} %get-tuple-element.58), channel_id=1, source_target_pairs={{0,1},{1,0},{2,3},{3,2},{4,5},{5,4},{6,7},{7,6},{8,9},{9,8},{10,11... | collective-permute-start | bytes 1572872 | tf_op jit(solution)/shard_map/ppermute | solution.py:653
  187.7 34.6 %collective-permute-start.6 = (bf16[32,64,128]{2,1,0:T(8,128)(2,1)}, bf16[32,64,128]{2,1,0:T(8,128)(2,1)S(1)}, u32[]{:S(2)}, u32[]{:S(2)}) collective-permute-start(bf16[32,64,128]{2,1,0:T(8,128)(2,1)} %get-tuple-element.62), channel_id=1, source_target_pairs={{0,1},{1,0},{2,3},{3,2},{4,5},{5,4},{6,7},{7,6},{8,9},{9,8},{10,11... | collective-permute-start | bytes 1572872 | tf_op jit(solution)/shard_map/ppermute | solution.py:656
